TPU v7x, 32 devices: a whole 2x2x4 slice. The times are simulated.
32 devices in a mesh: dp: 2 (over x), seq: 16 (over z, y, core).
Axes of the slice: x: 2, y: 2, z: 4, core: 2. Of those that a mesh axis runs over, the one named last changes fastest.
Arguments:
- clean: bfloat16 [2, 4096, 768], P('dp', 'seq'), may hold values from -12 to 12
- out_cot: bfloat16 [2, 4096, 768], P('dp', 'seq'), may hold values from -6 to 6
- mask_bits: int32 [2, 256], P('dp', 'seq'), may hold values from 0 to 65535
- levels: int32 [2, 256], P('dp', 'seq'), may hold values from 1 to 16
- importance: int32 [2, 256, 2], P('dp', 'seq'), may hold values from 1 to 8
- w_query: bfloat16 [768, 768], replicated, may hold values from -0.21875 to 0.21875
- w_key: bfloat16 [768, 768], replicated, may hold values from -0.21875 to 0.21875
- w_value: bfloat16 [768, 768], replicated, may hold values from -0.21875 to 0.21875
- mask_embed: bfloat16 [768], replicated, may hold values from -6 to 6
Outputs:
- attn_out: bfloat16 [2, 4096, 768], P('dp', 'seq')
- clean_grad: float32 [2, 4096, 768], P('dp', 'seq')
All inputs are finite; a program needn't handle non-finite values.
Results may differ from a plain program's by a relative error of at most 0.025.
Values may be sent and summed in bfloat16 or wider, within the bound.
No kernel may reach another device: no remote copies, remote signals or barrier semaphores. Data moves between devices by JAX's collectives and lax.ppermute only.
A program may use at most 64 MiB of HBM per device.

v0:
```python
import math

import jax
import jax.numpy as jnp
from jax import lax
from jax.sharding import PartitionSpec as P

HEADS = 12
HEAD_DIM = 64
BLOCK = 16
WINDOW = 1024
LEVELS = 16


EPS = 1e-06
CLIP = 0.25


def from_behind(block, axis, distance):
    devices = range(lax.axis_size(axis))
    route = [(i - distance, i) for i in devices if i - distance in devices]
    return lax.ppermute(block, axis, route)


def to_heads(rows):
    return rows.reshape(rows.shape[0], HEADS, HEAD_DIM).transpose(1, 0, 2)


def from_heads(stacked):
    return stacked.transpose(1, 0, 2).reshape(stacked.shape[1], HEADS * HEAD_DIM)


def forward_head(
    query_h, key_h, value_h, nkey_h, nvalue_h, grad_h, allow_clean, allow_noisy, scale
):
    score_clean = (
        jnp.einsum("qe,ke->qk", query_h, key_h, preferred_element_type=jnp.float32) * scale
    )
    score_noisy = (
        jnp.einsum("qe,ke->qk", query_h, nkey_h, preferred_element_type=jnp.float32) * scale
    )
    score_clean = jnp.where(allow_clean, score_clean, -jnp.inf)
    score_noisy = jnp.where(allow_noisy, score_noisy, -jnp.inf)
    peak = jnp.maximum(jnp.max(score_clean, axis=-1), jnp.max(score_noisy, axis=-1))
    exp_clean = jnp.where(allow_clean, jnp.exp(score_clean - peak[:, None]), 0.0)
    exp_noisy = jnp.where(allow_noisy, jnp.exp(score_noisy - peak[:, None]), 0.0)
    denom = jnp.sum(exp_clean, axis=-1) + jnp.sum(exp_noisy, axis=-1)
    prob_clean = exp_clean / denom[:, None]
    prob_noisy = exp_noisy / denom[:, None]
    weight_clean = prob_clean.astype(jnp.bfloat16)
    weight_noisy = prob_noisy.astype(jnp.bfloat16)
    mixed = jnp.einsum("qk,ke->qe", weight_clean, value_h, preferred_element_type=jnp.float32)
    mixed = mixed + jnp.einsum(
        "qk,ke->qe", weight_noisy, nvalue_h, preferred_element_type=jnp.float32
    )
    out_h = mixed.astype(jnp.bfloat16)
    delta = jnp.sum(grad_h.astype(jnp.float32) * out_h.astype(jnp.float32), axis=-1)
    return (out_h, prob_clean, weight_clean, peak, denom, delta)


def on_device(clean, out_cot, mask_bits, levels, importance, w_query, w_key, w_value, mask_embed):
    clean_rows = clean[0]
    cotangent = out_cot[0]
    tok_count = clean_rows.shape[0]
    width = clean_rows.shape[1]
    span = WINDOW // tok_count
    scale = 1.0 / math.sqrt(HEAD_DIM)
    position = lax.axis_index("seq") * tok_count
    local = jnp.arange(tok_count, dtype=jnp.int32)
    local_block = local // BLOCK
    within = local % BLOCK
    bits = jnp.right_shift(mask_bits[0][local_block], within) & 1
    masked = bits == 1
    noisy = jnp.where(masked[:, None], mask_embed[None, :], clean_rows)
    query = jnp.dot(noisy, w_query, preferred_element_type=jnp.float32).astype(jnp.bfloat16)
    key_noisy = jnp.dot(noisy, w_key, preferred_element_type=jnp.float32).astype(jnp.bfloat16)
    value_noisy = jnp.dot(noisy, w_value, preferred_element_type=jnp.float32).astype(jnp.bfloat16)
    key_wide = w_key.astype(jnp.float32).T
    value_wide = w_value.astype(jnp.float32).T
    key_mine = jnp.dot(clean_rows, w_key, preferred_element_type=jnp.float32).astype(jnp.bfloat16)
    value_mine = jnp.dot(clean_rows, w_value, preferred_element_type=jnp.float32).astype(
        jnp.bfloat16
    )
    carried = jnp.stack([key_mine, value_mine])
    collected = [carried]
    for step in range(span):
        carried = from_behind(carried, "seq", 1)
        collected.insert(0, carried)
    window_kv = jnp.concatenate(collected, axis=1)
    key_clean = window_kv[0]
    value_clean = window_kv[1]
    context = key_clean.shape[0]
    ctx_pos = position - span * tok_count + jnp.arange(context, dtype=jnp.int32)
    q_start = (position + local) // BLOCK * BLOCK
    allow_clean = (
        (ctx_pos[None, :] < q_start[:, None])
        & (ctx_pos[None, :] >= q_start[:, None] - WINDOW)
        & (ctx_pos[None, :] >= 0)
    )
    allow_noisy = local_block[None, :] == local_block[:, None]
    level_f = levels[0].astype(jnp.float32)
    ratio_f = importance[0].astype(jnp.float32)
    block_weight = LEVELS / level_f * (ratio_f[:, 0] / ratio_f[:, 1])
    token_weight = block_weight[local_block] * bits.astype(jnp.float32)
    grad_out = (cotangent.astype(jnp.float32) * token_weight[:, None]).astype(jnp.bfloat16)
    head_inputs = (
        to_heads(query),
        to_heads(key_clean),
        to_heads(value_clean),
        to_heads(key_noisy),
        to_heads(value_noisy),
        to_heads(grad_out),
    )

    def full_pass(items):
        query_h, key_h, value_h, nkey_h, nvalue_h, grad_h = items
        out_h, prob_clean, weight_clean, peak, denom, delta = forward_head(
            query_h, key_h, value_h, nkey_h, nvalue_h, grad_h, allow_clean, allow_noisy, scale
        )
        dprob = jnp.einsum("qe,ke->qk", grad_h, value_h, preferred_element_type=jnp.float32)
        dscore = (prob_clean * (dprob - delta[:, None]) * scale).astype(jnp.bfloat16)
        dkey_h = jnp.einsum("qk,qe->ke", dscore, query_h, preferred_element_type=jnp.float32)
        dvalue_h = jnp.einsum("qk,qe->ke", weight_clean, grad_h, preferred_element_type=jnp.float32)
        return (out_h, dkey_h, dvalue_h)

    out_heads, dkey_heads, dvalue_heads = lax.map(full_pass, head_inputs)
    terms = jnp.stack([from_heads(dkey_heads), from_heads(dvalue_heads)])
    running = terms[:, :tok_count]
    for step in range(span):
        running = from_behind(running, "seq", -1)
        running = running + terms[:, (step + 1) * tok_count : (step + 2) * tok_count]
    raw = jnp.dot(running[0], key_wide, precision=lax.Precision.HIGHEST)
    raw = raw + jnp.dot(running[1], value_wide, precision=lax.Precision.HIGHEST)
    attn_rows = from_heads(out_heads)
    squares = jnp.sum(raw * raw)
    total_squares = lax.psum(squares, ("dp", "seq"))
    entries = float(tok_count * width * lax.axis_size("dp") * lax.axis_size("seq"))
    rms = jnp.sqrt(total_squares / entries + EPS)
    factor = jnp.minimum(1.0, CLIP / rms)
    return (attn_rows[None], (raw * factor)[None])


def solution(mesh):
    in_specs = (
        P("dp", "seq", None),
        P("dp", "seq", None),
        P("dp", "seq"),
        P("dp", "seq"),
        P("dp", "seq", None),
        P(),
        P(),
        P(),
        P(),
    )
    out_specs = (P("dp", "seq", None), P("dp", "seq", None))
    return jax.shard_map(
        on_device, mesh=mesh, in_specs=in_specs, out_specs=out_specs, check_vma=False
    )
```

profile of v0, /device:TPU:0, one launch (start us, length us, event | category | flops | bytes accessed | tf_op | source)
XLA Modules:
  0.0 342.9 jit_solution(14128604512822295350)
XLA Ops:
  4.0 2.4 collective-permute-start
  6.4 1.8 collective-permute-done
  9.2 11.6 %collective-permute-start.1 = (bf16[2,256,768]{2,1,0:T(8,128)(2,1)S(1)}, bf16[2,256,768]{2,1,0:T(8,128)(2,1)S(1)}, u32[]{:S(2)}, u32[]{:S(2)}) collective-permute-start(bf16[2,256,768]{2,1,0:T(8,128)(2,1)S(1)} %collective-permute-done), channel_id=1, source_target_pairs={{0,1},{1,2},{2,3},{3,4},{4,5},{5,6},{6,7},{7,8},{8,9},{9,10},{10,1... | collective-permute-start | bytes 2359304 | tf_op jit(solution)/shard_map/ppermute | solution.py:22
  21.9 4.3 %compare_select_fusion.3 = f32[256,1]{0,1:T(1,128)S(1)} fusion(f32[]{:T(128)} %bitcast.43, f32[]{:T(128)} %bitcast.44, f32[]{:T(128)} %bitcast.45, f32[]{:T(128)} %bitcast.46, f32[]{:T(128)} %bitcast.47, f32[]{:T(128)} %bitcast.49, f32[]{:T(128)} %bitcast.48), kind=kLoop, calls=%fused_computation.113 | loop fusion | flops 5888 | bytes 1052 | tf_op jit(solution)/shard_map/gather | solution.py:104
  26.9 4.3 %compare_select_fusion.2 = s32[256,1]{0,1:T(1,128)S(1)} fusion(s32[]{:T(128)} %bitcast.9, s32[]{:T(128)} %bitcast.10, s32[]{:T(128)} %bitcast.11, s32[]{:T(128)} %bitcast.12, s32[]{:T(128)} %bitcast.13, s32[]{:T(128)} %bitcast.15, s32[]{:T(128)} %bitcast.14), kind=kLoop, calls=%fused_computation.112 | loop fusion | flops 5888 | bytes 1052 | tf_op jit(solution)/shard_map/gather | solution.py:72
  31.2 5.3 %collective-permute-start.2 = (bf16[2,256,768]{2,1,0:T(8,128)(2,1)S(1)}, bf16[2,256,768]{2,1,0:T(8,128)(2,1)}, u32[]{:S(2)}, u32[]{:S(2)}) collective-permute-start(bf16[2,256,768]{2,1,0:T(8,128)(2,1)S(1)} %collective-permute-done.1), channel_id=1, source_target_pairs={{0,1},{1,2},{2,3},{3,4},{4,5},{5,6},{6,7},{7,8},{8,9},{9,10},{10,1... | collective-permute-start | bytes 2359304 | tf_op jit(solution)/shard_map/ppermute | solution.py:22
  36.5 12.1 %select_multiply_fusion = (f32[256]{0:T(256)}, s32[256]{0:T(256)S(1)}) fusion(pred[256]{0:T(512)(128)(4,1)S(1)} %compare_reduce_fusion, pred[256]{0:T(512)(128)(4,1)S(1)} %compare_reduce_fusion.1, pred[256]{0:T(512)(128)(4,1)S(1)} %compare_reduce_fusion.2, pred[256]{0:T(512)(128)(4,1)S(1)} %compare_reduce_fusion.3, ...), kind=kLoop, calls=%fused_computation.136 | loop fusion | flops 7168 | bytes 6472 | tf_op jit(solution)/shard_map/mul | solution.py:104
  49.7 2.9 collective-permute-start.3
  61.8 4.0 %copy.21 = bf16[1,1280,768]{1,2,0:T(8,128)(2,1)} copy(bf16[1,1280,768]{2,1,0:T(8,128)(2,1)} %get-tuple-element.193) | data formatting | bytes 3932160 | tf_op jit(solution)/shard_map/slice | solution.py:91
  65.8 2.3 copy.19
  68.0 127.1 %while.16 = (s32[]{:T(128)}, bf16[12,256,64]{1,2,0:T(8,128)(2,1)}, f32[12,1280,64]{1,2,0:T(8,128)}, f32[12,1280,64]{1,2,0:T(8,128)}, bf16[12,256,64]{1,2,0:T(8,1...) while((s32[]{:T(128)}, bf16[12,256,64]{1,2,0:T(8,128)(2,1)}, ...), condition=%wide.region_6.7_spmd.clone.clone, body=%wide.region_0.6_spmd.clone.clone.sunk | while | flops 240876800 | bytes 9070557 | solution.py:126
  69.1 1.5 fusion.108
  71.4 1.6 fusion.112
  73.0 1.6 bitcast_dynamic-update-slice_fusion.2
  74.6 2.5 fusion.113
  79.6 1.5 fusion.108
  81.9 1.6 fusion.112
  83.6 1.6 bitcast_dynamic-update-slice_fusion.2
  85.2 2.6 fusion.113
  90.2 1.5 fusion.108
  92.5 1.6 fusion.112
  94.1 1.6 bitcast_dynamic-update-slice_fusion.2
  95.8 2.6 fusion.113
  100.8 1.5 fusion.108
  103.1 1.6 fusion.112
  104.7 1.6 bitcast_dynamic-update-slice_fusion.2
  106.4 2.6 fusion.113
  111.4 1.5 fusion.108
  113.7 1.6 fusion.112
  115.3 1.6 bitcast_dynamic-update-slice_fusion.2
  117.0 2.6 fusion.113
  124.3 1.6 fusion.112
  126.0 1.6 bitcast_dynamic-update-slice_fusion.2
  127.6 2.5 fusion.113
  134.9 1.6 fusion.112
  136.5 1.6 bitcast_dynamic-update-slice_fusion.2
  138.2 2.6 fusion.113
  145.5 1.6 fusion.112
  147.1 1.6 bitcast_dynamic-update-slice_fusion.2
  148.8 2.6 fusion.113
  153.8 1.5 fusion.108
  156.1 1.6 fusion.112
  157.7 1.6 bitcast_dynamic-update-slice_fusion.2
  159.4 2.6 fusion.113
  166.7 1.6 fusion.112
  168.3 1.6 bitcast_dynamic-update-slice_fusion.2
  170.0 2.6 fusion.113
  175.0 1.5 fusion.108
  177.3 1.6 fusion.112
  178.9 1.6 bitcast_dynamic-update-slice_fusion.2
  180.6 2.6 fusion.113
  187.9 1.6 fusion.112
  189.5 1.6 bitcast_dynamic-update-slice_fusion.2
  191.2 2.6 fusion.113
  195.1 1.6 fusion.58
  196.8 1.6 collective-permute-start.4
  198.3 8.3 %collective-permute-done.4 = f32[2,256,768]{1,2,0:T(8,128)S(1)} collective-permute-done((f32[2,256,768]{1,2,0:T(8,128)S(1)}, f32[2,256,768]{1,2,0:T(8,128)S(1)}, u32[]{:S(2)}, u32[]{:S(2)}) %collective-permute-start.4) | collective-permute-done | bytes 1572896 | tf_op jit(solution)/shard_map/ppermute | solution.py:22
  208.2 21.2 %collective-permute-done.5 = f32[2,256,768]{1,2,0:T(8,128)S(1)} collective-permute-done((f32[2,256,768]{1,2,0:T(8,128)S(1)}, f32[2,256,768]{1,2,0:T(8,128)S(1)}, u32[]{:S(2)}, u32[]{:S(2)}) %collective-permute-start.5) | collective-permute-done | bytes 1572896 | tf_op jit(solution)/shard_map/ppermute | solution.py:22
  231.0 20.4 %collective-permute-done.6 = f32[2,256,768]{1,2,0:T(8,128)S(1)} collective-permute-done((f32[2,256,768]{1,2,0:T(8,128)S(1)}, f32[2,256,768]{1,2,0:T(8,128)S(1)}, u32[]{:S(2)}, u32[]{:S(2)}) %collective-permute-start.6) | collective-permute-done | bytes 1572896 | tf_op jit(solution)/shard_map/ppermute | solution.py:22
  255.3 19.5 %collective-permute-done.7 = f32[2,256,768]{1,2,0:T(8,128)S(1)} collective-permute-done((f32[2,256,768]{1,2,0:T(8,128)}, f32[2,256,768]{1,2,0:T(8,128)S(1)}, u32[]{:S(2)}, u32[]{:S(2)}) %collective-permute-start.7) | collective-permute-done | bytes 1572896 | tf_op jit(solution)/shard_map/ppermute | solution.py:22
  274.8 1.6 fusion.63
  276.4 2.1 fusion.66
  278.4 2.8 multiply_reduce_fusion.1
  281.2 60.0 %psum.7 = f32[]{:T(128)} all-reduce(f32[]{:T(128)} %get-tuple-element.227), channel_id=1, replica_groups=mesh['dp'=2,'seq'=16] {'dp','seq'}, use_global_device_ids=true, to_apply=%region_8.9 | all-reduce | flops 1 | bytes 8 | tf_op jit(solution)/shard_map/psum | solution.py:136
  (220 shorter events, 70.6 us)
Async XLA Ops:
  0.6 1.3 copy-start
  0.6 2.7 copy-start.5
  0.7 2.7 copy-start.3
  3.4 17.4 %copy-start.15 = (s32[1,16,2]{1,2,0:T(2,128)S(1)}, s32[1,16,2]{1,2,0:T(2,128)}, u32[]{:S(2)}) copy-start(s32[1,16,2]{1,2,0:T(2,128)} %param.15) | copy-start | bytes 388
  3.4 17.7 %copy-start.16 = (s32[1,16]{1,0:T(1,128)S(1)}, s32[1,16]{1,0:T(1,128)}, u32[]{:S(2)}) copy-start(s32[1,16]{1,0:T(1,128)} %param.14) | copy-start | bytes 196
  3.4 22.7 %copy-start.12 = (s32[1,16]{1,0:T(1,128)S(1)}, s32[1,16]{1,0:T(1,128)}, u32[]{:S(2)}) copy-start(s32[1,16]{1,0:T(1,128)} %param.13) | copy-start | bytes 196
  3.4 45.2 %copy-start.18 = (bf16[768]{0:T(1024)(128)(2,1)S(1)}, bf16[768]{0:T(1024)(128)(2,1)}, u32[]{:S(2)}) copy-start(bf16[768]{0:T(1024)(128)(2,1)} %param.19) | copy-start | bytes 4612
  4.0 4.3 %collective-permute-start = (bf16[2,256,768]{2,1,0:T(8,128)(2,1)S(1)}, bf16[2,256,768]{2,1,0:T(8,128)(2,1)S(1)}, u32[]{:S(2)}, u32[]{:S(2)}) collective-permute-start(bf16[2,256,768]{2,1,0:T(8,128)(2,1)S(1)} %pad_maximum_fusion.1), channel_id=1, source_target_pairs={{0,1},{1,2},{2,3},{3,4},{4,5},{5,6},{6,7},{7,8},{8,9},{9,10},{10,1... | collective-permute-start | bytes 2359304 | tf_op jit(solution)/shard_map/ppermute | solution.py:22
  8.3 0.9 copy-start.6
  9.2 21.9 %collective-permute-start.1 = (bf16[2,256,768]{2,1,0:T(8,128)(2,1)S(1)}, bf16[2,256,768]{2,1,0:T(8,128)(2,1)S(1)}, u32[]{:S(2)}, u32[]{:S(2)}) collective-permute-start(bf16[2,256,768]{2,1,0:T(8,128)(2,1)S(1)} %collective-permute-done), channel_id=1, source_target_pairs={{0,1},{1,2},{2,3},{3,4},{4,5},{5,6},{6,7},{7,8},{8,9},{9,10},{10,1... | collective-permute-start | bytes 2359304 | tf_op jit(solution)/shard_map/ppermute | solution.py:22
  31.2 18.5 %copy-start.8 = (bf16[2,256,768]{2,1,0:T(8,128)(2,1)}, bf16[2,256,768]{2,1,0:T(8,128)(2,1)S(1)}, u32[]{:S(2)}) copy-start(bf16[2,256,768]{2,1,0:T(8,128)(2,1)S(1)} %collective-permute-done.1) | copy-start | bytes 2359300
  31.2 18.5 %collective-permute-start.2 = (bf16[2,256,768]{2,1,0:T(8,128)(2,1)S(1)}, bf16[2,256,768]{2,1,0:T(8,128)(2,1)}, u32[]{:S(2)}, u32[]{:S(2)}) collective-permute-start(bf16[2,256,768]{2,1,0:T(8,128)(2,1)S(1)} %collective-permute-done.1), channel_id=1, source_target_pairs={{0,1},{1,2},{2,3},{3,4},{4,5},{5,6},{6,7},{7,8},{8,9},{9,10},{10,1... | collective-permute-start | bytes 2359304 | tf_op jit(solution)/shard_map/ppermute | solution.py:22
  49.1 3.4 copy-start.17
  49.7 7.8 %collective-permute-start.3 = (bf16[2,256,768]{2,1,0:T(8,128)(2,1)}, bf16[2,256,768]{2,1,0:T(8,128)(2,1)}, u32[]{:S(2)}, u32[]{:S(2)}) collective-permute-start(bf16[2,256,768]{2,1,0:T(8,128)(2,1)} %collective-permute-done.2), channel_id=1, source_target_pairs={{0,1},{1,2},{2,3},{3,4},{4,5},{5,6},{6,7},{7,8},{8,9},{9,10},{10,1... | collective-permute-start | bytes 2359304 | tf_op jit(solution)/shard_map/ppermute | solution.py:22
  53.1 2.8 copy-start.11
  57.5 2.6 copy-start.9
  58.7 1.4 copy-start.7
  68.0 2.7 copy-start.13
  68.0 2.7 copy-start.14
  78.6 2.7 copy-start.13
  78.6 2.7 copy-start.14
  89.2 2.7 copy-start.13
  89.2 2.7 copy-start.14
  99.8 2.7 copy-start.13
  99.8 2.7 copy-start.14
  110.4 2.7 copy-start.13
  110.4 2.7 copy-start.14
  121.0 2.7 copy-start.13
  121.0 2.7 copy-start.14
  131.6 2.7 copy-start.13
  131.6 2.7 copy-start.14
  142.2 2.7 copy-start.13
  142.2 2.7 copy-start.14
  152.8 2.7 copy-start.13
  152.8 2.7 copy-start.14
  163.4 2.7 copy-start.13
  163.4 2.7 copy-start.14
  173.9 2.7 copy-start.13
  173.9 2.7 copy-start.14
  184.5 2.7 copy-start.13
  184.6 2.7 copy-start.14
  195.1 11.5 %copy-start.1 = (f32[12,1280,64]{1,2,0:T(8,128)S(1)}, f32[12,1280,64]{1,2,0:T(8,128)}, u32[]{:S(2)}) copy-start(f32[12,1280,64]{1,2,0:T(8,128)} %get-tuple-element.71) | copy-start | bytes 11796484
  195.1 11.5 %copy-start.2 = (f32[12,1280,64]{1,2,0:T(8,128)S(1)}, f32[12,1280,64]{1,2,0:T(8,128)}, u32[]{:S(2)}) copy-start(f32[12,1280,64]{1,2,0:T(8,128)} %get-tuple-element.70) | copy-start | bytes 11796484
  196.8 9.9 %collective-permute-start.4 = (f32[2,256,768]{1,2,0:T(8,128)S(1)}, f32[2,256,768]{1,2,0:T(8,128)S(1)}, u32[]{:S(2)}, u32[]{:S(2)}) collective-permute-start(f32[2,256,768]{1,2,0:T(8,128)S(1)} %fusion.58), channel_id=1, source_target_pairs={{1,0},{2,1},{3,2},{4,3},{5,4},{6,5},{7,6},{8,7},{9,8},{10,9},{11,1... | collective-permute-start | bytes 4718600 | tf_op jit(solution)/shard_map/ppermute | solution.py:22
  206.9 22.5 %collective-permute-start.5 = (f32[2,256,768]{1,2,0:T(8,128)S(1)}, f32[2,256,768]{1,2,0:T(8,128)S(1)}, u32[]{:S(2)}, u32[]{:S(2)}) collective-permute-start(f32[2,256,768]{1,2,0:T(8,128)S(1)} %fusion.60), channel_id=1, source_target_pairs={{1,0},{2,1},{3,2},{4,3},{5,4},{6,5},{7,6},{8,7},{9,8},{10,9},{11,1... | collective-permute-start | bytes 4718600 | tf_op jit(solution)/shard_map/ppermute | solution.py:22
  229.5 24.8 %copy-start.10 = (bf16[12,256,64]{1,2,0:T(8,128)(2,1)S(1)}, bf16[12,256,64]{1,2,0:T(8,128)(2,1)}, u32[]{:S(2)}) copy-start(bf16[12,256,64]{1,2,0:T(8,128)(2,1)} %get-tuple-element.69) | copy-start | bytes 1179652
  229.6 21.9 %collective-permute-start.6 = (f32[2,256,768]{1,2,0:T(8,128)S(1)}, f32[2,256,768]{1,2,0:T(8,128)S(1)}, u32[]{:S(2)}, u32[]{:S(2)}) collective-permute-start(f32[2,256,768]{1,2,0:T(8,128)S(1)} %fusion.62), channel_id=1, source_target_pairs={{1,0},{2,1},{3,2},{4,3},{5,4},{6,5},{7,6},{8,7},{9,8},{10,9},{11,1... | collective-permute-start | bytes 4718600 | tf_op jit(solution)/shard_map/ppermute | solution.py:22
  252.9 21.9 %collective-permute-start.7 = (f32[2,256,768]{1,2,0:T(8,128)}, f32[2,256,768]{1,2,0:T(8,128)S(1)}, u32[]{:S(2)}, u32[]{:S(2)}) collective-permute-start(f32[2,256,768]{1,2,0:T(8,128)} %fusion.57), channel_id=1, source_target_pairs={{1,0},{2,1},{3,2},{4,3},{5,4},{6,5},{7,6},{8,7},{9,8},{10,9},{11,1... | collective-permute-start | bytes 4718600 | tf_op jit(solution)/shard_map/ppermute | solution.py:22
  255.3 21.1 %copy-start.4 = (bf16[768,768]{1,0:T(8,128)(2,1)S(1)}, bf16[768,768]{1,0:T(8,128)(2,1)}, u32[]{:S(2)}) copy-start(bf16[768,768]{1,0:T(8,128)(2,1)} %param.18) | copy-start | bytes 3538948
where the time goes:
time: 346 us; the launch traced here: 343 us
  matrix products  126 us (36%)
  waiting for transfers between devices  71.3 us (21%)
  blocking collectives  60 us (17%)
  other arithmetic  37.7 us (11%)
  starting transfers between devices  27.9 us (8%)
  local copies, waits for them, and re-layouts  18.1 us (5%)
    ppermute x8, waiting for transfers between devices, from_behind(): return lax.ppermute(block, axis, route)  71.3 us
    psum x1, blocking collectives, on_device(): total_squares = lax.psum(squares, ('dp', 'seq'))  60 us
    dot_general x12, matrix products, full_pass(): jnp.einsum('qk,qe->ke', dscore, query_h, preferred_element_type=jnp.float32)  30.7 us
    ppermute x8, starting transfers between devices, from_behind(): return lax.ppermute(block, axis, route)  27.9 us
    dot_general x12, matrix products, forward_head(): jnp.einsum('qk,ke->qe', weight_noisy, nvalue_h, preferred_element_type=jn...  19.4 us
    dot_general x12, matrix products, forward_head(): jnp.einsum('qk,ke->qe', weight_clean, value_h, preferred_element_type=jnp...  19.4 us
    dot_general x12, matrix products, forward_head(): jnp.einsum('qe,ke->qk', query_h, key_h, preferred_element_type=jnp.float32)  18.4 us
    dot_general x12, matrix products, full_pass(): jnp.einsum('qk,qe->ke', weight_clean, grad_h, preferred_element_type=jnp....  17.1 us
  transfers between devices with their start and end apart: 8, of which 5 were waited for; matrix products, arithmetic and copies ran while one was open for 9% of the time, Pallas kernels for 0%

commit v1 on v0

v1 whole, which is shorter than its diff:
```python
import math

import jax
import jax.numpy as jnp
from jax import lax
from jax.experimental import pallas as pl
from jax.experimental.pallas import tpu as pltpu
from jax.sharding import PartitionSpec as P

HEADS = 12
HEAD_DIM = 64
BLOCK = 16
WINDOW = 1024
LEVELS = 16
EPS = 1e-06
CLIP = 0.25
LANES = 128
GROUP = 4
F32 = jnp.float32
BF16 = jnp.bfloat16
VMEM_LIMIT = 56 * 1024 * 1024
SCALE = 1.0 / math.sqrt(HEAD_DIM)


def iota(shape, dim):
    return lax.broadcasted_iota(jnp.int32, shape, dim)


def dot(a, b, precision=None):
    return jnp.dot(a, b, preferred_element_type=F32, precision=precision)


def dot_t(a, b, precision=None):
    return lax.dot_general(
        a, b, (((1,), (1,)), ((), ())), preferred_element_type=F32, precision=precision
    )


def token_mask_col(bits_row, tok):
    blocks = bits_row.shape[1]
    row, lane = iota((tok, blocks), 0), iota((tok, blocks), 1)
    bit = jnp.right_shift(jnp.broadcast_to(bits_row, (tok, blocks)), row % BLOCK) & 1
    return jnp.sum(jnp.where(row // BLOCK == lane, bit, 0).astype(F32), axis=1, keepdims=True)


def token_mask_row(bits_row, tok):
    blocks = bits_row.shape[1]
    diag = iota((blocks, blocks), 0) == iota((blocks, blocks), 1)
    col = jnp.sum(
        jnp.where(diag, jnp.broadcast_to(bits_row, (blocks, blocks)), 0).astype(F32),
        axis=1,
        keepdims=True,
    ).astype(jnp.int32)
    row, lane = iota((blocks, tok), 0), iota((blocks, tok), 1)
    bit = jnp.right_shift(jnp.broadcast_to(col, (blocks, tok)), lane % BLOCK) & 1
    return jnp.sum(jnp.where(lane // BLOCK == row, bit, 0).astype(F32), axis=0, keepdims=True)


def local_kernel(
    clean_ref, cot_ref, bits_ref, lev_ref, imp_ref, wq_ref, wk_ref, wv_ref, me_ref,
    q_ref, k_ref, v_ref, km_ref, vm_ref, a_ref, qk_ref, stats_ref,
):
    tok, width = clean_ref.shape
    blocks = tok // BLOCK
    bits = bits_ref[...]
    masked = token_mask_col(bits, tok)
    is_masked = masked > 0.5
    imp = imp_ref[...].astype(F32)
    ratio_col = imp[:, 0:1] / imp[:, 1:2]
    diag = iota((blocks, blocks), 0) == iota((blocks, blocks), 1)
    ratio = jnp.sum(
        jnp.where(diag, jnp.broadcast_to(ratio_col, (blocks, blocks)), 0.0), axis=0, keepdims=True
    )
    weight = LEVELS / lev_ref[...].astype(F32) * ratio
    row, lane = iota((tok, blocks), 0), iota((tok, blocks), 1)
    token_weight = masked * jnp.sum(
        jnp.where(row // BLOCK == lane, jnp.broadcast_to(weight, (tok, blocks)), 0.0),
        axis=1,
        keepdims=True,
    )
    grad = (cot_ref[...].astype(F32) * token_weight).astype(BF16)
    mask_rows = jnp.broadcast_to(me_ref[...], (BLOCK, width))
    rows = jnp.concatenate([clean_ref[...], mask_rows], axis=0)
    keys = dot(rows, wk_ref[...]).astype(BF16)
    values = dot(rows, wv_ref[...]).astype(BF16)
    queries = (dot(rows, wq_ref[...]).astype(BF16).astype(F32) * SCALE).astype(BF16)
    key, value = keys[:tok], values[:tok]
    qm, vm = queries[tok : tok + 1], values[tok : tok + 1]
    k_ref[...] = key
    v_ref[...] = value
    q_ref[...] = jnp.where(is_masked, qm.astype(F32), queries[:tok].astype(F32)).astype(BF16)
    km_ref[...] = keys[tok:]
    vm_ref[...] = values[tok:]
    head_of = iota((LANES, width), 1) // HEAD_DIM == iota((LANES, width), 0)
    spread = jnp.where(head_of, 1.0, 0.0).astype(BF16)
    qm_heads = jnp.where(head_of, jnp.broadcast_to(qm.astype(F32), (LANES, width)), 0.0).astype(BF16)
    score = dot_t(keys, qm_heads)
    own, mask_score = score[:tok], score[tok : tok + 1]
    a_ref[...] = own
    qk_ref[...] = dot_t(qm_heads, wk_ref[...])

    def block_sums(scores, vals):
        by_block = scores.reshape(blocks, BLOCK, LANES)
        top = jnp.max(by_block, axis=1)
        expo = jnp.exp(by_block - top[:, None, :])
        total = jnp.sum(expo, axis=1)
        wide = dot(expo.reshape(tok, LANES).astype(BF16), spread)
        mixed = jnp.sum((wide * vals).reshape(blocks, BLOCK, width), axis=1)
        return top, total, mixed

    value_f = value.astype(F32)
    top, total, mixed = block_sums(own, value_f)
    top_n, total_n, mixed_n = block_sums(
        jnp.where(is_masked, mask_score, own), jnp.where(is_masked, vm.astype(F32), value_f)
    )
    grad_sum = jnp.sum(grad.astype(F32).reshape(blocks, BLOCK, width), axis=1)
    grad_mix = dot_t(grad_sum * mixed_n, jnp.where(head_of, 1.0, 0.0), lax.Precision.HIGHEST)
    in_heads = iota((blocks, LANES), 1) < HEADS
    packed = jnp.where(in_heads, top, 0.0)
    for place, part in enumerate((total, top_n, total_n, grad_mix)):
        packed = packed + pltpu.roll(jnp.where(in_heads, part, 0.0), 16 * (place + 1), 1)
    high = packed.astype(BF16)
    rest = packed - high.astype(F32)
    mid = rest.astype(BF16)
    low = (rest - mid.astype(F32)).astype(BF16)
    stats_ref[0] = grad_sum.astype(BF16)
    stats_ref[1] = mixed.astype(BF16)
    stats_ref[2] = jnp.zeros((blocks, width), BF16)
    stats_ref[2, :, 0:LANES] = high
    stats_ref[2, :, LANES : 2 * LANES] = mid
    stats_ref[2, :, 2 * LANES : 3 * LANES] = low


def grad_kernel(
    place_ref, a_ref, v_ref, qk_ref, wv_ref, own_ref, back_ref, ahead_ref, y_ref, c_ref,
    raw_ref, square_ref, held,
):
    tok, width = v_ref.shape
    blocks = tok // BLOCK
    mine = place_ref[0]
    last = place_ref[1]
    at = mine % GROUP
    for part, ref in enumerate((back_ref, own_ref, ahead_ref)):
        held[part * GROUP + at] = ref[...]
        held[part * GROUP + (at ^ 2)] = y_ref[part]
        held[part * GROUP + (at ^ 1)] = c_ref[part]
        held[part * GROUP + (at ^ 3)] = c_ref[3 + part]
    near = GROUP * blocks
    count_b = 2 * near
    count_u = 3 * near
    pad_u = 4 * near
    grads = held[GROUP:, 0].reshape(count_b, width)
    mixed = held[:, 1].reshape(count_u, width)
    mixed = jnp.concatenate([mixed, jnp.zeros((pad_u - count_u, width), BF16)], axis=0)
    scalars = (
        held[:, 2, :, 0:LANES].astype(F32)
        + held[:, 2, :, LANES : 2 * LANES].astype(F32)
        + held[:, 2, :, 2 * LANES : 3 * LANES].astype(F32)
    ).reshape(count_u, LANES)
    flipped = jnp.concatenate([scalars, jnp.zeros((pad_u - count_u, LANES), F32)], axis=0).T
    of_b = scalars[near:]
    first_block = (mine - at - GROUP) * blocks
    b_at = iota((count_b, pad_u), 0) + near
    u_at = iota((count_b, pad_u), 1)
    seen = (u_at < b_at) & (u_at >= b_at - near) & (u_at + first_block >= 0)
    lane_b = iota((count_b, LANES), 1)
    peaks = jnp.zeros((count_b, LANES), F32)
    shares = jnp.zeros((count_b, LANES), F32)
    deltas = jnp.zeros((count_b, LANES), F32)
    for h in range(HEADS):
        pair = slice((h // 2) * LANES, (h // 2 + 1) * LANES)
        half = lane_b // HEAD_DIM == h % 2
        top = jnp.where(seen, flipped[h : h + 1], -jnp.inf)
        top_n = of_b[:, 32 + h : 33 + h]
        peak = jnp.maximum(jnp.max(top, axis=1, keepdims=True), top_n)
        expo = jnp.exp(top - peak)
        expo_n = jnp.exp(top_n - peak)
        den = jnp.sum(expo * flipped[16 + h : 17 + h], axis=1, keepdims=True)
        den = den + expo_n * of_b[:, 48 + h : 49 + h]
        out = dot(expo.astype(BF16), mixed[:, pair])
        delta = jnp.sum(jnp.where(half, out * grads[:, pair].astype(F32), 0.0), axis=1, keepdims=True)
        delta = (delta + expo_n * of_b[:, 64 + h : 65 + h]) / den
        peaks = jnp.where(lane_b == h, peak, peaks)
        shares = jnp.where(lane_b == h, 1.0 / den, shares)
        deltas = jnp.where(lane_b == h, delta, deltas)
    peaks, shares, deltas = peaks.T, shares.T, deltas.T
    own_at = near + at * blocks + iota((tok, count_b), 0) // BLOCK
    b_at = iota((tok, count_b), 1) + near
    seen = (own_at < b_at) & (own_at >= b_at - near) & (b_at + first_block < last)
    lane_u = iota((tok, LANES), 1)
    sigma = jnp.zeros((tok, LANES), F32)
    scores = a_ref[...]
    raw = jnp.zeros((tok, width), F32)
    for pair_at in range(HEADS // 2):
        pair = slice(pair_at * LANES, (pair_at + 1) * LANES)
        value = v_ref[:, pair]
        grad_pair = grads[:, pair]
        dvalue = None
        for h in (2 * pair_at, 2 * pair_at + 1):
            half = lane_u // HEAD_DIM == h % 2
            prob = jnp.exp(scores[:, h : h + 1] - peaks[h : h + 1]) * shares[h : h + 1]
            prob = jnp.where(seen, prob, 0.0)
            dprob = dot_t(jnp.where(half, value.astype(F32), 0.0).astype(BF16), grad_pair)
            term = jnp.sum(prob * (dprob - deltas[h : h + 1]), axis=1, keepdims=True)
            sigma = jnp.where(lane_u == h, term, sigma)
            part = dot(prob.astype(BF16), grad_pair)
            dvalue = part if dvalue is None else jnp.where(half, part, dvalue)
        high = dvalue.astype(BF16)
        low = (dvalue - high.astype(F32)).astype(BF16)
        raw = raw + dot_t(high, wv_ref[:, pair]) + dot_t(low, wv_ref[:, pair])
    raw = raw + dot(sigma, qk_ref[...], lax.Precision.HIGHEST)
    raw_ref[...] = raw
    square_ref[...] = jnp.full(square_ref.shape, jnp.sum(raw * raw), F32)


def attend_kernel(
    place_ref, bits_ref, q_ref, k_ref, v_ref, km_ref, vm_ref, wk_ref, wv_ref,
    far_ref, y_ref, c_ref, out_ref, keys, vals, score,
):
    tok, width = q_ref.shape
    mine = place_ref[0]
    bits = bits_ref[...]
    chunk_rows = (k_ref.shape[0],)
    for place, rows in enumerate((far_ref[...], y_ref[...], c_ref[0], c_ref[1])):
        keys[place] = dot(rows, wk_ref[...]).astype(BF16)
        vals[place] = dot(rows, wv_ref[...]).astype(BF16)
    row_b, col_b = iota((tok, tok), 0) // BLOCK, iota((tok, tok), 1) // BLOCK
    clear = token_mask_row(bits, tok) < 0.5
    own_bias = jnp.where((col_b < row_b) | ((col_b == row_b) & clear), 0.0, -jnp.inf)
    far_bias = jnp.where((col_b >= row_b) & (mine >= 4), 0.0, -jnp.inf)
    same = jnp.where(iota((tok, tok), 0) // BLOCK == iota((tok, tok), 1) // BLOCK, 1.0, 0.0)
    count = jnp.sum(same * token_mask_row(bits, tok), axis=1, keepdims=True)
    mask_bias = jnp.where(iota((tok, LANES), 1).astype(F32) < count, 0.0, -jnp.inf)
    biases = (far_bias,) + tuple(jnp.where(mine >= back, 0.0, -jnp.inf) for back in (2, 1, 3))
    lane = iota((tok, LANES), 1)

    def one_pair(pair_at, carry):
        pair = pl.ds(pl.multiple_of(pair_at * LANES, LANES), LANES)
        q_pair = q_ref[:, pair].astype(F32)
        k_own, v_own = k_ref[:, pair], v_ref[:, pair]
        k_mask = jnp.broadcast_to(km_ref[0:1, pair], (LANES, LANES))
        v_mask = jnp.broadcast_to(vm_ref[0:1, pair], (LANES, LANES))
        outs = []
        for half in range(2):
            here = lane // HEAD_DIM == half
            q_half = jnp.where(here, q_pair, 0.0).astype(BF16)
            s_own = dot_t(q_half, k_own) + own_bias
            s_mask = dot_t(q_half, k_mask) + mask_bias
            tops = [s_own[:, :LANES], s_own[:, LANES:], s_mask]
            for place in range(4):
                part = dot_t(q_half, keys[place, :, pair]) + biases[place]
                score[place] = part
                tops += [part[:, :LANES], part[:, LANES:]]
            while len(tops) > 1:
                tops = [jnp.maximum(*two) for two in zip(tops[::2], tops[1::2])] + (
                    [tops[-1]] if len(tops) % 2 else []
                )
            peak = jnp.max(tops[0], axis=1, keepdims=True)
            e_own, e_mask = jnp.exp(s_own - peak), jnp.exp(s_mask - peak)
            den = jnp.sum(e_own, axis=1, keepdims=True) + jnp.sum(e_mask, axis=1, keepdims=True)
            mixed = dot(e_own.astype(BF16), v_own) + dot(e_mask.astype(BF16), v_mask)
            for place in range(4):
                expo = jnp.exp(score[place] - peak)
                den = den + jnp.sum(expo, axis=1, keepdims=True)
                mixed = mixed + dot(expo.astype(BF16), vals[place, :, pair])
            outs.append(mixed / den)
        out_ref[:, pair] = jnp.where(lane < HEAD_DIM, outs[0], outs[1]).astype(BF16)
        return carry

    lax.fori_loop(0, HEADS // 2, one_pair, 0)


def scale_kernel(entries, square_ref, raw_ref, out_ref):
    total = jnp.sum(square_ref[:, 0:1], axis=0, keepdims=True)
    rms = jnp.sqrt(total / entries + EPS)
    out_ref[...] = raw_ref[...] * jnp.minimum(1.0, CLIP / rms)


def call(kernel, out_shape, scratch=(), smem=0, flops=0, **kw):
    def run(*args):
        spec = [pl.BlockSpec(memory_space=pltpu.SMEM)] * smem
        spec += [pl.BlockSpec(memory_space=pltpu.VMEM)] * (len(args) - smem)
        return pl.pallas_call(
            kernel,
            out_shape=out_shape,
            in_specs=spec,
            out_specs=jax.tree.map(lambda _: pl.BlockSpec(memory_space=pltpu.VMEM), out_shape),
            scratch_shapes=scratch,
            compiler_params=pltpu.CompilerParams(vmem_limit_bytes=VMEM_LIMIT),
            cost_estimate=pl.CostEstimate(flops=flops, bytes_accessed=4 << 20, transcendentals=0),
            **kw,
        )(*args)

    return run


def shift(rows, distance):
    devices = range(lax.axis_size("seq"))
    return lax.ppermute(rows, "seq", [(i, i + distance) for i in devices if i + distance in devices])


def swap(rows, bit):
    return lax.ppermute(rows, "seq", [(i, i ^ bit) for i in range(lax.axis_size("seq"))])


def on_device(clean, out_cot, mask_bits, levels, importance, w_query, w_key, w_value, mask_embed):
    clean_rows = clean[0]
    tok, width = clean_rows.shape
    blocks = tok // BLOCK
    place = lax.axis_index("seq")
    count = lax.axis_size("seq")
    where = jnp.stack([place, jnp.int32(count * blocks)]).astype(jnp.int32)

    def shape(*dims, dtype=BF16):
        return jax.ShapeDtypeStruct(dims, dtype)

    with jax.named_scope("halo"):
        far = shift(clean_rows, GROUP)
    with jax.named_scope("local"):
        q, k, v, km, vm, a, qk, stats = call(
            local_kernel,
            (
                shape(tok, width), shape(tok, width), shape(tok, width),
                shape(BLOCK, width), shape(BLOCK, width),
                shape(tok, LANES, dtype=F32), shape(LANES, width, dtype=F32),
                shape(3, blocks, width),
            ),
            flops=2_000_000_000,
        )(clean_rows, out_cot[0], mask_bits, levels, importance[0], w_query, w_key, w_value, mask_embed[None])
    with jax.named_scope("halo"):
        back, ahead = shift(stats, GROUP), shift(stats, -GROUP)
        mine3 = jnp.stack([back, stats, ahead])
        y3 = swap(mine3, 2)
        core6 = swap(jnp.concatenate([mine3, y3]), 1)
        two = swap(jnp.where(place & 2 == 0, clean_rows, far), 2)
        first = jnp.where(place & 1 == 0, clean_rows, two)
        second = jnp.where(place & 1 == 0, two, far)
        one_three = swap(jnp.stack([first, second]), 1)
    with jax.named_scope("grad"):
        parts = lax.axis_size("dp") * count
        raw, square = call(
            grad_kernel,
            (shape(tok, width, dtype=F32), shape(parts, LANES, dtype=F32)),
            scratch=[pltpu.VMEM((3 * GROUP, 3, blocks, width), BF16)],
            smem=1,
            flops=2_000_000_000,
        )(where, a, v, qk, w_value, stats, back, ahead, y3, core6)
        squares = lax.all_to_all(square, ("dp", "seq"), 0, 0)
    with jax.named_scope("attend"):
        attn = call(
            attend_kernel,
            shape(tok, width),
            scratch=[
                pltpu.VMEM((4, tok, width), BF16),
                pltpu.VMEM((4, tok, width), BF16),
                pltpu.VMEM((4, tok, tok), F32),
            ],
            smem=1,
            flops=8_000_000_000,
        )(where, mask_bits, q, k, v, km, vm, w_key, w_value, far, two, one_three)
    with jax.named_scope("clip"):
        entries = float(parts * tok * width)
        grad = call(lambda *refs: scale_kernel(entries, *refs), shape(tok, width, dtype=F32))(squares, raw)
    return attn[None], grad[None]


def solution(mesh):
    in_specs = (
        P("dp", "seq", None),
        P("dp", "seq", None),
        P("dp", "seq"),
        P("dp", "seq"),
        P("dp", "seq", None),
        P(),
        P(),
        P(),
        P(),
    )
    out_specs = (P("dp", "seq", None), P("dp", "seq", None))
    return jax.shard_map(
        on_device, mesh=mesh, in_specs=in_specs, out_specs=out_specs, check_vma=False
    )
```

time: 346 us -> 81.4 us (0.24)
  matrix products: 126 us -> 0 us
  waiting for transfers between devices: 71.3 us -> 16.7 us
  blocking collectives: 60 us -> 13.3 us
  other arithmetic: 37.7 us -> 2.91 us
  Pallas kernels: 0 us -> 30.3 us
  local copies, waits for them, and re-layouts: 18.1 us -> 3.54 us
  starting transfers between devices: 27.9 us -> 13.5 us
    dot_general x79 -> x0, matrix products: 126 us -> none  [the longest x12 30.7 us: full_pass(): jnp.einsum('qk,qe->ke', dscore, query_h, preferred_element_type=jnp.float32)]
    psum x1 -> x0, blocking collectives: 60 us -> none  [on_device(): total_squares = lax.psum(squares, ('dp', 'seq'))]
    ppermute x8 -> x7, waiting for transfers between devices: 71.3 us -> 16.7 us  [the longest x3 10.9 us: shift(): lax.ppermute(rows, 'seq', [(i, i + distance) for i in devices if i + dist...]
    pallas_call x0 -> x4, Pallas kernels: none -> 30.3 us  [run(): pl.pallas_call(kernel, out_shape=out_shape, in_specs=spec, out_specs=jax....]
    ppermute x8 -> x7, starting transfers between devices: 27.9 us -> 13.5 us  [the longest x3 11.3 us: shift(): lax.ppermute(rows, 'seq', [(i, i + distance) for i in devices if i + dist...]
    all_to_all x0 -> x1, blocking collectives: none -> 13.3 us  [on_device(): squares = lax.all_to_all(square, ('dp', 'seq'), 0, 0)]
    mul x3 -> x0, other arithmetic: 12.7 us -> none  [the longest x1 12.1 us: on_device(): token_weight = block_weight[local_block] * bits.astype(jnp.float32)]
    reduce_sum x36 -> x0, other arithmetic: 9.13 us -> none  [the longest x24 8.77 us: forward_head(): denom = jnp.sum(exp_clean, axis=-1) + jnp.sum(exp_noisy, axis=-1)]
  transfers between devices with their start and end apart: 8 -> 7, of which waited for: 5 -> 5; matrix products, arithmetic and copies ran while one was open for 9% -> 4% of each run, Pallas kernels for 0% -> 19%
where the time goes in v1:
time: 81.4 us; the launch traced here: 81.1 us
  Pallas kernels  30.3 us (37%)
  waiting for transfers between devices  16.7 us (21%)
  starting transfers between devices  13.5 us (17%)
  blocking collectives  13.3 us (16%)
  local copies, waits for them, and re-layouts  3.54 us (4%)
  other arithmetic  2.91 us (4%)
    pallas_call x4, Pallas kernels, run(): pl.pallas_call(kernel, out_shape=out_shape, in_specs=spec, out_specs=jax....  30.3 us
    all_to_all x1, blocking collectives, on_device(): squares = lax.all_to_all(square, ('dp', 'seq'), 0, 0)  13.3 us
    ppermute x3, starting transfers between devices, shift(): lax.ppermute(rows, 'seq', [(i, i + distance) for i in devices if i + dist...  11.3 us
    ppermute x3, waiting for transfers between devices, shift(): lax.ppermute(rows, 'seq', [(i, i + distance) for i in devices if i + dist...  10.9 us
    ppermute x4, waiting for transfers between devices, swap(): lax.ppermute(rows, 'seq', [(i, i ^ bit) for i in range(lax.axis_size('seq...  5.83 us
    unnamed x22, local copies, waits for them, and re-layouts  2.26 us
    ppermute x4, starting transfers between devices, swap(): lax.ppermute(rows, 'seq', [(i, i ^ bit) for i in range(lax.axis_size('seq...  2.23 us
  transfers between devices with their start and end apart: 7, of which 5 were waited for; matrix products, arithmetic and copies ran while one was open for 4% of the time, Pallas kernels for 19%

profile of v1, /device:TPU:0, one launch (start us, length us, event | category | flops | bytes accessed | tf_op | source)
XLA Modules:
  0.0 81.1 jit_solution(1848258543829236169)
XLA Ops:
  0.6 0.0 copy-start.7
  0.6 0.0 copy-start.8
  0.6 5.1 %collective-permute-start = (bf16[256,768]{1,0:T(8,128)(2,1)}, bf16[256,768]{1,0:T(8,128)(2,1)S(1)}, u32[]{:S(2)}, u32[]{:S(2)}) collective-permute-start(bf16[256,768]{1,0:T(8,128)(2,1)} %bitcast.19), channel_id=1, source_target_pairs={{0,4},{1,5},{2,6},{3,7},{4,8},{5,9},{6,10},{7,11},{8,12},{9,13},{1... | collective-permute-start | bytes 1179656 | tf_op jit(solution)/shard_map/halo/ppermute | solution.py:299
  5.8 8.6 %collective-permute-done.far_ref = bf16[256,768]{1,0:T(8,128)(2,1)S(1)} collective-permute-done((bf16[256,768]{1,0:T(8,128)(2,1)}, bf16[256,768]{1,0:T(8,128)(2,1)S(1)}, u32[]{:S(2)}, u32[]{:S(2)}) %collective-permute-start) | collective-permute-done | bytes 393248 | tf_op jit(solution)/shard_map/halo/ppermute | solution.py:299
  14.4 0.0 copy-start.1
  14.4 1.2 %broadcast_select_fusion = bf16[256,768]{1,0:T(8,128)(2,1)S(1)} fusion(bf16[256,768]{1,0:T(8,128)(2,1)S(1)} %collective-permute-done.far_ref, pred[]{:T(512)S(6)} %eq.7, bf16[1,256,768]{2,1,0:T(8,128)(2,1)} %param.9), kind=kLoop, calls=%fused_computation.4 | loop fusion | flops 196608 | bytes 1179649 | tf_op jit(solution)/shard_map/halo/jit(_where)/select_n | solution.py:335
  15.6 1.6 %collective-permute-start.1 = (bf16[256,768]{1,0:T(8,128)(2,1)S(1)}, bf16[256,768]{1,0:T(8,128)(2,1)S(1)}, u32[]{:S(2)}, u32[]{:S(2)}) collective-permute-start(bf16[256,768]{1,0:T(8,128)(2,1)S(1)} %broadcast_select_fusion), channel_id=1, source_target_pairs={{0,2},{1,3},{2,0},{3,1},{4,6},{5,7},{6,4},{7,5},{8,10},{9,11},{10,... | collective-permute-start | bytes 1179656 | tf_op jit(solution)/shard_map/halo/ppermute | solution.py:303
  17.2 0.0 copy-done.7
  17.2 0.6 broadcast_in_dim.9.me_ref
  17.8 0.0 copy-done.8
  17.8 0.7 copy.12.imp_ref
  18.4 0.0 copy-start
  18.4 5.7 %local.1 = (bf16[256,768]{1,0:T(8,128)(2,1)}, bf16[256,768]{1,0:T(8,128)(2,1)}, bf16[256,768]{1,0:T(8,128)(2,1)}, bf16[16,768]{1,0:T(8,128)(2,1)}, bf16[16,768]{...) custom-call(bf16[256,768]{1,0:T(8,128)(2,1)} %bitcast.20, ...), custom_call_target="tpu_custom_call" | custom-call | flops 2000000000 | bytes 4194304 | tf_op jit(solution)/shard_map/local/pallas_call | solution.py:283
  24.1 1.3 %collective-permute-start.4 = (bf16[3,16,768]{2,1,0:T(8,128)(2,1)}, bf16[3,16,768]{2,1,0:T(8,128)(2,1)S(1)}, u32[]{:S(2)}, u32[]{:S(2)}) collective-permute-start(bf16[3,16,768]{2,1,0:T(8,128)(2,1)} %get-tuple-element.19.own_ref), channel_id=1, source_target_pairs={{4,0},{5,1},{6,2},{7,3},{8,4},{9,5},{10,6},{11,7},{12,8},{13,9},{1... | collective-permute-start | bytes 221192 | tf_op jit(solution)/shard_map/halo/ppermute | solution.py:299
  25.4 4.9 %collective-permute-start.3 = (bf16[3,16,768]{2,1,0:T(8,128)(2,1)}, bf16[3,16,768]{2,1,0:T(8,128)(2,1)S(1)}, u32[]{:S(2)}, u32[]{:S(2)}) collective-permute-start(bf16[3,16,768]{2,1,0:T(8,128)(2,1)} %get-tuple-element.19.own_ref), channel_id=1, source_target_pairs={{0,4},{1,5},{2,6},{3,7},{4,8},{5,9},{6,10},{7,11},{8,12},{9,13},{1... | collective-permute-start | bytes 221192 | tf_op jit(solution)/shard_map/halo/ppermute | solution.py:299
  30.4 0.6 collective-permute-done.4.ahead_ref
  30.9 0.0 copy-start.4
  31.0 1.7 %collective-permute-done.3.back_ref = bf16[3,16,768]{2,1,0:T(8,128)(2,1)S(1)} collective-permute-done((bf16[3,16,768]{2,1,0:T(8,128)(2,1)}, bf16[3,16,768]{2,1,0:T(8,128)(2,1)S(1)}, u32[]{:S(2)}, u32[]{:S(2)}) %collective-permute-start.3) | collective-permute-done | bytes 73760 | tf_op jit(solution)/shard_map/halo/ppermute | solution.py:299
  32.6 0.0 copy-start.5
  32.6 0.9 %pad_maximum_fusion.2 = bf16[3,3,16,768]{3,2,1,0:T(8,128)(2,1)S(1)} fusion(bf16[1,3,16,768]{3,2,1,0:T(8,128)(2,1)S(1)} %bitcast.24, bf16[1,3,16,768]{3,2,1,0:T(8,128)(2,1)} %bitcast.22, bf16[1,3,16,768]{3,2,1,0:T(8,128)(2,1)S(1)} %bitcast.26), kind=kLoop, calls=%fused_computation.5 | loop fusion | flops 221184 | bytes 442368 | tf_op jit(solution)/shard_map/halo/stack | solution.py:332
  33.6 0.6 collective-permute-start.5
  34.1 0.0 collective-permute-done.1.y_ref
  34.1 0.0 copy-done.1
  34.1 0.0 copy-done
  34.2 0.0 copy-start.2
  34.2 0.1 select_bitcast_fusion.1
  34.2 0.0 copy-start.3
  34.3 0.1 pad_maximum_fusion
  34.3 0.6 copy-done.2
  34.9 0.0 collective-permute-start.2
  34.9 4.6 %collective-permute-done.5.y_ref = bf16[3,3,16,768]{3,2,1,0:T(8,128)(2,1)S(1)} collective-permute-done((bf16[3,3,16,768]{3,2,1,0:T(8,128)(2,1)S(1)}, bf16[3,3,16,768]{3,2,1,0:T(8,128)(2,1)S(1)}, u32[]{:S(2)}, u32[]{:S(2)}) %collective-permute-start.5) | collective-permute-done | bytes 221216 | tf_op jit(solution)/shard_map/halo/ppermute | solution.py:303
  39.6 0.0 copy-done.4
  39.6 0.0 copy-done.5
  39.6 0.0 copy-done.3
  39.6 0.0 copy-start.6
  39.6 0.1 pad_maximum_fusion.1
  39.6 0.1 collective-permute-start.6
  39.7 0.6 pad_add_fusion.place_ref
  40.3 1.2 %collective-permute-done.6.c_ref = bf16[6,3,16,768]{3,2,1,0:T(8,128)(2,1)S(1)} collective-permute-done((bf16[6,3,16,768]{3,2,1,0:T(8,128)(2,1)S(1)}, bf16[6,3,16,768]{3,2,1,0:T(8,128)(2,1)S(1)}, u32[]{:S(2)}, u32[]{:S(2)}) %collective-permute-start.6) | collective-permute-done | bytes 442400 | tf_op jit(solution)/shard_map/halo/ppermute | solution.py:303
  41.5 0.0 copy-start.10
  41.5 0.0 copy-done.6
  41.5 0.8 copy-done.10
  42.3 7.9 %grad.1 = (f32[256,768]{1,0:T(8,128)}, f32[32,128]{1,0:T(8,128)}) custom-call(s32[2]{0:T(128)} %pad_add_fusion.place_ref, f32[256,128]{1,0:T(8,128)} %get-tuple-element.17.a_ref, bf16[256,768]{1,0:T(8,128)(2,1)} %get-tuple-element.14.v_ref, f32[128,768]{1,0:T(8,128)} %get-tuple-element.18.qk_ref, bf16[768,768]{1,0:T(8,128)(2,1)} %wv_ref.5, ...), custom_call_target="tpu_custom_call" | custom-call | flops 2000000000 | bytes 4194304 | tf_op jit(solution)/shard_map/grad/pallas_call | solution.py:283
  50.2 13.3 %all_to_all.11 = f32[32,1,128]{2,1,0:T(1,128)} all-to-all(f32[32,1,128]{2,1,0:T(1,128)} %bitcast.29), channel_id=1, replica_groups=mesh['dp'=2,'seq'=16] {'dp','seq'}, dimensions={0} | all-to-all | bytes 32768 | tf_op jit(solution)/shard_map/grad/all_to_all | solution.py:348
  63.5 2.2 %clip.1 = f32[256,768]{1,0:T(8,128)} custom-call(f32[32,128]{1,0:T(8,128)} %bitcast.28, f32[256,768]{1,0:T(8,128)} %get-tuple-element.21.refs_1_), custom_call_target="tpu_custom_call" | custom-call | bytes 4194304 | tf_op jit(solution)/shard_map/clip/pallas_call | solution.py:283
  65.6 0.0 collective-permute-done.2.c_ref
  65.6 0.0 copy-start.9
  65.6 0.9 %copy-done.9 = bf16[2,256,768]{2,1,0:T(8,128)(2,1)} copy-done((bf16[2,256,768]{2,1,0:T(8,128)(2,1)}, bf16[2,256,768]{2,1,0:T(8,128)(2,1)S(1)}, u32[]{:S(2)}) %copy-start.9) | copy-done | bytes 786456
  66.5 14.5 %attend.1 = bf16[256,768]{1,0:T(8,128)(2,1)} custom-call(s32[2]{0:T(128)} %pad_add_fusion.place_ref, s32[1,16]{1,0:T(1,128)} %bits_ref.3, bf16[256,768]{1,0:T(8,128)(2,1)} %get-tuple-element.12.q_ref, bf16[256,768]{1,0:T(8,128)(2,1)} %get-tuple-element.13.k_ref, bf16[256,768]{1,0:T(8,128)(2,1)} %get-tuple-element.14.v_ref, ...), custom_call_target="tpu_custom_call" | custom-call | flops 8000000000 | bytes 4194304 | tf_op jit(solution)/shard_map/attend/pallas_call | solution.py:283
Async XLA Ops:
  0.6 16.5 %copy-start.7 = (bf16[768]{0:T(1024)(128)(2,1)S(1)}, bf16[768]{0:T(1024)(128)(2,1)}, u32[]{:S(2)}) copy-start(bf16[768]{0:T(1024)(128)(2,1)} %param.17) | copy-start | bytes 4612
  0.6 17.1 %copy-start.8 = (s32[1,16,2]{1,2,0:T(2,128)S(1)}, s32[1,16,2]{1,2,0:T(2,128)}, u32[]{:S(2)}) copy-start(s32[1,16,2]{1,2,0:T(2,128)} %param.13) | copy-start | bytes 388
  0.6 13.7 %collective-permute-start = (bf16[256,768]{1,0:T(8,128)(2,1)}, bf16[256,768]{1,0:T(8,128)(2,1)S(1)}, u32[]{:S(2)}, u32[]{:S(2)}) collective-permute-start(bf16[256,768]{1,0:T(8,128)(2,1)} %bitcast.19), channel_id=1, source_target_pairs={{0,4},{1,5},{2,6},{3,7},{4,8},{5,9},{6,10},{7,11},{8,12},{9,13},{1... | collective-permute-start | bytes 1179656 | tf_op jit(solution)/shard_map/halo/ppermute | solution.py:299
  14.4 19.8 %copy-start.1 = (bf16[256,768]{1,0:T(8,128)(2,1)}, bf16[256,768]{1,0:T(8,128)(2,1)S(1)}, u32[]{:S(2)}) copy-start(bf16[256,768]{1,0:T(8,128)(2,1)S(1)} %collective-permute-done.far_ref) | copy-start | bytes 1179652
  15.6 18.6 %collective-permute-start.1 = (bf16[256,768]{1,0:T(8,128)(2,1)S(1)}, bf16[256,768]{1,0:T(8,128)(2,1)S(1)}, u32[]{:S(2)}, u32[]{:S(2)}) collective-permute-start(bf16[256,768]{1,0:T(8,128)(2,1)S(1)} %broadcast_select_fusion), channel_id=1, source_target_pairs={{0,2},{1,3},{2,0},{3,1},{4,6},{5,7},{6,4},{7,5},{8,10},{9,11},{10,... | collective-permute-start | bytes 1179656 | tf_op jit(solution)/shard_map/halo/ppermute | solution.py:303
  18.4 15.7 %copy-start = (bf16[1,256,768]{2,1,0:T(8,128)(2,1)S(1)}, bf16[1,256,768]{2,1,0:T(8,128)(2,1)}, u32[]{:S(2)}) copy-start(bf16[1,256,768]{2,1,0:T(8,128)(2,1)} %param.9) | copy-start | bytes 1179652
  24.1 6.8 %collective-permute-start.4 = (bf16[3,16,768]{2,1,0:T(8,128)(2,1)}, bf16[3,16,768]{2,1,0:T(8,128)(2,1)S(1)}, u32[]{:S(2)}, u32[]{:S(2)}) collective-permute-start(bf16[3,16,768]{2,1,0:T(8,128)(2,1)} %get-tuple-element.19.own_ref), channel_id=1, source_target_pairs={{4,0},{5,1},{6,2},{7,3},{8,4},{9,5},{10,6},{11,7},{12,8},{13,9},{1... | collective-permute-start | bytes 221192 | tf_op jit(solution)/shard_map/halo/ppermute | solution.py:299
  25.4 7.2 %collective-permute-start.3 = (bf16[3,16,768]{2,1,0:T(8,128)(2,1)}, bf16[3,16,768]{2,1,0:T(8,128)(2,1)S(1)}, u32[]{:S(2)}, u32[]{:S(2)}) collective-permute-start(bf16[3,16,768]{2,1,0:T(8,128)(2,1)} %get-tuple-element.19.own_ref), channel_id=1, source_target_pairs={{0,4},{1,5},{2,6},{3,7},{4,8},{5,9},{6,10},{7,11},{8,12},{9,13},{1... | collective-permute-start | bytes 221192 | tf_op jit(solution)/shard_map/halo/ppermute | solution.py:299
  30.9 8.6 %copy-start.4 = (bf16[3,16,768]{2,1,0:T(8,128)(2,1)}, bf16[3,16,768]{2,1,0:T(8,128)(2,1)S(1)}, u32[]{:S(2)}) copy-start(bf16[3,16,768]{2,1,0:T(8,128)(2,1)S(1)} %collective-permute-done.4.ahead_ref) | copy-start | bytes 221188
  32.6 6.9 %copy-start.5 = (bf16[3,16,768]{2,1,0:T(8,128)(2,1)}, bf16[3,16,768]{2,1,0:T(8,128)(2,1)S(1)}, u32[]{:S(2)}) copy-start(bf16[3,16,768]{2,1,0:T(8,128)(2,1)S(1)} %collective-permute-done.3.back_ref) | copy-start | bytes 221188
  33.6 6.0 %collective-permute-start.5 = (bf16[3,3,16,768]{3,2,1,0:T(8,128)(2,1)S(1)}, bf16[3,3,16,768]{3,2,1,0:T(8,128)(2,1)S(1)}, u32[]{:S(2)}, u32[]{:S(2)}) collective-permute-start(bf16[3,3,16,768]{3,2,1,0:T(8,128)(2,1)S(1)} %pad_maximum_fusion.2), channel_id=1, source_target_pairs={{0,2},{1,3},{2,0},{3,1},{4,6},{5,7},{6,4},{7,5},{8,10},{9,11},{10,... | collective-permute-start | bytes 663560 | tf_op jit(solution)/shard_map/halo/ppermute | solution.py:303
  34.2 0.8 copy-start.2
  34.2 5.3 %copy-start.3 = (bf16[3,16,768]{2,1,0:T(8,128)(2,1)S(1)}, bf16[3,16,768]{2,1,0:T(8,128)(2,1)}, u32[]{:S(2)}) copy-start(bf16[3,16,768]{2,1,0:T(8,128)(2,1)} %get-tuple-element.19.own_ref) | copy-start | bytes 221188
  34.9 30.7 %collective-permute-start.2 = (bf16[2,256,768]{2,1,0:T(8,128)(2,1)S(1)}, bf16[2,256,768]{2,1,0:T(8,128)(2,1)S(1)}, u32[]{:S(2)}, u32[]{:S(2)}) collective-permute-start(bf16[2,256,768]{2,1,0:T(8,128)(2,1)S(1)} %pad_maximum_fusion), channel_id=1, source_target_pairs={{0,1},{1,0},{2,3},{3,2},{4,5},{5,4},{6,7},{7,6},{8,9},{9,8},{10,11... | collective-permute-start | bytes 2359304 | tf_op jit(solution)/shard_map/halo/ppermute | solution.py:303
  39.6 1.9 %copy-start.6 = (bf16[3,3,16,768]{3,2,1,0:T(8,128)(2,1)}, bf16[3,3,16,768]{3,2,1,0:T(8,128)(2,1)S(1)}, u32[]{:S(2)}) copy-start(bf16[3,3,16,768]{3,2,1,0:T(8,128)(2,1)S(1)} %collective-permute-done.5.y_ref) | copy-start | bytes 663556
  39.6 1.9 %collective-permute-start.6 = (bf16[6,3,16,768]{3,2,1,0:T(8,128)(2,1)S(1)}, bf16[6,3,16,768]{3,2,1,0:T(8,128)(2,1)S(1)}, u32[]{:S(2)}, u32[]{:S(2)}) collective-permute-start(bf16[6,3,16,768]{3,2,1,0:T(8,128)(2,1)S(1)} %pad_maximum_fusion.1), channel_id=1, source_target_pairs={{0,1},{1,0},{2,3},{3,2},{4,5},{5,4},{6,7},{7,6},{8,9},{9,8},{10,11... | collective-permute-start | bytes 1327112 | tf_op jit(solution)/shard_map/halo/ppermute | solution.py:303
  41.5 0.8 copy-start.10
  65.6 0.9 %copy-start.9 = (bf16[2,256,768]{2,1,0:T(8,128)(2,1)}, bf16[2,256,768]{2,1,0:T(8,128)(2,1)S(1)}, u32[]{:S(2)}) copy-start(bf16[2,256,768]{2,1,0:T(8,128)(2,1)S(1)} %collective-permute-done.2.c_ref) | copy-start | bytes 2359300

commit v2 on v1

v2 whole, which is shorter than its diff:
```python
import math

import jax
import jax.numpy as jnp
from jax import lax
from jax.experimental import pallas as pl
from jax.experimental.pallas import tpu as pltpu
from jax.sharding import PartitionSpec as P

HEADS = 12
HEAD_DIM = 64
BLOCK = 16
WINDOW = 1024
LEVELS = 16
EPS = 1e-06
CLIP = 0.25
LANES = 128
NEVER = -1e30
GROUP = 4
F32 = jnp.float32
BF16 = jnp.bfloat16
VMEM_LIMIT = 56 * 1024 * 1024
SCALE = 1.0 / math.sqrt(HEAD_DIM)


def iota(shape, dim):
    return lax.broadcasted_iota(jnp.int32, shape, dim)


def dot(a, b, precision=None):
    return jnp.dot(a, b, preferred_element_type=F32, precision=precision)


def dot_t(a, b, precision=None):
    return lax.dot_general(
        a, b, (((1,), (1,)), ((), ())), preferred_element_type=F32, precision=precision
    )


def token_mask_col(bits_row, tok):
    blocks = bits_row.shape[1]
    row, lane = iota((tok, blocks), 0), iota((tok, blocks), 1)
    bit = jnp.right_shift(jnp.broadcast_to(bits_row, (tok, blocks)), row % BLOCK) & 1
    return jnp.sum(jnp.where(row // BLOCK == lane, bit, 0).astype(F32), axis=1, keepdims=True)


def token_mask_row(bits_row, tok):
    blocks = bits_row.shape[1]
    diag = iota((blocks, blocks), 0) == iota((blocks, blocks), 1)
    col = jnp.sum(
        jnp.where(diag, jnp.broadcast_to(bits_row, (blocks, blocks)), 0).astype(F32),
        axis=1,
        keepdims=True,
    ).astype(jnp.int32)
    row, lane = iota((blocks, tok), 0), iota((blocks, tok), 1)
    bit = jnp.right_shift(jnp.broadcast_to(col, (blocks, tok)), lane % BLOCK) & 1
    return jnp.sum(jnp.where(lane // BLOCK == row, bit, 0).astype(F32), axis=0, keepdims=True)


def start_all(copies):
    for copy in copies:
        copy.start()
    return copies


def columns(at, count):
    return slice(at * count, (at + 1) * count)


def both_heads(pair):
    low = iota(pair.shape, 1) < HEAD_DIM
    wide = pair.astype(F32)
    return jnp.concatenate([jnp.where(low, wide, 0.0), jnp.where(low, 0.0, wide)], axis=0).astype(BF16)


def local_kernel(
    clean_hbm, wk_hbm, wv_hbm, wq_hbm, cot_hbm, me_hbm, bits_hbm, lev_hbm, imp_hbm,
    stats_ref, a_ref, qk_ref, km_ref, vm_ref, q_hbm, k_hbm, v_hbm,
    clean_ref, wk_ref, wv_ref, wq_ref, cot_ref, me_ref, bits_ref, lev_ref, imp_ref,
    q_ref, k_ref, v_ref, in_sems, out_sems,
):
    sources = (clean_hbm, me_hbm, wk_hbm, wv_hbm, wq_hbm, bits_hbm, lev_hbm, imp_hbm, cot_hbm)
    targets = (clean_ref, me_ref, wk_ref, wv_ref, wq_ref, bits_ref, lev_ref, imp_ref, cot_ref)
    copies = start_all(
        [
            pltpu.make_async_copy(src, dst, in_sems.at[i])
            for i, (src, dst) in enumerate(zip(sources, targets))
        ]
    )
    tok, width = clean_ref.shape
    blocks = tok // BLOCK
    head_of = iota((LANES, width), 1) // HEAD_DIM == iota((LANES, width), 0)
    spread = jnp.where(head_of, 1.0, 0.0).astype(BF16)
    copies[0].wait()
    copies[1].wait()
    mask_rows = jnp.broadcast_to(me_ref[...].reshape(1, width), (BLOCK, width))
    rows = jnp.concatenate([clean_ref[...], mask_rows], axis=0)
    copies[2].wait()
    keys = dot(rows, wk_ref[...]).astype(BF16)
    k_ref[...] = keys[:tok]
    km_ref[...] = keys[tok:]
    copies[3].wait()
    values = dot(rows, wv_ref[...]).astype(BF16)
    v_ref[...] = values[:tok]
    vm_ref[...] = values[tok:]
    copies[4].wait()
    queries = (dot(rows, wq_ref[...]).astype(BF16).astype(F32) * SCALE).astype(BF16)
    for copy in copies[5:]:
        copy.wait()
    bits = bits_ref[...]
    masked = token_mask_col(bits, tok)
    is_masked = masked > 0.5
    qm, vm = queries[tok : tok + 1], values[tok : tok + 1]
    q_ref[...] = jnp.where(is_masked, qm.astype(F32), queries[:tok].astype(F32)).astype(BF16)
    outs = start_all(
        [
            pltpu.make_async_copy(src, dst, out_sems.at[i])
            for i, (src, dst) in enumerate(((q_ref, q_hbm), (k_ref, k_hbm), (v_ref, v_hbm)))
        ]
    )
    imp = imp_ref[...].astype(F32)
    weight = LEVELS / lev_ref[...].astype(F32) * (imp[0:1] / imp[1:2])
    row, lane = iota((tok, blocks), 0), iota((tok, blocks), 1)
    token_weight = masked * jnp.sum(
        jnp.where(row // BLOCK == lane, jnp.broadcast_to(weight, (tok, blocks)), 0.0),
        axis=1,
        keepdims=True,
    )
    grad = (cot_ref[...].astype(F32) * token_weight).astype(BF16)
    qm_heads = jnp.where(head_of, jnp.broadcast_to(qm.astype(F32), (LANES, width)), 0.0).astype(BF16)
    score = dot_t(keys, qm_heads)
    own, mask_score = score[:tok], score[tok : tok + 1]
    a_ref[...] = own
    back = dot_t(qm_heads, wk_ref[...])[:BLOCK]
    high = back.astype(BF16)
    low = (back - high.astype(F32)).astype(BF16)
    qk_ref[...] = jnp.zeros(qk_ref.shape, BF16)
    qk_ref[0:BLOCK] = high
    qk_ref[BLOCK : 2 * BLOCK] = high
    qk_ref[2 * BLOCK : 3 * BLOCK] = low

    def block_sums(scores, vals):
        by_block = scores.reshape(blocks, BLOCK, LANES)
        top = jnp.max(by_block, axis=1)
        expo = jnp.exp(by_block - top[:, None, :])
        total = jnp.sum(expo, axis=1)
        share = expo * (1.0 / total)[:, None, :]
        wide = dot(share.reshape(tok, LANES).astype(BF16), spread)
        mixed = jnp.sum((wide * vals).reshape(blocks, BLOCK, width), axis=1)
        return top + jnp.log(total), mixed

    value_f = values[:tok].astype(F32)
    top, mixed = block_sums(own, value_f)
    top_n, mixed_n = block_sums(
        jnp.where(is_masked, mask_score, own), jnp.where(is_masked, vm.astype(F32), value_f)
    )
    grad_sum = jnp.sum(grad.astype(F32).reshape(blocks, BLOCK, width), axis=1)
    product = grad_sum * mixed_n
    high = product.astype(BF16)
    low = (product - high.astype(F32)).astype(BF16)
    grad_mix = dot_t(high, spread) + dot_t(low, spread)
    in_heads = iota((blocks, LANES), 1) < HEADS
    packed = jnp.where(in_heads, top, 0.0)
    for place, part in enumerate((top_n, grad_mix)):
        packed = packed + pltpu.roll(jnp.where(in_heads, part, 0.0), 16 * (place + 1), 1)
    high = packed.astype(BF16)
    rest = packed - high.astype(F32)
    mid = rest.astype(BF16)
    low = (rest - mid.astype(F32)).astype(BF16)
    stats_ref[0] = grad_sum.astype(BF16)
    stats_ref[1] = mixed.astype(BF16)
    stats_ref[2] = jnp.zeros((blocks, width), BF16)
    stats_ref[2, :, 0:LANES] = high
    stats_ref[2, :, LANES : 2 * LANES] = mid
    stats_ref[2, :, 2 * LANES : 3 * LANES] = low
    for copy in outs:
        copy.wait()


def grad_kernel(
    place_ref, own_hbm, back_hbm, ahead_hbm, y_hbm, c_hbm, a_hbm, v_hbm, qk_hbm, wv_hbm,
    square_ref, raw_hbm,
    held, a_ref, v_ref, qk_ref, wv_ref, dvalues, raw_ref, in_sems, out_sems,
):
    tok, width = v_ref.shape
    blocks = tok // BLOCK
    mine = place_ref[0]
    last = place_ref[1]
    at = mine % GROUP
    held[...] = jnp.zeros(held.shape, BF16)
    y_side = jnp.where(at & 2 == 0, 0, 2 * GROUP)
    c_side = jnp.where(at & 1 == 0, 0, 2 * GROUP)
    moves = (
        (back_hbm, held.at[at]),
        (own_hbm, held.at[GROUP + at]),
        (ahead_hbm, held.at[2 * GROUP + at]),
        (y_hbm.at[0], held.at[GROUP + (at ^ 2)]),
        (y_hbm.at[1], held.at[y_side + (at ^ 2)]),
        (c_hbm.at[0], held.at[GROUP + (at ^ 1)]),
        (c_hbm.at[1], held.at[c_side + (at ^ 1)]),
        (c_hbm.at[2], held.at[GROUP + (at ^ 3)]),
        (c_hbm.at[3], held.at[y_side + (at ^ 3)]),
        (a_hbm, a_ref),
        (v_hbm, v_ref),
        (qk_hbm, qk_ref),
        (wv_hbm, wv_ref),
    )
    copies = start_all(
        [pltpu.make_async_copy(src, dst, in_sems.at[i]) for i, (src, dst) in enumerate(moves)]
    )
    near = GROUP * blocks
    count_b = 2 * near
    count_u = 3 * near
    pad_u = 4 * near
    first_block = (mine - at - GROUP) * blocks
    u_at = iota((count_u, count_b), 0)
    b_at = iota((count_u, count_b), 1) + near
    seen = (u_at < b_at) & (u_at >= b_at - near) & (u_at + first_block >= 0)
    bias = jnp.where(seen, 0.0, -jnp.inf)
    for copy in copies[:9]:
        copy.wait()
    grads = held[GROUP:, 0].reshape(count_b, width)
    mixed = held[:, 1].reshape(count_u, width)
    scalars = (
        held[:, 2, :, 0:LANES].astype(F32)
        + held[:, 2, :, LANES : 2 * LANES].astype(F32)
        + held[:, 2, :, 2 * LANES : 3 * LANES].astype(F32)
    ).reshape(count_u, LANES)
    padded = jnp.concatenate(
        [scalars[near:], jnp.zeros((pad_u - count_b, LANES), F32)], axis=0
    )
    flipped = padded.T[:, :count_b]
    logs, deltas = [], []
    for pair_at in range(HEADS // 2):
        pair = columns(pair_at, LANES)
        products = dot_t(both_heads(mixed[:, pair]), grads[:, pair])
        for half in range(2):
            h = 2 * pair_at + half
            top = scalars[:, h : h + 1] + bias
            top_n = flipped[16 + h : 17 + h]
            peak = jnp.maximum(jnp.max(top, axis=0, keepdims=True), top_n)
            expo = jnp.exp(top - peak)
            expo_n = jnp.exp(top_n - peak)
            den = jnp.sum(expo, axis=0, keepdims=True) + expo_n
            delta = jnp.sum(expo * products[columns(half, count_u)], axis=0, keepdims=True)
            delta = (delta + expo_n * flipped[32 + h : 33 + h]) / den
            logs.append(peak + jnp.log(den))
            deltas.append(delta)
    own_at = near + at * blocks + iota((tok, count_b), 0) // BLOCK
    b_at = iota((tok, count_b), 1) + near
    seen = (own_at < b_at) & (own_at >= b_at - near) & (b_at + first_block < last)
    bias = jnp.where(seen, 0.0, -jnp.inf)
    lane_u = iota((tok, LANES), 1)
    sigma = jnp.zeros((tok, LANES), F32)
    copies[9].wait()
    copies[10].wait()
    scores = a_ref[...]
    for pair_at in range(HEADS // 2):
        pair = columns(pair_at, LANES)
        grad_pair = grads[:, pair]
        dprobs = dot_t(both_heads(v_ref[:, pair]), grad_pair)
        probs = []
        for half in range(2):
            h = 2 * pair_at + half
            prob = jnp.exp(scores[:, h : h + 1] - logs[h] + bias)
            term = prob * (dprobs[columns(half, tok)] - deltas[h])
            sigma = jnp.where(lane_u == h, jnp.sum(term, axis=1, keepdims=True), sigma)
            probs.append(prob.astype(BF16))
        parts = dot(jnp.concatenate(probs, axis=0), grad_pair)
        dvalues[:, pair] = jnp.where(lane_u < HEAD_DIM, parts[:tok], parts[tok:]).astype(BF16)
    high = sigma.astype(BF16).astype(F32)
    low = (sigma - high).astype(BF16).astype(F32)
    split = (high + pltpu.roll(low, 16, 1) + pltpu.roll(high, 32, 1)).astype(BF16)
    copies[11].wait()
    copies[12].wait()
    squares = jnp.zeros((1, 1), F32)
    outs = []
    part = 2 * LANES
    for at_part in range(width // part):
        cols = columns(at_part, part)
        raw = dot_t(dvalues[...], wv_ref[cols]) + dot(split, qk_ref[:, cols])
        raw_ref[:, cols] = raw
        outs.append(
            pltpu.make_async_copy(raw_ref.at[:, cols], raw_hbm.at[:, cols], out_sems.at[at_part])
        )
        outs[-1].start()
        total = jnp.sum(raw * raw, axis=0, keepdims=True)
        squares = squares + jnp.sum(total, axis=1, keepdims=True)
    square_ref[...] = jnp.broadcast_to(squares, square_ref.shape)
    for copy in outs:
        copy.wait()


def own_kernel(
    q_hbm, k_hbm, v_hbm, km_ref, vm_ref, bits_ref,
    log_ref, mixed_ref,
    q_ref, k_ref, v_ref, in_sems,
):
    tok, width = q_ref.shape
    pairs = HEADS // 2
    copies = start_all(
        [
            pltpu.make_async_copy(src, dst, in_sems.at[i])
            for i, (src, dst) in enumerate(((q_hbm, q_ref), (k_hbm, k_ref), (v_hbm, v_ref)))
        ]
    )
    row_b, col_b = iota((tok, tok), 0) // BLOCK, iota((tok, tok), 1) // BLOCK
    masked = token_mask_row(bits_ref[...], tok)
    own_bias = jnp.where((col_b < row_b) | ((col_b == row_b) & (masked < 0.5)), 0.0, -jnp.inf)
    count = jnp.sum(jnp.where(row_b == col_b, masked, 0.0), axis=1, keepdims=True)
    mask_bias = jnp.where(iota((tok, LANES), 1).astype(F32) < count, 0.0, -jnp.inf)
    bias = jnp.concatenate([own_bias, mask_bias], axis=1)
    bias = jnp.concatenate([bias, bias], axis=0)
    lane = iota((tok, LANES), 1)
    logs = jnp.zeros((tok, LANES), F32)
    for copy in copies:
        copy.wait()
    for pair_at in range(pairs):
        pair = columns(pair_at, LANES)
        k_mask = jnp.broadcast_to(km_ref[0:1, pair], (LANES, LANES))
        v_mask = jnp.broadcast_to(vm_ref[0:1, pair], (LANES, LANES))
        keys = jnp.concatenate([k_ref[:, pair], k_mask], axis=0)
        vals = jnp.concatenate([v_ref[:, pair], v_mask], axis=0)
        score = dot_t(both_heads(q_ref[:, pair]), keys) + bias
        peak = jnp.max(score, axis=1, keepdims=True)
        expo = jnp.exp(score - peak)
        den = jnp.sum(expo, axis=1, keepdims=True)
        mixed = dot(expo.astype(BF16), vals) / den
        log = peak + jnp.log(den)
        logs = jnp.where(lane == 2 * pair_at, log[:tok], logs)
        logs = jnp.where(lane == 2 * pair_at + 1, log[tok:], logs)
        mixed_ref[:, pair] = jnp.where(lane < HEAD_DIM, mixed[:tok], mixed[tok:]).astype(BF16)
    log_ref[...] = logs


def rest_kernel(
    place_ref, far_hbm, two_hbm, ones_hbm,
    wk_hbm, wv_hbm, q_hbm, mixed_hbm, log_hbm, after_hbm,
    out_ref,
    rows, wk_ref, wv_ref, q_ref, mixed_ref, log_ref, keys, vals, total_ref, in_sems,
):
    tok, width = q_ref.shape
    shards = rows.shape[0]
    mine = place_ref[0]
    part = 2 * LANES
    parts = width // part

    def load(src, dst, at):
        return pltpu.make_async_copy(src, dst, in_sems.at[at])

    weights = []
    for at in range(parts):
        cols = columns(at, part)
        for i, (src, dst) in enumerate(((wk_hbm, wk_ref), (wv_hbm, wv_ref))):
            weights.append(load(src.at[:, cols], dst.at[:, cols], shards + 2 * at + i))
    others = [
        load(src, dst, shards + 2 * parts + i)
        for i, (src, dst) in enumerate(((q_hbm, q_ref), (mixed_hbm, mixed_ref), (log_hbm, log_ref)))
    ]
    shard_copies = [
        load(src, rows.at[at], at)
        for at, src in enumerate((far_hbm, two_hbm, ones_hbm.at[0], ones_hbm.at[1]))
    ]
    start_all(shard_copies[:1])
    start_all(weights[:2])
    start_all(shard_copies[1:])
    start_all(others)
    start_all(weights[2:])
    row_b, col_b = iota((tok, tok), 0) // BLOCK, iota((tok, tok), 1) // BLOCK
    far_bias = jnp.where((col_b >= row_b) & (mine >= GROUP), 0.0, NEVER)
    far_bias = jnp.concatenate([far_bias, far_bias], axis=0)
    biases = [far_bias] + [jnp.where(mine >= back, 0.0, NEVER) for back in (2, 1, 3)]
    lane = iota((tok, LANES), 1)
    for at in range(parts):
        cols = columns(at, part)
        for copy in weights[2 * at : 2 * at + 2]:
            copy.wait()
        for place in range(shards):
            if at == 0:
                shard_copies[place].wait()
            span = columns(place, tok)
            keys[span, cols] = dot(rows[place], wk_ref[:, cols]).astype(BF16)
            vals[span, cols] = dot(rows[place], wv_ref[:, cols]).astype(BF16)
    for copy in others:
        copy.wait()
    logs = jnp.zeros((tok, LANES), F32)
    for pair_at in range(HEADS // 2):
        pair = columns(pair_at, LANES)
        score = dot_t(both_heads(q_ref[:, pair]), keys[:, pair])
        pieces = [score[:, columns(place, tok)] + biases[place] for place in range(shards)]
        peak = jnp.maximum(jnp.maximum(pieces[0], pieces[1]), jnp.maximum(pieces[2], pieces[3]))
        peak = jnp.max(peak, axis=1, keepdims=True)
        pieces = [jnp.exp(piece - peak) for piece in pieces]
        den = jnp.sum((pieces[0] + pieces[1]) + (pieces[2] + pieces[3]), axis=1, keepdims=True)
        expo = jnp.concatenate([piece.astype(BF16) for piece in pieces], axis=1)
        mixed = dot(expo, vals[:, pair]) / den
        log = peak + jnp.log(den)
        logs = jnp.where(lane == 2 * pair_at, log[:tok], logs)
        logs = jnp.where(lane == 2 * pair_at + 1, log[tok:], logs)
        total_ref[:, pair] = jnp.where(lane < HEAD_DIM, mixed[:tok], mixed[tok:])
    share = 1.0 / (1.0 + jnp.exp(logs - log_ref[...]))
    high = share.astype(BF16)
    less = (share - high.astype(F32)).astype(BF16)
    head_of = iota((LANES, width), 1) // HEAD_DIM == iota((LANES, width), 0)
    spread = jnp.where(head_of, 1.0, 0.0).astype(BF16)
    share = dot(high, spread) + dot(less, spread)
    total = total_ref[...]
    out_ref[...] = (total + share * (mixed_ref[...].astype(F32) - total)).astype(BF16)


def scale_kernel(entries, square_hbm, raw_hbm, out_hbm, square_ref, raw_ref, in_sems, out_sems):
    tok = raw_ref.shape[0]
    pieces = 4
    spans = [columns(at, tok // pieces) for at in range(pieces)]
    first = pltpu.make_async_copy(square_hbm, square_ref, in_sems.at[pieces])
    first.start()
    copies = start_all(
        [
            pltpu.make_async_copy(raw_hbm.at[span], raw_ref.at[span], in_sems.at[at])
            for at, span in enumerate(spans)
        ]
    )
    first.wait()
    total = jnp.sum(square_ref[:, 0:1], axis=0, keepdims=True)
    rms = jnp.sqrt(total / entries + EPS)
    factor = jnp.minimum(1.0, CLIP / rms)
    outs = []
    for at, span in enumerate(spans):
        copies[at].wait()
        raw_ref[span] = raw_ref[span] * factor
        outs.append(pltpu.make_async_copy(raw_ref.at[span], out_hbm.at[span], out_sems.at[at]))
        outs[-1].start()
    for copy in outs:
        copy.wait()


def call(kernel, out_shape, hbm_out, args, scratch, smem=(), vmem=(), flops=0):
    args = [pltpu.with_memory_space_constraint(array, pltpu.HBM) for array in (*args, *vmem)]
    kinds = [pltpu.SMEM] * len(smem) + [pl.ANY] * (len(args) - len(vmem)) + [pltpu.VMEM] * len(vmem)
    out_kinds = [pltpu.VMEM] * (len(out_shape) - hbm_out) + [pl.ANY] * hbm_out
    return pl.pallas_call(
        kernel,
        out_shape=[pltpu.HBM(array.shape, array.dtype) for array in out_shape],
        in_specs=[pl.BlockSpec(memory_space=kind) for kind in kinds],
        out_specs=[pl.BlockSpec(memory_space=kind) for kind in out_kinds],
        scratch_shapes=scratch,
        compiler_params=pltpu.CompilerParams(vmem_limit_bytes=VMEM_LIMIT),
        cost_estimate=pl.CostEstimate(flops=flops, bytes_accessed=1 << 10, transcendentals=0),
    )(*smem, *args)


def shift(rows, distance):
    devices = range(lax.axis_size("seq"))
    return lax.ppermute(rows, "seq", [(i, i + distance) for i in devices if i + distance in devices])


def swap(rows, bit, test=None):
    devices = range(lax.axis_size("seq"))
    return lax.ppermute(rows, "seq", [(i, i ^ bit) for i in devices if test is None or test(i)])


def on_device(clean, out_cot, mask_bits, levels, importance, w_query, w_key, w_value, mask_embed):
    clean_rows = clean[0]
    tok, width = clean_rows.shape
    blocks = tok // BLOCK
    place = lax.axis_index("seq")
    count = lax.axis_size("seq")
    parts = lax.axis_size("dp") * count
    where = jnp.stack([place, jnp.int32(count * blocks)]).astype(jnp.int32)
    rows = (tok, width)
    square_w = (width, width)

    def like(*dims, dtype=BF16):
        return jax.ShapeDtypeStruct(dims, dtype)

    def vmem(*dims, dtype=BF16):
        return pltpu.VMEM(dims, dtype)

    def sems(count):
        return pltpu.SemaphoreType.DMA((count,))

    with jax.named_scope("local"):
        ratio = importance[0].T
        stats, a, qk, km, vm, q, k, v = call(
            local_kernel,
            [
                like(3, blocks, width), like(tok, LANES, dtype=F32), like(LANES, width),
                like(BLOCK, width), like(BLOCK, width), like(*rows), like(*rows), like(*rows),
            ],
            3,
            [clean_rows, w_key, w_value, w_query, out_cot[0], mask_embed, mask_bits, levels, ratio],
            [
                vmem(*rows), vmem(*square_w), vmem(*square_w), vmem(*square_w), vmem(*rows),
                vmem(width), vmem(1, blocks, dtype=jnp.int32), vmem(1, blocks, dtype=jnp.int32),
                vmem(2, blocks, dtype=jnp.int32), vmem(*rows), vmem(*rows), vmem(*rows),
                sems(9), sems(3),
            ],
            flops=1_000_000_000,
        )
    with jax.named_scope("halo"):
        back, ahead = shift(stats, GROUP), shift(stats, -GROUP)
        back, ahead, clean_rows = lax.optimization_barrier((back, ahead, clean_rows))
        y2 = swap(jnp.stack([stats, jnp.where(place & 2 == 0, ahead, back)]), 2)
        far = shift(clean_rows, GROUP)
    with jax.named_scope("own"):
        log, mixed = call(
            own_kernel,
            [like(tok, LANES, dtype=F32), like(*rows)],
            0,
            [q, k, v],
            [vmem(*rows), vmem(*rows), vmem(*rows), sems(3)],
            vmem=[km, vm, mask_bits],
            flops=4_000_000_000,
        )
    with jax.named_scope("halo"):
        y2, log, clean_rows = lax.optimization_barrier((y2, log, clean_rows))
        y_last = swap(clean_rows, 2, lambda i: i & 2 == 0)
        y_first = swap(far, 2, lambda i: i & 2 == 2)
        sides = jnp.stack([stats, jnp.where(place & 1 == 0, ahead, back)])
        core4 = swap(jnp.concatenate([sides, y2]), 1)
    with jax.named_scope("grad"):
        square, raw = call(
            grad_kernel,
            [like(parts, LANES, dtype=F32), like(*rows, dtype=F32)],
            1,
            [stats, back, ahead, y2, core4, a, v, qk, w_value],
            [
                vmem(3 * GROUP, 3, blocks, width), vmem(tok, LANES, dtype=F32), vmem(*rows),
                vmem(LANES, width), vmem(*square_w), vmem(*rows), vmem(*rows, dtype=F32),
                sems(13), sems(width // LANES // 2),
            ],
            smem=[where],
            flops=4_000_000_000,
        )
        y_first, y_last, square = lax.optimization_barrier((y_first, y_last, square))
        two = jnp.where(place & 2 == 0, y_first, y_last)
        mine = place & 1 == 0
        ones = swap(jnp.stack([jnp.where(mine, clean_rows, two), jnp.where(mine, two, far)]), 1)
        squares = lax.all_to_all(square, ("dp", "seq"), 0, 0)
    with jax.named_scope("rest"):
        (attn,) = call(
            rest_kernel,
            [like(*rows)],
            0,
            [far, two, ones, w_key, w_value, q, mixed, log, square],
            [
                vmem(GROUP, *rows), vmem(*square_w), vmem(*square_w), vmem(*rows), vmem(*rows),
                vmem(tok, LANES, dtype=F32), vmem(GROUP * tok, width), vmem(GROUP * tok, width),
                vmem(*rows, dtype=F32), sems(GROUP + width // LANES + 3),
            ],
            smem=[where],
            flops=8_000_000_000,
        )
    with jax.named_scope("clip"):
        squares, attn = lax.optimization_barrier((squares, attn))
        entries = float(parts * tok * width)
        (grad,) = call(
            lambda *refs: scale_kernel(entries, *refs),
            [like(*rows, dtype=F32)],
            1,
            [squares, raw],
            [vmem(parts, LANES, dtype=F32), vmem(*rows, dtype=F32), sems(5), sems(4)],
        )
    return attn[None], grad[None]


def solution(mesh):
    in_specs = (
        P("dp", "seq", None),
        P("dp", "seq", None),
        P("dp", "seq"),
        P("dp", "seq"),
        P("dp", "seq", None),
        P(),
        P(),
        P(),
        P(),
    )
    out_specs = (P("dp", "seq", None), P("dp", "seq", None))
    return jax.shard_map(
        on_device, mesh=mesh, in_specs=in_specs, out_specs=out_specs, check_vma=False
    )
```

time: 81.4 us -> 63.8 us (0.78)
  blocking collectives: 13.3 us -> 0 us
  waiting for transfers between devices: 16.7 us -> 9.36 us
  starting transfers between devices: 13.5 us -> 18.2 us
  other arithmetic: 2.91 us -> 1.82 us
    all_to_all x1 -> x0, blocking collectives: 13.3 us -> none  [on_device(): squares = lax.all_to_all(square, ('dp', 'seq'), 0, 0)]
    ppermute x3, waiting for transfers between devices: 10.9 us -> 5.15 us  [shift(): lax.ppermute(rows, 'seq', [(i, i + distance) for i in devices if i + dist...]
    ppermute x4 -> x5, starting transfers between devices: 2.23 us -> 5.38 us  [swap(): lax.ppermute(rows, 'seq', [(i, i ^ bit) for i in devices if test is None...]
    all_to_all x0 -> x1, starting transfers between devices: none -> 3.14 us  [on_device(): squares = lax.all_to_all(square, ('dp', 'seq'), 0, 0)]
    ppermute x4 -> x5, waiting for transfers between devices: 5.83 us -> 4.21 us  [swap(): lax.ppermute(rows, 'seq', [(i, i ^ bit) for i in devices if test is None...]
    ppermute x3, starting transfers between devices: 11.3 us -> 9.72 us  [shift(): lax.ppermute(rows, 'seq', [(i, i + distance) for i in devices if i + dist...]
    select_n x1 -> x0, other arithmetic: 1.18 us -> none  [on_device(): two = swap(jnp.where(place & 2 == 0, clean_rows, far), 2)]
    unnamed x22 -> x20, local copies, waits for them, and re-layouts: 2.26 us -> 2.81 us
  transfers between devices with their start and end apart: 7 -> 9, of which waited for: 5 -> 3; matrix products, arithmetic and copies ran while one was open for 4% -> 1% of each run, Pallas kernels for 19% -> 36%
where the time goes in v2:
time: 63.8 us; the launch traced here: 63.3 us
  Pallas kernels  30.1 us (47%)
  starting transfers between devices  18.2 us (29%)
  waiting for transfers between devices  9.36 us (15%)
  local copies, waits for them, and re-layouts  2.81 us (4%)
  other arithmetic  1.82 us (3%)
  between operations  1.05 us (2%)
    pallas_call x5, Pallas kernels, call(): pl.pallas_call(kernel, out_shape=[pltpu.HBM(array.shape, array.dtype) for...  30.1 us
    ppermute x3, starting transfers between devices, shift(): lax.ppermute(rows, 'seq', [(i, i + distance) for i in devices if i + dist...  9.72 us
    ppermute x5, starting transfers between devices, swap(): lax.ppermute(rows, 'seq', [(i, i ^ bit) for i in devices if test is None...  5.38 us
    ppermute x3, waiting for transfers between devices, shift(): lax.ppermute(rows, 'seq', [(i, i + distance) for i in devices if i + dist...  5.15 us
    ppermute x5, waiting for transfers between devices, swap(): lax.ppermute(rows, 'seq', [(i, i ^ bit) for i in devices if test is None...  4.21 us
    all_to_all x1, starting transfers between devices, on_device(): squares = lax.all_to_all(square, ('dp', 'seq'), 0, 0)  3.14 us
    unnamed x20, local copies, waits for them, and re-layouts  2.81 us
  transfers between devices with their start and end apart: 9, of which 3 were waited for; matrix products, arithmetic and copies ran while one was open for 1% of the time, Pallas kernels for 36%

profile of v2, /device:TPU:0, one launch (start us, length us, event | category | flops | bytes accessed | tf_op | source)
XLA Modules:
  0.0 63.3 jit_solution(515280721973309799)
XLA Ops:
  0.6 0.0 copy-start
  0.6 5.6 %local.1 = (bf16[3,16,768]{2,1,0:T(8,128)(2,1)}, f32[256,128]{1,0:T(8,128)}, bf16[128,768]{1,0:T(8,128)(2,1)}, bf16[16,768]{1,0:T(8,128)(2,1)}, bf16[16,768]{1,0...) custom-call(bf16[256,768]{1,0:T(8,128)(2,1)} %bitcast.21, ...), custom_call_target="tpu_custom_call" | custom-call | flops 1000000000 | bytes 1024 | tf_op jit(solution)/shard_map/local/pallas_call | solution.py:441
  6.3 4.9 %collective-permute-start = (bf16[3,16,768]{2,1,0:T(8,128)(2,1)}, bf16[3,16,768]{2,1,0:T(8,128)(2,1)S(1)}, u32[]{:S(2)}, u32[]{:S(2)}) collective-permute-start(bf16[3,16,768]{2,1,0:T(8,128)(2,1)} %get-tuple-element.25.own_hbm), channel_id=1, source_target_pairs={{0,4},{1,5},{2,6},{3,7},{4,8},{5,9},{6,10},{7,11},{8,12},{9,13},{1... | collective-permute-start | bytes 221192 | tf_op jit(solution)/shard_map/halo/ppermute | solution.py:454
  11.2 1.3 %collective-permute-start.1 = (bf16[3,16,768]{2,1,0:T(8,128)(2,1)}, bf16[3,16,768]{2,1,0:T(8,128)(2,1)S(1)}, u32[]{:S(2)}, u32[]{:S(2)}) collective-permute-start(bf16[3,16,768]{2,1,0:T(8,128)(2,1)} %get-tuple-element.25.own_hbm), channel_id=1, source_target_pairs={{4,0},{5,1},{6,2},{7,3},{8,4},{9,5},{10,6},{11,7},{12,8},{13,9},{1... | collective-permute-start | bytes 221192 | tf_op jit(solution)/shard_map/halo/ppermute | solution.py:454
  12.5 1.0 %collective-permute-done.back_hbm = bf16[3,16,768]{2,1,0:T(8,128)(2,1)S(1)} collective-permute-done((bf16[3,16,768]{2,1,0:T(8,128)(2,1)}, bf16[3,16,768]{2,1,0:T(8,128)(2,1)S(1)}, u32[]{:S(2)}, u32[]{:S(2)}) %collective-permute-start) | collective-permute-done | bytes 73760 | tf_op jit(solution)/shard_map/halo/ppermute | solution.py:454
  13.5 0.0 copy-start.5
  13.5 4.2 %collective-permute-done.1.ahead_hbm = bf16[3,16,768]{2,1,0:T(8,128)(2,1)S(1)} collective-permute-done((bf16[3,16,768]{2,1,0:T(8,128)(2,1)}, bf16[3,16,768]{2,1,0:T(8,128)(2,1)S(1)}, u32[]{:S(2)}, u32[]{:S(2)}) %collective-permute-start.1) | collective-permute-done | bytes 73760 | tf_op jit(solution)/shard_map/halo/ppermute | solution.py:454
  17.6 0.0 copy-start.6
  17.7 0.9 %pad_maximum_fusion.2 = bf16[2,3,16,768]{3,2,1,0:T(8,128)(2,1)S(1)} fusion(bf16[1,3,16,768]{3,2,1,0:T(8,128)(2,1)S(1)} %get-tuple-element.51, bf16[1,3,16,768]{3,2,1,0:T(8,128)(2,1)} %bitcast.27), kind=kLoop, calls=%fused_computation.5 | loop fusion | flops 73728 | bytes 294912 | tf_op jit(solution)/shard_map/halo/stack | solution.py:503
  18.6 1.6 %collective-permute-start.4 = (bf16[2,3,16,768]{3,2,1,0:T(8,128)(2,1)S(1)}, bf16[2,3,16,768]{3,2,1,0:T(8,128)(2,1)S(1)}, u32[]{:S(2)}, u32[]{:S(2)}) collective-permute-start(bf16[2,3,16,768]{3,2,1,0:T(8,128)(2,1)S(1)} %pad_maximum_fusion.2), channel_id=1, source_target_pairs={{0,2},{1,3},{2,0},{3,1},{4,6},{5,7},{6,4},{7,5},{8,10},{9,11},{10,... | collective-permute-start | bytes 442376 | tf_op jit(solution)/shard_map/halo/ppermute | solution.py:459
  20.2 0.0 copy-done
  20.2 3.5 %collective-permute-start.2 = (bf16[256,768]{1,0:T(8,128)(2,1)S(1)}, bf16[256,768]{1,0:T(8,128)(2,1)S(1)}, u32[]{:S(2)}, u32[]{:S(2)}) collective-permute-start(bf16[256,768]{1,0:T(8,128)(2,1)S(1)} %bitcast.22), channel_id=1, source_target_pairs={{0,4},{1,5},{2,6},{3,7},{4,8},{5,9},{6,10},{7,11},{8,12},{9,13},{1... | collective-permute-start | bytes 1179656 | tf_op jit(solution)/shard_map/halo/ppermute | solution.py:454
  23.7 0.0 copy-start.3
  23.7 5.3 %own.1 = (f32[256,128]{1,0:T(8,128)}, bf16[256,768]{1,0:T(8,128)(2,1)}) custom-call(bf16[256,768]{1,0:T(8,128)(2,1)} %get-tuple-element.29.q_hbm, bf16[256,768]{1,0:T(8,128)(2,1)} %get-tuple-element.30.k_hbm, bf16[256,768]{1,0:T(8,128)(2,1)} %get-tuple-element.31.v_hbm, bf16[16,768]{1,0:T(8,128)(2,1)} %get-tuple-element.32.km_ref, ...), custom_call_target="tpu_custom_call" | custom-call | flops 4000000000 | bytes 1024 | tf_op jit(solution)/shard_map/own/pallas_call | solution.py:441
  29.0 0.0 copy-done.5
  29.0 0.0 copy-done.6
  29.1 0.0 collective-permute-done.4.y_hbm
  29.1 0.0 copy-start.4
  29.1 0.0 copy-done.3
  29.1 0.1 collective-permute-start.6
  29.2 2.4 %collective-permute-start.5 = (bf16[256,768]{1,0:T(8,128)(2,1)S(1)}, bf16[256,768]{1,0:T(8,128)(2,1)S(1)}, u32[]{:S(2)}, u32[]{:S(2)}) collective-permute-start(bf16[256,768]{1,0:T(8,128)(2,1)S(1)} %bitcast.23), channel_id=1, source_target_pairs={{0,2},{1,3},{4,6},{5,7},{8,10},{9,11},{12,14},{13,15},{16,18},{17,... | collective-permute-start | bytes 1179656 | tf_op jit(solution)/shard_map/halo/ppermute | solution.py:459
  31.6 0.0 collective-permute-done.2.far_hbm
  31.6 0.0 copy-start.2
  31.7 1.3 %collective-permute-start.3 = (bf16[256,768]{1,0:T(8,128)(2,1)S(1)}, bf16[256,768]{1,0:T(8,128)(2,1)S(1)}, u32[]{:S(2)}, u32[]{:S(2)}) collective-permute-start(bf16[256,768]{1,0:T(8,128)(2,1)S(1)} %collective-permute-done.2.far_hbm), channel_id=1, source_target_pairs={{2,0},{3,1},{6,4},{7,5},{10,8},{11,9},{14,12},{15,13},{18,16},{19,... | collective-permute-start | bytes 1179656 | tf_op jit(solution)/shard_map/halo/ppermute | solution.py:459
  33.0 0.7 %pad_add_fusion.place_ref = s32[2]{0:T(128)} fusion(s32[1]{0:T(128)} %constant.3.clone.1, s32[1]{0:T(128)} %bitcast.6), kind=kLoop, calls=%fused_computation.8 | loop fusion | flops 2 | bytes 16 | tf_op jit(solution)/shard_map/stack | solution.py:469
  33.6 0.0 collective-permute-done.6.c_hbm
  33.6 0.0 copy-start.9
  33.6 0.0 copy-done.4
  33.6 0.7 %copy-done.9 = bf16[4,3,16,768]{3,2,1,0:T(8,128)(2,1)} copy-done((bf16[4,3,16,768]{3,2,1,0:T(8,128)(2,1)}, bf16[4,3,16,768]{3,2,1,0:T(8,128)(2,1)S(1)}, u32[]{:S(2)}) %copy-start.9) | copy-done | bytes 294936
  34.3 6.2 %grad.1 = (f32[32,128]{1,0:T(8,128)}, f32[256,768]{1,0:T(8,128)}) custom-call(s32[2]{0:T(128)} %pad_add_fusion.place_ref, bf16[3,16,768]{2,1,0:T(8,128)(2,1)} %get-tuple-element.25.own_hbm, bf16[3,16,768]{2,1,0:T(8,128)(2,1)} %copy-done.5, bf16[3,16,768]{2,1,0:T(8,128)(2,1)} %copy-done.6, bf16[2,3,16,768]{3,2,1,0:T(8,128)(2,1)} %copy-done.4, ...), custom_call_target="tpu_custom_call" | custom-call | flops 4000000000 | bytes 1024 | tf_op jit(solution)/shard_map/grad/pallas_call | solution.py:441
  40.6 0.0 collective-permute-done.5
  40.6 4.2 %collective-permute-done.3 = bf16[256,768]{1,0:T(8,128)(2,1)S(1)} collective-permute-done((bf16[256,768]{1,0:T(8,128)(2,1)S(1)}, bf16[256,768]{1,0:T(8,128)(2,1)S(1)}, u32[]{:S(2)}, u32[]{:S(2)}) %collective-permute-start.3) | collective-permute-done | bytes 393248 | tf_op jit(solution)/shard_map/halo/ppermute | solution.py:459
  44.8 0.1 select_bitcast_fusion.1
  44.8 0.0 copy-start.1
  44.9 0.0 copy-done.2
  44.9 0.1 pad_maximum_fusion
  45.0 0.6 copy-done.1
  45.6 0.0 collective-permute-start.7
  45.6 3.1 %all-to-all-start = ((f32[32,1,128]{2,1,0:T(1,128)}), f32[32,1,128]{2,1,0:T(1,128)S(1)}, u32[]{:S(2)}, u32[]{:S(2)}) async-start(f32[32,1,128]{2,1,0:T(1,128)} %bitcast.9), calls=%async_computation | async-start | bytes 32768 | tf_op jit(solution)/shard_map/grad/all_to_all | solution.py:539
  48.8 0.0 collective-permute-done.7.ones_hbm
  48.8 0.0 copy-start.8
  48.8 0.9 %copy-done.8 = bf16[2,256,768]{2,1,0:T(8,128)(2,1)} copy-done((bf16[2,256,768]{2,1,0:T(8,128)(2,1)}, bf16[2,256,768]{2,1,0:T(8,128)(2,1)S(1)}, u32[]{:S(2)}) %copy-start.8) | copy-done | bytes 786456
  49.7 10.9 %rest.1 = bf16[256,768]{1,0:T(8,128)(2,1)} custom-call(s32[2]{0:T(128)} %pad_add_fusion.place_ref, bf16[256,768]{1,0:T(8,128)(2,1)} %copy-done.2, bf16[256,768]{1,0:T(8,128)(2,1)} %copy-done.1, bf16[2,256,768]{2,1,0:T(8,128)(2,1)} %copy-done.8, bf16[768,768]{1,0:T(8,128)(2,1)} %wk_hbm.3, bf16[768,768]{1,0:T(8,128)(2,1)} %wv_hbm.5, ...), custom_call_target="tpu_custom_call" | custom-call | flops 8000000000 | bytes 1024 | tf_op jit(solution)/shard_map/rest/pallas_call | solution.py:441
  60.6 0.0 all-to-all-done
  60.6 0.0 copy-start.7
  60.6 0.6 copy-done.7
  61.2 2.0 %clip.1 = f32[256,768]{1,0:T(8,128)} custom-call(f32[32,128]{1,0:T(8,128)} %bitcast.29, f32[256,768]{1,0:T(8,128)} %get-tuple-element.47.refs_1_), custom_call_target="tpu_custom_call" | custom-call | bytes 1024 | tf_op jit(solution)/shard_map/clip/pallas_call | solution.py:441
  (3 shorter events, 0.1 us)
Async XLA Ops:
  0.6 19.6 %copy-start = (bf16[1,256,768]{2,1,0:T(8,128)(2,1)S(1)}, bf16[1,256,768]{2,1,0:T(8,128)(2,1)}, u32[]{:S(2)}) copy-start(bf16[1,256,768]{2,1,0:T(8,128)(2,1)} %param.9) | copy-start | bytes 1179652
  6.3 7.2 %collective-permute-start = (bf16[3,16,768]{2,1,0:T(8,128)(2,1)}, bf16[3,16,768]{2,1,0:T(8,128)(2,1)S(1)}, u32[]{:S(2)}, u32[]{:S(2)}) collective-permute-start(bf16[3,16,768]{2,1,0:T(8,128)(2,1)} %get-tuple-element.25.own_hbm), channel_id=1, source_target_pairs={{0,4},{1,5},{2,6},{3,7},{4,8},{5,9},{6,10},{7,11},{8,12},{9,13},{1... | collective-permute-start | bytes 221192 | tf_op jit(solution)/shard_map/halo/ppermute | solution.py:454
  11.2 6.5 %collective-permute-start.1 = (bf16[3,16,768]{2,1,0:T(8,128)(2,1)}, bf16[3,16,768]{2,1,0:T(8,128)(2,1)S(1)}, u32[]{:S(2)}, u32[]{:S(2)}) collective-permute-start(bf16[3,16,768]{2,1,0:T(8,128)(2,1)} %get-tuple-element.25.own_hbm), channel_id=1, source_target_pairs={{4,0},{5,1},{6,2},{7,3},{8,4},{9,5},{10,6},{11,7},{12,8},{13,9},{1... | collective-permute-start | bytes 221192 | tf_op jit(solution)/shard_map/halo/ppermute | solution.py:454
  13.5 15.6 %copy-start.5 = (bf16[3,16,768]{2,1,0:T(8,128)(2,1)}, bf16[3,16,768]{2,1,0:T(8,128)(2,1)S(1)}, u32[]{:S(2)}) copy-start(bf16[3,16,768]{2,1,0:T(8,128)(2,1)S(1)} %collective-permute-done.back_hbm) | copy-start | bytes 221188
  17.6 11.4 %copy-start.6 = (bf16[3,16,768]{2,1,0:T(8,128)(2,1)}, bf16[3,16,768]{2,1,0:T(8,128)(2,1)S(1)}, u32[]{:S(2)}) copy-start(bf16[3,16,768]{2,1,0:T(8,128)(2,1)S(1)} %collective-permute-done.1.ahead_hbm) | copy-start | bytes 221188
  18.6 10.5 %collective-permute-start.4 = (bf16[2,3,16,768]{3,2,1,0:T(8,128)(2,1)S(1)}, bf16[2,3,16,768]{3,2,1,0:T(8,128)(2,1)S(1)}, u32[]{:S(2)}, u32[]{:S(2)}) collective-permute-start(bf16[2,3,16,768]{3,2,1,0:T(8,128)(2,1)S(1)} %pad_maximum_fusion.2), channel_id=1, source_target_pairs={{0,2},{1,3},{2,0},{3,1},{4,6},{5,7},{6,4},{7,5},{8,10},{9,11},{10,... | collective-permute-start | bytes 442376 | tf_op jit(solution)/shard_map/halo/ppermute | solution.py:459
  20.2 11.5 %collective-permute-start.2 = (bf16[256,768]{1,0:T(8,128)(2,1)S(1)}, bf16[256,768]{1,0:T(8,128)(2,1)S(1)}, u32[]{:S(2)}, u32[]{:S(2)}) collective-permute-start(bf16[256,768]{1,0:T(8,128)(2,1)S(1)} %bitcast.22), channel_id=1, source_target_pairs={{0,4},{1,5},{2,6},{3,7},{4,8},{5,9},{6,10},{7,11},{8,12},{9,13},{1... | collective-permute-start | bytes 1179656 | tf_op jit(solution)/shard_map/halo/ppermute | solution.py:454
  23.7 5.4 %copy-start.3 = (bf16[3,16,768]{2,1,0:T(8,128)(2,1)S(1)}, bf16[3,16,768]{2,1,0:T(8,128)(2,1)}, u32[]{:S(2)}) copy-start(bf16[3,16,768]{2,1,0:T(8,128)(2,1)} %get-tuple-element.25.own_hbm) | copy-start | bytes 221188
  29.1 4.6 %copy-start.4 = (bf16[2,3,16,768]{3,2,1,0:T(8,128)(2,1)}, bf16[2,3,16,768]{3,2,1,0:T(8,128)(2,1)S(1)}, u32[]{:S(2)}) copy-start(bf16[2,3,16,768]{3,2,1,0:T(8,128)(2,1)S(1)} %collective-permute-done.4.y_hbm) | copy-start | bytes 442372
  29.1 4.5 %collective-permute-start.6 = (bf16[4,3,16,768]{3,2,1,0:T(8,128)(2,1)S(1)}, bf16[4,3,16,768]{3,2,1,0:T(8,128)(2,1)S(1)}, u32[]{:S(2)}, u32[]{:S(2)}) collective-permute-start(bf16[4,3,16,768]{3,2,1,0:T(8,128)(2,1)S(1)} %pad_maximum_fusion.1), channel_id=1, source_target_pairs={{0,1},{1,0},{2,3},{3,2},{4,5},{5,4},{6,7},{7,6},{8,9},{9,8},{10,11... | collective-permute-start | bytes 884744 | tf_op jit(solution)/shard_map/halo/ppermute | solution.py:459
  29.2 11.4 %collective-permute-start.5 = (bf16[256,768]{1,0:T(8,128)(2,1)S(1)}, bf16[256,768]{1,0:T(8,128)(2,1)S(1)}, u32[]{:S(2)}, u32[]{:S(2)}) collective-permute-start(bf16[256,768]{1,0:T(8,128)(2,1)S(1)} %bitcast.23), channel_id=1, source_target_pairs={{0,2},{1,3},{4,6},{5,7},{8,10},{9,11},{12,14},{13,15},{16,18},{17,... | collective-permute-start | bytes 1179656 | tf_op jit(solution)/shard_map/halo/ppermute | solution.py:459
  31.6 13.2 %copy-start.2 = (bf16[256,768]{1,0:T(8,128)(2,1)}, bf16[256,768]{1,0:T(8,128)(2,1)S(1)}, u32[]{:S(2)}) copy-start(bf16[256,768]{1,0:T(8,128)(2,1)S(1)} %collective-permute-done.2.far_hbm) | copy-start | bytes 1179652
  31.7 13.1 %collective-permute-start.3 = (bf16[256,768]{1,0:T(8,128)(2,1)S(1)}, bf16[256,768]{1,0:T(8,128)(2,1)S(1)}, u32[]{:S(2)}, u32[]{:S(2)}) collective-permute-start(bf16[256,768]{1,0:T(8,128)(2,1)S(1)} %collective-permute-done.2.far_hbm), channel_id=1, source_target_pairs={{2,0},{3,1},{6,4},{7,5},{10,8},{11,9},{14,12},{15,13},{18,16},{19,... | collective-permute-start | bytes 1179656 | tf_op jit(solution)/shard_map/halo/ppermute | solution.py:459
  33.6 0.7 %copy-start.9 = (bf16[4,3,16,768]{3,2,1,0:T(8,128)(2,1)}, bf16[4,3,16,768]{3,2,1,0:T(8,128)(2,1)S(1)}, u32[]{:S(2)}) copy-start(bf16[4,3,16,768]{3,2,1,0:T(8,128)(2,1)S(1)} %collective-permute-done.6.c_hbm) | copy-start | bytes 884740
  44.8 0.8 %copy-start.1 = (bf16[256,768]{1,0:T(8,128)(2,1)}, bf16[256,768]{1,0:T(8,128)(2,1)S(1)}, u32[]{:S(2)}) copy-start(bf16[256,768]{1,0:T(8,128)(2,1)S(1)} %get-tuple-element.49.two_hbm) | copy-start | bytes 1179652
  45.6 3.2 %collective-permute-start.7 = (bf16[2,256,768]{2,1,0:T(8,128)(2,1)S(1)}, bf16[2,256,768]{2,1,0:T(8,128)(2,1)S(1)}, u32[]{:S(2)}, u32[]{:S(2)}) collective-permute-start(bf16[2,256,768]{2,1,0:T(8,128)(2,1)S(1)} %pad_maximum_fusion), channel_id=1, source_target_pairs={{0,1},{1,0},{2,3},{3,2},{4,5},{5,4},{6,7},{7,6},{8,9},{9,8},{10,11... | collective-permute-start | bytes 2359304 | tf_op jit(solution)/shard_map/grad/ppermute | solution.py:459
  45.6 15.0 %all-to-all-start = ((f32[32,1,128]{2,1,0:T(1,128)}), f32[32,1,128]{2,1,0:T(1,128)S(1)}, u32[]{:S(2)}, u32[]{:S(2)}) async-start(f32[32,1,128]{2,1,0:T(1,128)} %bitcast.9), calls=%async_computation | async-start | bytes 32768 | tf_op jit(solution)/shard_map/grad/all_to_all | solution.py:539
  48.8 0.9 %copy-start.8 = (bf16[2,256,768]{2,1,0:T(8,128)(2,1)}, bf16[2,256,768]{2,1,0:T(8,128)(2,1)S(1)}, u32[]{:S(2)}) copy-start(bf16[2,256,768]{2,1,0:T(8,128)(2,1)S(1)} %collective-permute-done.7.ones_hbm) | copy-start | bytes 2359300
  60.6 0.6 copy-start.7

commit v3 on v2

--- a/solution.py
+++ b/solution.py
@@ -19,7 +19,7 @@
 GROUP = 4
 F32 = jnp.float32
 BF16 = jnp.bfloat16
-VMEM_LIMIT = 56 * 1024 * 1024
+VMEM_LIMIT = 32 * 1024 * 1024
 SCALE = 1.0 / math.sqrt(HEAD_DIM)
 
 
@@ -178,9 +178,9 @@
 
 
 def grad_kernel(
-    place_ref, own_hbm, back_hbm, ahead_hbm, y_hbm, c_hbm, a_hbm, v_hbm, qk_hbm, wv_hbm,
-    square_ref, raw_hbm,
-    held, a_ref, v_ref, qk_ref, wv_ref, dvalues, raw_ref, in_sems, out_sems,
+    place_ref, back_hbm, ahead_hbm, y_hbm, c_hbm, own_hbm, a_hbm, v_hbm, qk_hbm, wv_hbm,
+    square_ref, raw_ref,
+    held, a_ref, v_ref, qk_ref, wv_ref, dvalues, in_sems,
 ):
     tok, width = v_ref.shape
     blocks = tok // BLOCK
@@ -273,37 +273,29 @@
     split = (high + pltpu.roll(low, 16, 1) + pltpu.roll(high, 32, 1)).astype(BF16)
     copies[11].wait()
     copies[12].wait()
-    squares = jnp.zeros((1, 1), F32)
-    outs = []
-    part = 2 * LANES
-    for at_part in range(width // part):
-        cols = columns(at_part, part)
-        raw = dot_t(dvalues[...], wv_ref[cols]) + dot(split, qk_ref[:, cols])
-        raw_ref[:, cols] = raw
-        outs.append(
-            pltpu.make_async_copy(raw_ref.at[:, cols], raw_hbm.at[:, cols], out_sems.at[at_part])
-        )
-        outs[-1].start()
-        total = jnp.sum(raw * raw, axis=0, keepdims=True)
-        squares = squares + jnp.sum(total, axis=1, keepdims=True)
-    square_ref[...] = jnp.broadcast_to(squares, square_ref.shape)
-    for copy in outs:
-        copy.wait()
+    raw = dot_t(dvalues[...], wv_ref[...]) + dot(split, qk_ref[...])
+    raw_ref[...] = raw
+    total = jnp.sum(raw * raw, axis=0, keepdims=True)
+    total = jnp.sum(total, axis=1, keepdims=True)
+    square_ref[...] = jnp.broadcast_to(total, square_ref.shape)
 
 
 def own_kernel(
-    q_hbm, k_hbm, v_hbm, km_ref, vm_ref, bits_ref,
+    q_hbm, k_hbm, v_hbm, km_hbm, vm_hbm, bits_hbm,
     log_ref, mixed_ref,
-    q_ref, k_ref, v_ref, in_sems,
+    bits_ref, q_ref, k_ref, v_ref, km_ref, vm_ref, in_sems,
 ):
     tok, width = q_ref.shape
     pairs = HEADS // 2
+    sources = (bits_hbm, q_hbm, k_hbm, v_hbm, km_hbm, vm_hbm)
+    targets = (bits_ref, q_ref, k_ref, v_ref, km_ref, vm_ref)
     copies = start_all(
         [
             pltpu.make_async_copy(src, dst, in_sems.at[i])
-            for i, (src, dst) in enumerate(((q_hbm, q_ref), (k_hbm, k_ref), (v_hbm, v_ref)))
+            for i, (src, dst) in enumerate(zip(sources, targets))
         ]
     )
+    copies[0].wait()
     row_b, col_b = iota((tok, tok), 0) // BLOCK, iota((tok, tok), 1) // BLOCK
     masked = token_mask_row(bits_ref[...], tok)
     own_bias = jnp.where((col_b < row_b) | ((col_b == row_b) & (masked < 0.5)), 0.0, -jnp.inf)
@@ -313,7 +305,7 @@
     bias = jnp.concatenate([bias, bias], axis=0)
     lane = iota((tok, LANES), 1)
     logs = jnp.zeros((tok, LANES), F32)
-    for copy in copies:
+    for copy in copies[1:]:
         copy.wait()
     for pair_at in range(pairs):
         pair = columns(pair_at, LANES)
@@ -334,8 +326,7 @@
 
 
 def rest_kernel(
-    place_ref, far_hbm, two_hbm, ones_hbm,
-    wk_hbm, wv_hbm, q_hbm, mixed_hbm, log_hbm, after_hbm,
+    place_ref, far_hbm, two_hbm, one_hbm, three_hbm, q_hbm, mixed_hbm, log_hbm, after_hbm, wk_hbm, wv_hbm,
     out_ref,
     rows, wk_ref, wv_ref, q_ref, mixed_ref, log_ref, keys, vals, total_ref, in_sems,
 ):
@@ -359,7 +350,7 @@
     ]
     shard_copies = [
         load(src, rows.at[at], at)
-        for at, src in enumerate((far_hbm, two_hbm, ones_hbm.at[0], ones_hbm.at[1]))
+        for at, src in enumerate((far_hbm, two_hbm, one_hbm, three_hbm))
     ]
     start_all(shard_copies[:1])
     start_all(weights[:2])
@@ -408,39 +399,30 @@
     out_ref[...] = (total + share * (mixed_ref[...].astype(F32) - total)).astype(BF16)
 
 
-def scale_kernel(entries, square_hbm, raw_hbm, out_hbm, square_ref, raw_ref, in_sems, out_sems):
+def scale_kernel(entries, square_ref, raw_ref, out_hbm, out_ref, sems):
     tok = raw_ref.shape[0]
     pieces = 4
-    spans = [columns(at, tok // pieces) for at in range(pieces)]
-    first = pltpu.make_async_copy(square_hbm, square_ref, in_sems.at[pieces])
-    first.start()
-    copies = start_all(
-        [
-            pltpu.make_async_copy(raw_hbm.at[span], raw_ref.at[span], in_sems.at[at])
-            for at, span in enumerate(spans)
-        ]
-    )
-    first.wait()
     total = jnp.sum(square_ref[:, 0:1], axis=0, keepdims=True)
     rms = jnp.sqrt(total / entries + EPS)
     factor = jnp.minimum(1.0, CLIP / rms)
     outs = []
-    for at, span in enumerate(spans):
-        copies[at].wait()
-        raw_ref[span] = raw_ref[span] * factor
-        outs.append(pltpu.make_async_copy(raw_ref.at[span], out_hbm.at[span], out_sems.at[at]))
+    for at in range(pieces):
+        span = columns(at, tok // pieces)
+        out_ref[span] = raw_ref[span] * factor
+        outs.append(pltpu.make_async_copy(out_ref.at[span], out_hbm.at[span], sems.at[at]))
         outs[-1].start()
     for copy in outs:
         copy.wait()
 
 
-def call(kernel, out_shape, hbm_out, args, scratch, smem=(), vmem=(), flops=0):
-    args = [pltpu.with_memory_space_constraint(array, pltpu.HBM) for array in (*args, *vmem)]
+def call(kernel, out_shape, hbm_out, args, scratch, smem=(), vmem=(), loose=(), flops=0):
+    args = [pltpu.with_memory_space_constraint(array, pltpu.HBM) for array in args]
+    args = [*loose, *args, *vmem]
     kinds = [pltpu.SMEM] * len(smem) + [pl.ANY] * (len(args) - len(vmem)) + [pltpu.VMEM] * len(vmem)
     out_kinds = [pltpu.VMEM] * (len(out_shape) - hbm_out) + [pl.ANY] * hbm_out
     return pl.pallas_call(
         kernel,
-        out_shape=[pltpu.HBM(array.shape, array.dtype) for array in out_shape],
+        out_shape=out_shape,
         in_specs=[pl.BlockSpec(memory_space=kind) for kind in kinds],
         out_specs=[pl.BlockSpec(memory_space=kind) for kind in out_kinds],
         scratch_shapes=scratch,
@@ -454,9 +436,8 @@
     return lax.ppermute(rows, "seq", [(i, i + distance) for i in devices if i + distance in devices])
 
 
-def swap(rows, bit, test=None):
-    devices = range(lax.axis_size("seq"))
-    return lax.ppermute(rows, "seq", [(i, i ^ bit) for i in devices if test is None or test(i)])
+def swap(rows, bit):
+    return lax.ppermute(rows, "seq", [(i, i ^ bit) for i in range(lax.axis_size("seq"))])
 
 
 def on_device(clean, out_cot, mask_bits, levels, importance, w_query, w_key, w_value, mask_embed):
@@ -479,6 +460,8 @@
     def sems(count):
         return pltpu.SemaphoreType.DMA((count,))
 
+    with jax.named_scope("halo"):
+        far = shift(clean_rows, GROUP)
     with jax.named_scope("local"):
         ratio = importance[0].T
         stats, a, qk, km, vm, q, k, v = call(
@@ -499,56 +482,58 @@
         )
     with jax.named_scope("halo"):
         back, ahead = shift(stats, GROUP), shift(stats, -GROUP)
-        back, ahead, clean_rows = lax.optimization_barrier((back, ahead, clean_rows))
-        y2 = swap(jnp.stack([stats, jnp.where(place & 2 == 0, ahead, back)]), 2)
-        far = shift(clean_rows, GROUP)
     with jax.named_scope("own"):
         log, mixed = call(
             own_kernel,
             [like(tok, LANES, dtype=F32), like(*rows)],
             0,
-            [q, k, v],
-            [vmem(*rows), vmem(*rows), vmem(*rows), sems(3)],
-            vmem=[km, vm, mask_bits],
-            flops=4_000_000_000,
+            [mask_bits],
+            [
+                vmem(1, blocks, dtype=jnp.int32), vmem(*rows), vmem(*rows), vmem(*rows),
+                vmem(BLOCK, width), vmem(BLOCK, width), sems(6),
+            ],
+            loose=[q, k, v, km, vm],
+            flops=1_000_000_000,
         )
     with jax.named_scope("halo"):
-        y2, log, clean_rows = lax.optimization_barrier((y2, log, clean_rows))
-        y_last = swap(clean_rows, 2, lambda i: i & 2 == 0)
-        y_first = swap(far, 2, lambda i: i & 2 == 2)
+        back, ahead, far, log = lax.optimization_barrier((back, ahead, far, log))
+        y2 = swap(jnp.stack([stats, jnp.where(place & 2 == 0, ahead, back)]), 2)
+        clean_rows, far = lax.optimization_barrier((clean_rows, far))
+        two = shift(clean_rows, 2)
         sides = jnp.stack([stats, jnp.where(place & 1 == 0, ahead, back)])
         core4 = swap(jnp.concatenate([sides, y2]), 1)
     with jax.named_scope("grad"):
         square, raw = call(
             grad_kernel,
             [like(parts, LANES, dtype=F32), like(*rows, dtype=F32)],
-            1,
-            [stats, back, ahead, y2, core4, a, v, qk, w_value],
+            0,
+            [w_value],
             [
                 vmem(3 * GROUP, 3, blocks, width), vmem(tok, LANES, dtype=F32), vmem(*rows),
-                vmem(LANES, width), vmem(*square_w), vmem(*rows), vmem(*rows, dtype=F32),
-                sems(13), sems(width // LANES // 2),
+                vmem(LANES, width), vmem(*square_w), vmem(*rows), sems(13),
             ],
             smem=[where],
-            flops=4_000_000_000,
+            loose=[back, ahead, y2, core4, stats, a, v, qk],
+            flops=100_000_000,
         )
-        y_first, y_last, square = lax.optimization_barrier((y_first, y_last, square))
-        two = jnp.where(place & 2 == 0, y_first, y_last)
+        two, square = lax.optimization_barrier((two, square))
         mine = place & 1 == 0
-        ones = swap(jnp.stack([jnp.where(mine, clean_rows, two), jnp.where(mine, two, far)]), 1)
+        one = swap(jnp.where(mine, clean_rows, two), 1)
+        three = swap(jnp.where(mine, two, far), 1)
         squares = lax.all_to_all(square, ("dp", "seq"), 0, 0)
     with jax.named_scope("rest"):
         (attn,) = call(
             rest_kernel,
             [like(*rows)],
             0,
-            [far, two, ones, w_key, w_value, q, mixed, log, square],
+            [w_key, w_value],
             [
                 vmem(GROUP, *rows), vmem(*square_w), vmem(*square_w), vmem(*rows), vmem(*rows),
                 vmem(tok, LANES, dtype=F32), vmem(GROUP * tok, width), vmem(GROUP * tok, width),
                 vmem(*rows, dtype=F32), sems(GROUP + width // LANES + 3),
             ],
             smem=[where],
+            loose=[far, two, one, three, q, mixed, log, square],
             flops=8_000_000_000,
         )
     with jax.named_scope("clip"):
@@ -558,8 +543,9 @@
             lambda *refs: scale_kernel(entries, *refs),
             [like(*rows, dtype=F32)],
             1,
-            [squares, raw],
-            [vmem(parts, LANES, dtype=F32), vmem(*rows, dtype=F32), sems(5), sems(4)],
+            [],
+            [vmem(*rows, dtype=F32), sems(4)],
+            vmem=[squares, raw],
         )
     return attn[None], grad[None]
 

time: 63.8 us -> 53.5 us (0.84)
  waiting for transfers between devices: 9.36 us -> 4.74 us
  Pallas kernels: 30.1 us -> 26.6 us
  local copies, waits for them, and re-layouts: 2.81 us -> 0.01 us
  starting transfers between devices: 18.2 us -> 19.8 us
  other arithmetic: 1.82 us -> 1.11 us
    ppermute x3 -> x4, waiting for transfers between devices: 5.15 us -> 1.47 us  [shift(): lax.ppermute(rows, 'seq', [(i, i + distance) for i in devices if i + dist...]
    pallas_call x5, Pallas kernels: 30.1 us -> 26.6 us  [call(): pl.pallas_call(kernel, out_shape=out_shape, in_specs=[pl.BlockSpec(memory...]
    ppermute x5 -> x4, starting transfers between devices: 5.38 us -> 2.16 us  [swap(): lax.ppermute(rows, 'seq', [(i, i ^ bit) for i in range(lax.axis_size('seq...]
    unnamed x20 -> x2, local copies, waits for them, and re-layouts: 2.81 us -> 0.01 us
    ppermute x3 -> x4, starting transfers between devices: 9.72 us -> 12.2 us  [shift(): lax.ppermute(rows, 'seq', [(i, i + distance) for i in devices if i + dist...]
    all_to_all x1, starting transfers between devices: 3.14 us -> 5.53 us  [on_device(): squares = lax.all_to_all(square, ('dp', 'seq'), 0, 0)]
    select_n x0 -> x1, other arithmetic: none -> 0.97 us  [on_device(): three = swap(jnp.where(mine, two, far), 1)]
    ppermute x5 -> x4, waiting for transfers between devices: 4.21 us -> 3.26 us  [swap(): lax.ppermute(rows, 'seq', [(i, i ^ bit) for i in range(lax.axis_size('seq...]
  transfers between devices with their start and end apart: 9 -> 9, of which waited for: 3 -> 3; matrix products, arithmetic and copies ran while one was open for 1% -> 0% of each run, Pallas kernels for 36% -> 48%
where the time goes in v3:
time: 53.5 us; the launch traced here: 53.2 us
  Pallas kernels  26.6 us (50%)
  starting transfers between devices  19.8 us (37%)
  waiting for transfers between devices  4.74 us (9%)
  other arithmetic  1.11 us (2%)
  between operations  0.95 us (2%)
    pallas_call x5, Pallas kernels, call(): pl.pallas_call(kernel, out_shape=out_shape, in_specs=[pl.BlockSpec(memory...  26.6 us
    ppermute x4, starting transfers between devices, shift(): lax.ppermute(rows, 'seq', [(i, i + distance) for i in devices if i + dist...  12.2 us
    all_to_all x1, starting transfers between devices, on_device(): squares = lax.all_to_all(square, ('dp', 'seq'), 0, 0)  5.53 us
    ppermute x4, waiting for transfers between devices, swap(): lax.ppermute(rows, 'seq', [(i, i ^ bit) for i in range(lax.axis_size('seq...  3.26 us
    ppermute x4, starting transfers between devices, swap(): lax.ppermute(rows, 'seq', [(i, i ^ bit) for i in range(lax.axis_size('seq...  2.16 us
    ppermute x4, waiting for transfers between devices, shift(): lax.ppermute(rows, 'seq', [(i, i + distance) for i in devices if i + dist...  1.47 us
  transfers between devices with their start and end apart: 9, of which 3 were waited for; matrix products, arithmetic and copies ran while one was open for 0% of the time, Pallas kernels for 48%

profile of v3, /device:TPU:0, one launch (start us, length us, event | category | flops | bytes accessed | tf_op | source)
XLA Modules:
  0.0 53.2 jit_solution(3963342058172300849)
XLA Ops:
  0.6 5.0 %collective-permute-start.2 = (bf16[256,768]{1,0:T(8,128)(2,1)}, bf16[256,768]{1,0:T(8,128)(2,1)S(1)}, u32[]{:S(2)}, u32[]{:S(2)}) collective-permute-start(bf16[256,768]{1,0:T(8,128)(2,1)} %bitcast.20), channel_id=1, source_target_pairs={{0,4},{1,5},{2,6},{3,7},{4,8},{5,9},{6,10},{7,11},{8,12},{9,13},{1... | collective-permute-start | bytes 1179656 | tf_op jit(solution)/shard_map/halo/ppermute | solution.py:436
  5.6 5.4 %local.1 = (bf16[3,16,768]{2,1,0:T(8,128)(2,1)S(1)}, f32[256,128]{1,0:T(8,128)S(1)}, bf16[128,768]{1,0:T(8,128)(2,1)S(1)}, bf16[16,768]{1,0:T(8,128)(2,1)S(1)}, ...) custom-call(bf16[256,768]{1,0:T(8,128)(2,1)} %bitcast.21, ...), custom_call_target="tpu_custom_call" | custom-call | flops 1000000000 | bytes 1024 | tf_op jit(solution)/shard_map/local/pallas_call | solution.py:423
  11.0 3.5 %collective-permute-start = (bf16[3,16,768]{2,1,0:T(8,128)(2,1)S(1)}, bf16[3,16,768]{2,1,0:T(8,128)(2,1)S(1)}, u32[]{:S(2)}, u32[]{:S(2)}) collective-permute-start(bf16[3,16,768]{2,1,0:T(8,128)(2,1)S(1)} %get-tuple-element.24.own_hbm), channel_id=1, source_target_pairs={{0,4},{1,5},{2,6},{3,7},{4,8},{5,9},{6,10},{7,11},{8,12},{9,13},{1... | collective-permute-start | bytes 221192 | tf_op jit(solution)/shard_map/halo/ppermute | solution.py:436
  14.5 1.3 %collective-permute-start.1 = (bf16[3,16,768]{2,1,0:T(8,128)(2,1)S(1)}, bf16[3,16,768]{2,1,0:T(8,128)(2,1)S(1)}, u32[]{:S(2)}, u32[]{:S(2)}) collective-permute-start(bf16[3,16,768]{2,1,0:T(8,128)(2,1)S(1)} %get-tuple-element.24.own_hbm), channel_id=1, source_target_pairs={{4,0},{5,1},{6,2},{7,3},{8,4},{9,5},{10,6},{11,7},{12,8},{13,9},{1... | collective-permute-start | bytes 221192 | tf_op jit(solution)/shard_map/halo/ppermute | solution.py:436
  15.8 0.0 copy-start
  15.9 3.4 %own.1 = (f32[256,128]{1,0:T(8,128)S(1)}, bf16[256,768]{1,0:T(8,128)(2,1)S(1)}) custom-call(bf16[256,768]{1,0:T(8,128)(2,1)S(1)} %get-tuple-element.25.q_hbm, bf16[256,768]{1,0:T(8,128)(2,1)S(1)} %get-tuple-element.26.k_hbm, bf16[256,768]{1,0:T(8,128)(2,1)S(1)} %get-tuple-element.27.v_hbm, bf16[16,768]{1,0:T(8,128)(2,1)S(1)} %get-tuple-element.28.km_hbm, ...), custom_call_target="tpu_custom_call" | custom-call | flops 1000000000 | bytes 1024 | tf_op jit(solution)/shard_map/own/pallas_call | solution.py:423
  19.3 0.0 collective-permute-done.back_hbm
  19.3 1.5 %collective-permute-done.1.ahead_hbm = bf16[3,16,768]{2,1,0:T(8,128)(2,1)S(1)} collective-permute-done((bf16[3,16,768]{2,1,0:T(8,128)(2,1)S(1)}, bf16[3,16,768]{2,1,0:T(8,128)(2,1)S(1)}, u32[]{:S(2)}, u32[]{:S(2)}) %collective-permute-start.1) | collective-permute-done | bytes 73760 | tf_op jit(solution)/shard_map/halo/ppermute | solution.py:436
  20.8 0.0 collective-permute-done.2.far_hbm
  20.8 1.6 %collective-permute-start.4 = (bf16[2,3,16,768]{3,2,1,0:T(8,128)(2,1)S(1)}, bf16[2,3,16,768]{3,2,1,0:T(8,128)(2,1)S(1)}, u32[]{:S(2)}, u32[]{:S(2)}) collective-permute-start(bf16[2,3,16,768]{3,2,1,0:T(8,128)(2,1)S(1)} %pad_maximum_fusion.1), channel_id=1, source_target_pairs={{0,2},{1,3},{2,0},{3,1},{4,6},{5,7},{6,4},{7,5},{8,10},{9,11},{10,... | collective-permute-start | bytes 442376 | tf_op jit(solution)/shard_map/halo/ppermute | solution.py:440
  22.4 0.0 copy-done
  22.4 2.4 %collective-permute-start.3 = (bf16[256,768]{1,0:T(8,128)(2,1)S(1)}, bf16[256,768]{1,0:T(8,128)(2,1)S(1)}, u32[]{:S(2)}, u32[]{:S(2)}) collective-permute-start(bf16[256,768]{1,0:T(8,128)(2,1)S(1)} %bitcast.22), channel_id=1, source_target_pairs={{0,2},{1,3},{2,4},{3,5},{4,6},{5,7},{6,8},{7,9},{8,10},{9,11},{10,... | collective-permute-start | bytes 1179656 | tf_op jit(solution)/shard_map/halo/ppermute | solution.py:436
  24.9 1.8 %collective-permute-done.4.y_hbm = bf16[2,3,16,768]{3,2,1,0:T(8,128)(2,1)S(1)} collective-permute-done((bf16[2,3,16,768]{3,2,1,0:T(8,128)(2,1)S(1)}, bf16[2,3,16,768]{3,2,1,0:T(8,128)(2,1)S(1)}, u32[]{:S(2)}, u32[]{:S(2)}) %collective-permute-start.4) | collective-permute-done | bytes 147488 | tf_op jit(solution)/shard_map/halo/ppermute | solution.py:440
  26.7 0.1 collective-permute-start.5
  26.7 0.1 pad_add_fusion.place_ref
  26.8 1.5 %collective-permute-done.5.c_hbm = bf16[4,3,16,768]{3,2,1,0:T(8,128)(2,1)S(1)} collective-permute-done((bf16[4,3,16,768]{3,2,1,0:T(8,128)(2,1)S(1)}, bf16[4,3,16,768]{3,2,1,0:T(8,128)(2,1)S(1)}, u32[]{:S(2)}, u32[]{:S(2)}) %collective-permute-start.5) | collective-permute-done | bytes 294944 | tf_op jit(solution)/shard_map/halo/ppermute | solution.py:440
  28.3 5.8 %grad.1 = (f32[32,128]{1,0:T(8,128)}, f32[256,768]{1,0:T(8,128)S(1)}) custom-call(s32[2]{0:T(128)S(1)} %pad_add_fusion.place_ref, bf16[3,16,768]{2,1,0:T(8,128)(2,1)S(1)} %collective-permute-done.back_hbm, bf16[3,16,768]{2,1,0:T(8,128)(2,1)S(1)} %collective-permute-done.1.ahead_hbm, bf16[2,3,16,768]{3,2,1,0:T(8,128)(2,1)S(1)} %collective-permute-done.4.y_hbm, ...), custom_call_target="tpu_custom_call" | custom-call | flops 100000000 | bytes 1024 | tf_op jit(solution)/shard_map/grad/pallas_call | solution.py:423
  34.1 0.0 collective-permute-done.3.two_hbm
  34.1 1.0 %broadcast_select_fusion = (bf16[256,768]{1,0:T(8,128)(2,1)}, bf16[256,768]{1,0:T(8,128)(2,1)}) fusion(bf16[256,768]{1,0:T(8,128)(2,1)S(1)} %collective-permute-done.3.two_hbm, bf16[256,768]{1,0:T(8,128)(2,1)S(1)} %collective-permute-done.2.far_hbm, pred[]{:T(512)S(6)} %eq.8, bf16[256,768]{1,0:T(8,128)(2,1)S(1)} %bitcast.23), kind=kLoop, calls=%fused_computation | loop fusion | flops 393216 | bytes 1966081 | tf_op jit(solution)/shard_map/grad/jit(_where)/select_n | solution.py:522
  35.1 0.2 collective-permute-start.6
  35.2 0.4 collective-permute-start.7
  35.6 5.5 %all-to-all-start = ((f32[32,1,128]{2,1,0:T(1,128)}), f32[32,1,128]{2,1,0:T(1,128)S(1)}, u32[]{:S(2)}, u32[]{:S(2)}) async-start(f32[32,1,128]{2,1,0:T(1,128)} %bitcast.9), calls=%async_computation | async-start | bytes 32768 | tf_op jit(solution)/shard_map/grad/all_to_all | solution.py:523
  41.1 0.0 collective-permute-done.6.one_hbm
  41.1 0.0 collective-permute-done.7.three_hbm
  41.1 10.9 %rest.1 = bf16[256,768]{1,0:T(8,128)(2,1)} custom-call(s32[2]{0:T(128)S(1)} %pad_add_fusion.place_ref, bf16[256,768]{1,0:T(8,128)(2,1)S(1)} %collective-permute-done.2.far_hbm, bf16[256,768]{1,0:T(8,128)(2,1)S(1)} %collective-permute-done.3.two_hbm, bf16[256,768]{1,0:T(8,128)(2,1)S(1)} %collective-permute-done.6.one_hbm, ...), custom_call_target="tpu_custom_call" | custom-call | flops 8000000000 | bytes 1024 | tf_op jit(solution)/shard_map/rest/pallas_call | solution.py:423
  52.0 0.0 all-to-all-done
  52.0 1.0 %clip.1 = f32[256,768]{1,0:T(8,128)} custom-call(f32[32,128]{1,0:T(8,128)S(1)} %bitcast.19, f32[256,768]{1,0:T(8,128)S(1)} %get-tuple-element.45.refs_1_), custom_call_target="tpu_custom_call" | custom-call | bytes 1024 | tf_op jit(solution)/shard_map/clip/pallas_call | solution.py:423
  (3 shorter events, 0.1 us)
Async XLA Ops:
  0.6 20.2 %collective-permute-start.2 = (bf16[256,768]{1,0:T(8,128)(2,1)}, bf16[256,768]{1,0:T(8,128)(2,1)S(1)}, u32[]{:S(2)}, u32[]{:S(2)}) collective-permute-start(bf16[256,768]{1,0:T(8,128)(2,1)} %bitcast.20), channel_id=1, source_target_pairs={{0,4},{1,5},{2,6},{3,7},{4,8},{5,9},{6,10},{7,11},{8,12},{9,13},{1... | collective-permute-start | bytes 1179656 | tf_op jit(solution)/shard_map/halo/ppermute | solution.py:436
  11.0 8.3 %collective-permute-start = (bf16[3,16,768]{2,1,0:T(8,128)(2,1)S(1)}, bf16[3,16,768]{2,1,0:T(8,128)(2,1)S(1)}, u32[]{:S(2)}, u32[]{:S(2)}) collective-permute-start(bf16[3,16,768]{2,1,0:T(8,128)(2,1)S(1)} %get-tuple-element.24.own_hbm), channel_id=1, source_target_pairs={{0,4},{1,5},{2,6},{3,7},{4,8},{5,9},{6,10},{7,11},{8,12},{9,13},{1... | collective-permute-start | bytes 221192 | tf_op jit(solution)/shard_map/halo/ppermute | solution.py:436
  14.5 6.2 %collective-permute-start.1 = (bf16[3,16,768]{2,1,0:T(8,128)(2,1)S(1)}, bf16[3,16,768]{2,1,0:T(8,128)(2,1)S(1)}, u32[]{:S(2)}, u32[]{:S(2)}) collective-permute-start(bf16[3,16,768]{2,1,0:T(8,128)(2,1)S(1)} %get-tuple-element.24.own_hbm), channel_id=1, source_target_pairs={{4,0},{5,1},{6,2},{7,3},{8,4},{9,5},{10,6},{11,7},{12,8},{13,9},{1... | collective-permute-start | bytes 221192 | tf_op jit(solution)/shard_map/halo/ppermute | solution.py:436
  15.8 6.6 %copy-start = (bf16[1,256,768]{2,1,0:T(8,128)(2,1)S(1)}, bf16[1,256,768]{2,1,0:T(8,128)(2,1)}, u32[]{:S(2)}) copy-start(bf16[1,256,768]{2,1,0:T(8,128)(2,1)} %param.9) | copy-start | bytes 1179652
  20.8 5.8 %collective-permute-start.4 = (bf16[2,3,16,768]{3,2,1,0:T(8,128)(2,1)S(1)}, bf16[2,3,16,768]{3,2,1,0:T(8,128)(2,1)S(1)}, u32[]{:S(2)}, u32[]{:S(2)}) collective-permute-start(bf16[2,3,16,768]{3,2,1,0:T(8,128)(2,1)S(1)} %pad_maximum_fusion.1), channel_id=1, source_target_pairs={{0,2},{1,3},{2,0},{3,1},{4,6},{5,7},{6,4},{7,5},{8,10},{9,11},{10,... | collective-permute-start | bytes 442376 | tf_op jit(solution)/shard_map/halo/ppermute | solution.py:440
  22.4 11.7 %collective-permute-start.3 = (bf16[256,768]{1,0:T(8,128)(2,1)S(1)}, bf16[256,768]{1,0:T(8,128)(2,1)S(1)}, u32[]{:S(2)}, u32[]{:S(2)}) collective-permute-start(bf16[256,768]{1,0:T(8,128)(2,1)S(1)} %bitcast.22), channel_id=1, source_target_pairs={{0,2},{1,3},{2,4},{3,5},{4,6},{5,7},{6,8},{7,9},{8,10},{9,11},{10,... | collective-permute-start | bytes 1179656 | tf_op jit(solution)/shard_map/halo/ppermute | solution.py:436
  26.7 1.6 %collective-permute-start.5 = (bf16[4,3,16,768]{3,2,1,0:T(8,128)(2,1)S(1)}, bf16[4,3,16,768]{3,2,1,0:T(8,128)(2,1)S(1)}, u32[]{:S(2)}, u32[]{:S(2)}) collective-permute-start(bf16[4,3,16,768]{3,2,1,0:T(8,128)(2,1)S(1)} %pad_maximum_fusion), channel_id=1, source_target_pairs={{0,1},{1,0},{2,3},{3,2},{4,5},{5,4},{6,7},{7,6},{8,9},{9,8},{10,11... | collective-permute-start | bytes 884744 | tf_op jit(solution)/shard_map/halo/ppermute | solution.py:440
  35.1 6.0 %collective-permute-start.6 = (bf16[256,768]{1,0:T(8,128)(2,1)}, bf16[256,768]{1,0:T(8,128)(2,1)S(1)}, u32[]{:S(2)}, u32[]{:S(2)}) collective-permute-start(bf16[256,768]{1,0:T(8,128)(2,1)} %get-tuple-element.47), channel_id=1, source_target_pairs={{0,1},{1,0},{2,3},{3,2},{4,5},{5,4},{6,7},{7,6},{8,9},{9,8},{10,11... | collective-permute-start | bytes 1179656 | tf_op jit(solution)/shard_map/grad/ppermute | solution.py:440
  35.2 5.9 %collective-permute-start.7 = (bf16[256,768]{1,0:T(8,128)(2,1)}, bf16[256,768]{1,0:T(8,128)(2,1)S(1)}, u32[]{:S(2)}, u32[]{:S(2)}) collective-permute-start(bf16[256,768]{1,0:T(8,128)(2,1)} %get-tuple-element.46), channel_id=1, source_target_pairs={{0,1},{1,0},{2,3},{3,2},{4,5},{5,4},{6,7},{7,6},{8,9},{9,8},{10,11... | collective-permute-start | bytes 1179656 | tf_op jit(solution)/shard_map/grad/ppermute | solution.py:440
  35.6 16.5 %all-to-all-start = ((f32[32,1,128]{2,1,0:T(1,128)}), f32[32,1,128]{2,1,0:T(1,128)S(1)}, u32[]{:S(2)}, u32[]{:S(2)}) async-start(f32[32,1,128]{2,1,0:T(1,128)} %bitcast.9), calls=%async_computation | async-start | bytes 32768 | tf_op jit(solution)/shard_map/grad/all_to_all | solution.py:523

commit v4 on v3

--- a/solution.py
+++ b/solution.py
@@ -75,9 +75,8 @@
 
 def local_kernel(
     clean_hbm, wk_hbm, wv_hbm, wq_hbm, cot_hbm, me_hbm, bits_hbm, lev_hbm, imp_hbm,
-    stats_ref, a_ref, qk_ref, km_ref, vm_ref, q_hbm, k_hbm, v_hbm,
-    clean_ref, wk_ref, wv_ref, wq_ref, cot_ref, me_ref, bits_ref, lev_ref, imp_ref,
-    q_ref, k_ref, v_ref, in_sems, out_sems,
+    stats_ref, a_ref, qk_ref, km_ref, vm_ref, flags_ref, q_ref, k_ref, v_ref,
+    clean_ref, wk_ref, wv_ref, wq_ref, cot_ref, me_ref, bits_ref, lev_ref, imp_ref, in_sems,
 ):
     sources = (clean_hbm, me_hbm, wk_hbm, wv_hbm, wq_hbm, bits_hbm, lev_hbm, imp_hbm, cot_hbm)
     targets = (clean_ref, me_ref, wk_ref, wv_ref, wq_ref, bits_ref, lev_ref, imp_ref, cot_ref)
@@ -112,12 +111,7 @@
     is_masked = masked > 0.5
     qm, vm = queries[tok : tok + 1], values[tok : tok + 1]
     q_ref[...] = jnp.where(is_masked, qm.astype(F32), queries[:tok].astype(F32)).astype(BF16)
-    outs = start_all(
-        [
-            pltpu.make_async_copy(src, dst, out_sems.at[i])
-            for i, (src, dst) in enumerate(((q_ref, q_hbm), (k_ref, k_hbm), (v_ref, v_hbm)))
-        ]
-    )
+    flags_ref[...] = jnp.broadcast_to(token_mask_row(bits, tok), flags_ref.shape)
     imp = imp_ref[...].astype(F32)
     weight = LEVELS / lev_ref[...].astype(F32) * (imp[0:1] / imp[1:2])
     row, lane = iota((tok, blocks), 0), iota((tok, blocks), 1)
@@ -173,14 +167,12 @@
     stats_ref[2, :, 0:LANES] = high
     stats_ref[2, :, LANES : 2 * LANES] = mid
     stats_ref[2, :, 2 * LANES : 3 * LANES] = low
-    for copy in outs:
-        copy.wait()
 
 
 def grad_kernel(
-    place_ref, back_hbm, ahead_hbm, y_hbm, c_hbm, own_hbm, a_hbm, v_hbm, qk_hbm, wv_hbm,
+    place_ref, back_hbm, ahead_hbm, y_hbm, c_hbm, own_hbm, wv_hbm, a_ref, v_ref, qk_ref,
     square_ref, raw_ref,
-    held, a_ref, v_ref, qk_ref, wv_ref, dvalues, in_sems,
+    held, wv_ref, dvalues, in_sems,
 ):
     tok, width = v_ref.shape
     blocks = tok // BLOCK
@@ -200,9 +192,6 @@
         (c_hbm.at[1], held.at[c_side + (at ^ 1)]),
         (c_hbm.at[2], held.at[GROUP + (at ^ 3)]),
         (c_hbm.at[3], held.at[y_side + (at ^ 3)]),
-        (a_hbm, a_ref),
-        (v_hbm, v_ref),
-        (qk_hbm, qk_ref),
         (wv_hbm, wv_ref),
     )
     copies = start_all(
@@ -252,8 +241,6 @@
     bias = jnp.where(seen, 0.0, -jnp.inf)
     lane_u = iota((tok, LANES), 1)
     sigma = jnp.zeros((tok, LANES), F32)
-    copies[9].wait()
-    copies[10].wait()
     scores = a_ref[...]
     for pair_at in range(HEADS // 2):
         pair = columns(pair_at, LANES)
@@ -271,8 +258,7 @@
     high = sigma.astype(BF16).astype(F32)
     low = (sigma - high).astype(BF16).astype(F32)
     split = (high + pltpu.roll(low, 16, 1) + pltpu.roll(high, 32, 1)).astype(BF16)
-    copies[11].wait()
-    copies[12].wait()
+    copies[9].wait()
     raw = dot_t(dvalues[...], wv_ref[...]) + dot(split, qk_ref[...])
     raw_ref[...] = raw
     total = jnp.sum(raw * raw, axis=0, keepdims=True)
@@ -280,24 +266,11 @@
     square_ref[...] = jnp.broadcast_to(total, square_ref.shape)
 
 
-def own_kernel(
-    q_hbm, k_hbm, v_hbm, km_hbm, vm_hbm, bits_hbm,
-    log_ref, mixed_ref,
-    bits_ref, q_ref, k_ref, v_ref, km_ref, vm_ref, in_sems,
-):
+def own_kernel(q_ref, k_ref, v_ref, km_ref, vm_ref, flags_ref, log_ref, mixed_ref):
     tok, width = q_ref.shape
     pairs = HEADS // 2
-    sources = (bits_hbm, q_hbm, k_hbm, v_hbm, km_hbm, vm_hbm)
-    targets = (bits_ref, q_ref, k_ref, v_ref, km_ref, vm_ref)
-    copies = start_all(
-        [
-            pltpu.make_async_copy(src, dst, in_sems.at[i])
-            for i, (src, dst) in enumerate(zip(sources, targets))
-        ]
-    )
-    copies[0].wait()
     row_b, col_b = iota((tok, tok), 0) // BLOCK, iota((tok, tok), 1) // BLOCK
-    masked = token_mask_row(bits_ref[...], tok)
+    masked = flags_ref[0:1]
     own_bias = jnp.where((col_b < row_b) | ((col_b == row_b) & (masked < 0.5)), 0.0, -jnp.inf)
     count = jnp.sum(jnp.where(row_b == col_b, masked, 0.0), axis=1, keepdims=True)
     mask_bias = jnp.where(iota((tok, LANES), 1).astype(F32) < count, 0.0, -jnp.inf)
@@ -305,8 +278,6 @@
     bias = jnp.concatenate([bias, bias], axis=0)
     lane = iota((tok, LANES), 1)
     logs = jnp.zeros((tok, LANES), F32)
-    for copy in copies[1:]:
-        copy.wait()
     for pair_at in range(pairs):
         pair = columns(pair_at, LANES)
         k_mask = jnp.broadcast_to(km_ref[0:1, pair], (LANES, LANES))
@@ -326,56 +297,42 @@
 
 
 def rest_kernel(
-    place_ref, far_hbm, two_hbm, one_hbm, three_hbm, q_hbm, mixed_hbm, log_hbm, after_hbm, wk_hbm, wv_hbm,
+    place_ref, after_hbm, mixed_hbm, wk_hbm, wv_hbm,
+    far_ref, two_ref, two_over_ref, over_ref, q_ref, log_ref,
     out_ref,
-    rows, wk_ref, wv_ref, q_ref, mixed_ref, log_ref, keys, vals, total_ref, in_sems,
+    wk_ref, wv_ref, mixed_ref, keys, vals, total_ref, in_sems,
 ):
     tok, width = q_ref.shape
-    shards = rows.shape[0]
+    rows = (far_ref, two_ref, two_over_ref, over_ref)
+    shards = len(rows)
     mine = place_ref[0]
     part = 2 * LANES
     parts = width // part
-
-    def load(src, dst, at):
-        return pltpu.make_async_copy(src, dst, in_sems.at[at])
-
     weights = []
     for at in range(parts):
         cols = columns(at, part)
         for i, (src, dst) in enumerate(((wk_hbm, wk_ref), (wv_hbm, wv_ref))):
-            weights.append(load(src.at[:, cols], dst.at[:, cols], shards + 2 * at + i))
-    others = [
-        load(src, dst, shards + 2 * parts + i)
-        for i, (src, dst) in enumerate(((q_hbm, q_ref), (mixed_hbm, mixed_ref), (log_hbm, log_ref)))
-    ]
-    shard_copies = [
-        load(src, rows.at[at], at)
-        for at, src in enumerate((far_hbm, two_hbm, one_hbm, three_hbm))
-    ]
-    start_all(shard_copies[:1])
-    start_all(weights[:2])
-    start_all(shard_copies[1:])
-    start_all(others)
-    start_all(weights[2:])
+            weights.append(
+                pltpu.make_async_copy(src.at[:, cols], dst.at[:, cols], in_sems.at[2 * at + i])
+            )
+    start_all(weights)
+    mixed_copy = pltpu.make_async_copy(mixed_hbm, mixed_ref, in_sems.at[2 * parts])
+    mixed_copy.start()
     row_b, col_b = iota((tok, tok), 0) // BLOCK, iota((tok, tok), 1) // BLOCK
     far_bias = jnp.where((col_b >= row_b) & (mine >= GROUP), 0.0, NEVER)
     far_bias = jnp.concatenate([far_bias, far_bias], axis=0)
-    biases = [far_bias] + [jnp.where(mine >= back, 0.0, NEVER) for back in (2, 1, 3)]
+    over = jnp.where(mine & 1 == 0, 1, 3)
+    biases = [far_bias] + [jnp.where(mine >= back, 0.0, NEVER) for back in (2, over, 4 - over)]
     lane = iota((tok, LANES), 1)
-    for at in range(parts):
+
+    def project(at):
         cols = columns(at, part)
-        for copy in weights[2 * at : 2 * at + 2]:
-            copy.wait()
         for place in range(shards):
-            if at == 0:
-                shard_copies[place].wait()
             span = columns(place, tok)
-            keys[span, cols] = dot(rows[place], wk_ref[:, cols]).astype(BF16)
-            vals[span, cols] = dot(rows[place], wv_ref[:, cols]).astype(BF16)
-    for copy in others:
-        copy.wait()
-    logs = jnp.zeros((tok, LANES), F32)
-    for pair_at in range(HEADS // 2):
+            keys[span, cols] = dot(rows[place][...], wk_ref[:, cols]).astype(BF16)
+            vals[span, cols] = dot(rows[place][...], wv_ref[:, cols]).astype(BF16)
+
+    def attend(pair_at, logs):
         pair = columns(pair_at, LANES)
         score = dot_t(both_heads(q_ref[:, pair]), keys[:, pair])
         pieces = [score[:, columns(place, tok)] + biases[place] for place in range(shards)]
@@ -385,10 +342,23 @@
         den = jnp.sum((pieces[0] + pieces[1]) + (pieces[2] + pieces[3]), axis=1, keepdims=True)
         expo = jnp.concatenate([piece.astype(BF16) for piece in pieces], axis=1)
         mixed = dot(expo, vals[:, pair]) / den
+        total_ref[:, pair] = jnp.where(lane < HEAD_DIM, mixed[:tok], mixed[tok:])
         log = peak + jnp.log(den)
         logs = jnp.where(lane == 2 * pair_at, log[:tok], logs)
-        logs = jnp.where(lane == 2 * pair_at + 1, log[tok:], logs)
-        total_ref[:, pair] = jnp.where(lane < HEAD_DIM, mixed[:tok], mixed[tok:])
+        return jnp.where(lane == 2 * pair_at + 1, log[tok:], logs)
+
+    logs = jnp.zeros((tok, LANES), F32)
+    for copy in weights[:2]:
+        copy.wait()
+    project(0)
+    for copy in weights[2:]:
+        copy.wait()
+    for at in range(parts):
+        if at + 1 < parts:
+            project(at + 1)
+        for pair_at in (2 * at, 2 * at + 1):
+            logs = attend(pair_at, logs)
+    mixed_copy.wait()
     share = 1.0 / (1.0 + jnp.exp(logs - log_ref[...]))
     high = share.astype(BF16)
     less = (share - high.astype(F32)).astype(BF16)
@@ -464,19 +434,19 @@
         far = shift(clean_rows, GROUP)
     with jax.named_scope("local"):
         ratio = importance[0].T
-        stats, a, qk, km, vm, q, k, v = call(
+        stats, a, qk, km, vm, flags, q, k, v = call(
             local_kernel,
             [
                 like(3, blocks, width), like(tok, LANES, dtype=F32), like(LANES, width),
-                like(BLOCK, width), like(BLOCK, width), like(*rows), like(*rows), like(*rows),
+                like(BLOCK, width), like(BLOCK, width), like(8, tok, dtype=F32),
+                like(*rows), like(*rows), like(*rows),
             ],
-            3,
+            0,
             [clean_rows, w_key, w_value, w_query, out_cot[0], mask_embed, mask_bits, levels, ratio],
             [
                 vmem(*rows), vmem(*square_w), vmem(*square_w), vmem(*square_w), vmem(*rows),
                 vmem(width), vmem(1, blocks, dtype=jnp.int32), vmem(1, blocks, dtype=jnp.int32),
-                vmem(2, blocks, dtype=jnp.int32), vmem(*rows), vmem(*rows), vmem(*rows),
-                sems(9), sems(3),
+                vmem(2, blocks, dtype=jnp.int32), sems(9),
             ],
             flops=1_000_000_000,
         )
@@ -487,19 +457,16 @@
             own_kernel,
             [like(tok, LANES, dtype=F32), like(*rows)],
             0,
-            [mask_bits],
-            [
-                vmem(1, blocks, dtype=jnp.int32), vmem(*rows), vmem(*rows), vmem(*rows),
-                vmem(BLOCK, width), vmem(BLOCK, width), sems(6),
-            ],
-            loose=[q, k, v, km, vm],
+            [],
+            [],
+            vmem=[q, k, v, km, vm, flags],
             flops=1_000_000_000,
         )
     with jax.named_scope("halo"):
         back, ahead, far, log = lax.optimization_barrier((back, ahead, far, log))
+        over = swap(jnp.where(place & 1 == 0, clean_rows, far), 1)
         y2 = swap(jnp.stack([stats, jnp.where(place & 2 == 0, ahead, back)]), 2)
-        clean_rows, far = lax.optimization_barrier((clean_rows, far))
-        two = shift(clean_rows, 2)
+        two = swap(jnp.where(place & 2 == 0, clean_rows, far), 2)
         sides = jnp.stack([stats, jnp.where(place & 1 == 0, ahead, back)])
         core4 = swap(jnp.concatenate([sides, y2]), 1)
     with jax.named_scope("grad"):
@@ -509,31 +476,29 @@
             0,
             [w_value],
             [
-                vmem(3 * GROUP, 3, blocks, width), vmem(tok, LANES, dtype=F32), vmem(*rows),
-                vmem(LANES, width), vmem(*square_w), vmem(*rows), sems(13),
+                vmem(3 * GROUP, 3, blocks, width), vmem(*square_w), vmem(*rows), sems(10),
             ],
             smem=[where],
-            loose=[back, ahead, y2, core4, stats, a, v, qk],
+            loose=[back, ahead, y2, core4, stats],
+            vmem=[a, v, qk],
             flops=100_000_000,
         )
         two, square = lax.optimization_barrier((two, square))
-        mine = place & 1 == 0
-        one = swap(jnp.where(mine, clean_rows, two), 1)
-        three = swap(jnp.where(mine, two, far), 1)
+        two_over = swap(two, 1)
         squares = lax.all_to_all(square, ("dp", "seq"), 0, 0)
     with jax.named_scope("rest"):
         (attn,) = call(
             rest_kernel,
             [like(*rows)],
             0,
-            [w_key, w_value],
+            [mixed, w_key, w_value],
             [
-                vmem(GROUP, *rows), vmem(*square_w), vmem(*square_w), vmem(*rows), vmem(*rows),
-                vmem(tok, LANES, dtype=F32), vmem(GROUP * tok, width), vmem(GROUP * tok, width),
-                vmem(*rows, dtype=F32), sems(GROUP + width // LANES + 3),
+                vmem(*square_w), vmem(*square_w), vmem(*rows), vmem(GROUP * tok, width),
+                vmem(GROUP * tok, width), vmem(*rows, dtype=F32), sems(width // LANES + 1),
             ],
             smem=[where],
-            loose=[far, two, one, three, q, mixed, log, square],
+            loose=[square],
+            vmem=[far, two, two_over, over, q, log],
             flops=8_000_000_000,
         )
     with jax.named_scope("clip"):

time: 53.5 us -> 50.3 us (0.940)
  starting transfers between devices: 19.8 us -> 16.7 us
  waiting for transfers between devices: 4.74 us -> 7.13 us
  Pallas kernels: 26.6 us -> 24.3 us
    ppermute x4 -> x3, starting transfers between devices: 12.2 us -> 9.71 us  [shift(): lax.ppermute(rows, 'seq', [(i, i + distance) for i in devices if i + dist...]
    pallas_call x5, Pallas kernels: 26.6 us -> 24.3 us  [call(): pl.pallas_call(kernel, out_shape=out_shape, in_specs=[pl.BlockSpec(memory...]
    ppermute x4 -> x5, waiting for transfers between devices: 3.26 us -> 4.86 us  [swap(): lax.ppermute(rows, 'seq', [(i, i ^ bit) for i in range(lax.axis_size('seq...]
    all_to_all x1, starting transfers between devices: 5.53 us -> 4.12 us  [on_device(): squares = lax.all_to_all(square, ('dp', 'seq'), 0, 0)]
    ppermute x4 -> x3, waiting for transfers between devices: 1.47 us -> 2.27 us  [shift(): lax.ppermute(rows, 'seq', [(i, i + distance) for i in devices if i + dist...]
    ppermute x4 -> x5, starting transfers between devices: 2.16 us -> 2.86 us  [swap(): lax.ppermute(rows, 'seq', [(i, i ^ bit) for i in range(lax.axis_size('seq...]
  transfers between devices with their start and end apart: 9 -> 9, of which waited for: 3 -> 3; matrix products, arithmetic and copies ran while one was open for 0% -> 2% of each run, Pallas kernels for 48% -> 47%
where the time goes in v4:
time: 50.3 us; the launch traced here: 50.1 us
  Pallas kernels  24.3 us (48%)
  starting transfers between devices  16.7 us (33%)
  waiting for transfers between devices  7.13 us (14%)
  between operations  0.96 us (2%)
  other arithmetic  0.94 us (2%)
    pallas_call x5, Pallas kernels, call(): pl.pallas_call(kernel, out_shape=out_shape, in_specs=[pl.BlockSpec(memory...  24.3 us
    ppermute x3, starting transfers between devices, shift(): lax.ppermute(rows, 'seq', [(i, i + distance) for i in devices if i + dist...  9.71 us
    ppermute x5, waiting for transfers between devices, swap(): lax.ppermute(rows, 'seq', [(i, i ^ bit) for i in range(lax.axis_size('seq...  4.86 us
    all_to_all x1, starting transfers between devices, on_device(): squares = lax.all_to_all(square, ('dp', 'seq'), 0, 0)  4.12 us
    ppermute x5, starting transfers between devices, swap(): lax.ppermute(rows, 'seq', [(i, i ^ bit) for i in range(lax.axis_size('seq...  2.86 us
    ppermute x3, waiting for transfers between devices, shift(): lax.ppermute(rows, 'seq', [(i, i + distance) for i in devices if i + dist...  2.27 us
  transfers between devices with their start and end apart: 9, of which 3 were waited for; matrix products, arithmetic and copies ran while one was open for 2% of the time, Pallas kernels for 47%

profile of v4, /device:TPU:0, one launch (start us, length us, event | category | flops | bytes accessed | tf_op | source)
XLA Modules:
  0.0 50.1 jit_solution(16103781250484526530)
XLA Ops:
  0.6 5.0 %collective-permute-start.2 = (bf16[256,768]{1,0:T(8,128)(2,1)}, bf16[256,768]{1,0:T(8,128)(2,1)S(1)}, u32[]{:S(2)}, u32[]{:S(2)}) collective-permute-start(bf16[256,768]{1,0:T(8,128)(2,1)} %bitcast.22), channel_id=1, source_target_pairs={{0,4},{1,5},{2,6},{3,7},{4,8},{5,9},{6,10},{7,11},{8,12},{9,13},{1... | collective-permute-start | bytes 1179656 | tf_op jit(solution)/shard_map/halo/ppermute | solution.py:406
  5.6 4.8 %local.1 = (bf16[3,16,768]{2,1,0:T(8,128)(2,1)S(1)}, f32[256,128]{1,0:T(8,128)S(1)}, bf16[128,768]{1,0:T(8,128)(2,1)S(1)}, bf16[16,768]{1,0:T(8,128)(2,1)S(1)}, ...) custom-call(bf16[256,768]{1,0:T(8,128)(2,1)} %bitcast.23, ...), custom_call_target="tpu_custom_call" | custom-call | flops 1000000000 | bytes 1024 | tf_op jit(solution)/shard_map/local/pallas_call | solution.py:393
  10.4 3.5 %collective-permute-start = (bf16[3,16,768]{2,1,0:T(8,128)(2,1)S(1)}, bf16[3,16,768]{2,1,0:T(8,128)(2,1)S(1)}, u32[]{:S(2)}, u32[]{:S(2)}) collective-permute-start(bf16[3,16,768]{2,1,0:T(8,128)(2,1)S(1)} %get-tuple-element.23.own_hbm), channel_id=1, source_target_pairs={{0,4},{1,5},{2,6},{3,7},{4,8},{5,9},{6,10},{7,11},{8,12},{9,13},{1... | collective-permute-start | bytes 221192 | tf_op jit(solution)/shard_map/halo/ppermute | solution.py:406
  13.8 1.3 %collective-permute-start.1 = (bf16[3,16,768]{2,1,0:T(8,128)(2,1)S(1)}, bf16[3,16,768]{2,1,0:T(8,128)(2,1)S(1)}, u32[]{:S(2)}, u32[]{:S(2)}) collective-permute-start(bf16[3,16,768]{2,1,0:T(8,128)(2,1)S(1)} %get-tuple-element.23.own_hbm), channel_id=1, source_target_pairs={{4,0},{5,1},{6,2},{7,3},{8,4},{9,5},{10,6},{11,7},{12,8},{13,9},{1... | collective-permute-start | bytes 221192 | tf_op jit(solution)/shard_map/halo/ppermute | solution.py:406
  15.2 0.0 copy-start.1
  15.2 2.6 %own.1 = (f32[256,128]{1,0:T(8,128)S(1)}, bf16[256,768]{1,0:T(8,128)(2,1)S(1)}) custom-call(bf16[256,768]{1,0:T(8,128)(2,1)S(1)} %get-tuple-element.24.q_ref, bf16[256,768]{1,0:T(8,128)(2,1)S(1)} %get-tuple-element.25.k_ref, bf16[256,768]{1,0:T(8,128)(2,1)S(1)} %get-tuple-element.26.v_ref, bf16[16,768]{1,0:T(8,128)(2,1)S(1)} %get-tuple-element.27.km_ref, ...), custom_call_target="tpu_custom_call" | custom-call | flops 1000000000 | bytes 1024 | tf_op jit(solution)/shard_map/own/pallas_call | solution.py:393
  17.8 0.0 copy-start
  17.8 0.0 collective-permute-done.back_hbm
  17.8 2.3 %collective-permute-done.1.ahead_hbm = bf16[3,16,768]{2,1,0:T(8,128)(2,1)S(1)} collective-permute-done((bf16[3,16,768]{2,1,0:T(8,128)(2,1)S(1)}, bf16[3,16,768]{2,1,0:T(8,128)(2,1)S(1)}, u32[]{:S(2)}, u32[]{:S(2)}) %collective-permute-start.1) | collective-permute-done | bytes 73760 | tf_op jit(solution)/shard_map/halo/ppermute | solution.py:406
  20.1 0.0 collective-permute-done.2.far_ref
  20.1 1.6 %collective-permute-start.4 = (bf16[2,3,16,768]{3,2,1,0:T(8,128)(2,1)S(1)}, bf16[2,3,16,768]{3,2,1,0:T(8,128)(2,1)S(1)}, u32[]{:S(2)}, u32[]{:S(2)}) collective-permute-start(bf16[2,3,16,768]{3,2,1,0:T(8,128)(2,1)S(1)} %pad_maximum_fusion.1), channel_id=1, source_target_pairs={{0,2},{1,3},{2,0},{3,1},{4,6},{5,7},{6,4},{7,5},{8,10},{9,11},{10,... | collective-permute-start | bytes 442376 | tf_op jit(solution)/shard_map/halo/ppermute | solution.py:410
  21.7 0.0 copy-done.1
  21.7 0.8 %broadcast_select_fusion = (bf16[256,768]{1,0:T(8,128)(2,1)}, bf16[256,768]{1,0:T(8,128)(2,1)S(1)}) fusion(bf16[256,768]{1,0:T(8,128)(2,1)S(1)} %collective-permute-done.2.far_ref, pred[]{:T(512)S(6)} %eq.9, bf16[1,256,768]{2,1,0:T(8,128)(2,1)S(1)} %copy-done.1, pred[]{:T(512)S(6)} %eq.8), kind=kLoop, calls=%fused_computation | loop fusion | flops 393216 | bytes 1572866 | tf_op jit(solution)/shard_map/halo/jit(_where)/select_n | solution.py:467
  22.5 0.5 %collective-permute-start.3 = (bf16[256,768]{1,0:T(8,128)(2,1)S(1)}, bf16[256,768]{1,0:T(8,128)(2,1)S(1)}, u32[]{:S(2)}, u32[]{:S(2)}) collective-permute-start(bf16[256,768]{1,0:T(8,128)(2,1)S(1)} %get-tuple-element.45), channel_id=1, source_target_pairs={{0,2},{1,3},{2,0},{3,1},{4,6},{5,7},{6,4},{7,5},{8,10},{9,11},{10,... | collective-permute-start | bytes 1179656 | tf_op jit(solution)/shard_map/halo/ppermute | solution.py:410
  23.0 3.9 %collective-permute-done.4.y_hbm = bf16[2,3,16,768]{3,2,1,0:T(8,128)(2,1)S(1)} collective-permute-done((bf16[2,3,16,768]{3,2,1,0:T(8,128)(2,1)S(1)}, bf16[2,3,16,768]{3,2,1,0:T(8,128)(2,1)S(1)}, u32[]{:S(2)}, u32[]{:S(2)}) %collective-permute-start.4) | collective-permute-done | bytes 147488 | tf_op jit(solution)/shard_map/halo/ppermute | solution.py:410
  26.9 0.0 copy-done
  26.9 0.1 collective-permute-start.5
  27.0 0.1 pad_add_fusion.place_ref
  27.1 0.5 collective-permute-start.7
  27.6 1.0 %collective-permute-done.5.c_hbm = bf16[4,3,16,768]{3,2,1,0:T(8,128)(2,1)S(1)} collective-permute-done((bf16[4,3,16,768]{3,2,1,0:T(8,128)(2,1)S(1)}, bf16[4,3,16,768]{3,2,1,0:T(8,128)(2,1)S(1)}, u32[]{:S(2)}, u32[]{:S(2)}) %collective-permute-start.5) | collective-permute-done | bytes 294944 | tf_op jit(solution)/shard_map/halo/ppermute | solution.py:410
  28.6 5.5 %grad.1 = (f32[32,128]{1,0:T(8,128)}, f32[256,768]{1,0:T(8,128)S(1)}) custom-call(s32[2]{0:T(128)S(1)} %pad_add_fusion.place_ref, bf16[3,16,768]{2,1,0:T(8,128)(2,1)S(1)} %collective-permute-done.back_hbm, bf16[3,16,768]{2,1,0:T(8,128)(2,1)S(1)} %collective-permute-done.1.ahead_hbm, bf16[2,3,16,768]{3,2,1,0:T(8,128)(2,1)S(1)} %collective-permute-done.4.y_hbm, ...), custom_call_target="tpu_custom_call" | custom-call | flops 100000000 | bytes 1024 | tf_op jit(solution)/shard_map/grad/pallas_call | solution.py:393
  34.0 0.0 collective-permute-done.3.two_ref
  34.1 0.2 collective-permute-start.6
  34.3 4.1 %all-to-all-start = ((f32[32,1,128]{2,1,0:T(1,128)}), f32[32,1,128]{2,1,0:T(1,128)S(1)}, u32[]{:S(2)}, u32[]{:S(2)}) async-start(f32[32,1,128]{2,1,0:T(1,128)} %bitcast.9), calls=%async_computation | async-start | bytes 32768 | tf_op jit(solution)/shard_map/grad/all_to_all | solution.py:488
  38.4 0.0 collective-permute-done.7.over_ref
  38.4 0.0 collective-permute-done.6.two_over_ref
  38.4 10.5 %rest.1 = bf16[256,768]{1,0:T(8,128)(2,1)} custom-call(s32[2]{0:T(128)S(1)} %pad_add_fusion.place_ref, f32[32,128]{1,0:T(8,128)} %get-tuple-element.37.after_hbm, bf16[256,768]{1,0:T(8,128)(2,1)} %copy-done, bf16[768,768]{1,0:T(8,128)(2,1)} %wk_hbm.3, bf16[768,768]{1,0:T(8,128)(2,1)} %wv_hbm.5, bf16[256,768]{1,0:T(8,128)(2,1)S(1)} %collective-permute-done.2.far_ref, ...), custom_call_target="tpu_custom_call" | custom-call | flops 8000000000 | bytes 1024 | tf_op jit(solution)/shard_map/rest/pallas_call | solution.py:393
  48.9 0.0 all-to-all-done
  48.9 1.0 %clip.1 = f32[256,768]{1,0:T(8,128)} custom-call(f32[32,128]{1,0:T(8,128)S(1)} %bitcast.21, f32[256,768]{1,0:T(8,128)S(1)} %get-tuple-element.43.refs_1_), custom_call_target="tpu_custom_call" | custom-call | bytes 1024 | tf_op jit(solution)/shard_map/clip/pallas_call | solution.py:393
  (3 shorter events, 0.1 us)
Async XLA Ops:
  0.6 19.5 %collective-permute-start.2 = (bf16[256,768]{1,0:T(8,128)(2,1)}, bf16[256,768]{1,0:T(8,128)(2,1)S(1)}, u32[]{:S(2)}, u32[]{:S(2)}) collective-permute-start(bf16[256,768]{1,0:T(8,128)(2,1)} %bitcast.22), channel_id=1, source_target_pairs={{0,4},{1,5},{2,6},{3,7},{4,8},{5,9},{6,10},{7,11},{8,12},{9,13},{1... | collective-permute-start | bytes 1179656 | tf_op jit(solution)/shard_map/halo/ppermute | solution.py:406
  10.4 7.5 %collective-permute-start = (bf16[3,16,768]{2,1,0:T(8,128)(2,1)S(1)}, bf16[3,16,768]{2,1,0:T(8,128)(2,1)S(1)}, u32[]{:S(2)}, u32[]{:S(2)}) collective-permute-start(bf16[3,16,768]{2,1,0:T(8,128)(2,1)S(1)} %get-tuple-element.23.own_hbm), channel_id=1, source_target_pairs={{0,4},{1,5},{2,6},{3,7},{4,8},{5,9},{6,10},{7,11},{8,12},{9,13},{1... | collective-permute-start | bytes 221192 | tf_op jit(solution)/shard_map/halo/ppermute | solution.py:406
  13.8 6.2 %collective-permute-start.1 = (bf16[3,16,768]{2,1,0:T(8,128)(2,1)S(1)}, bf16[3,16,768]{2,1,0:T(8,128)(2,1)S(1)}, u32[]{:S(2)}, u32[]{:S(2)}) collective-permute-start(bf16[3,16,768]{2,1,0:T(8,128)(2,1)S(1)} %get-tuple-element.23.own_hbm), channel_id=1, source_target_pairs={{4,0},{5,1},{6,2},{7,3},{8,4},{9,5},{10,6},{11,7},{12,8},{13,9},{1... | collective-permute-start | bytes 221192 | tf_op jit(solution)/shard_map/halo/ppermute | solution.py:406
  15.2 6.6 %copy-start.1 = (bf16[1,256,768]{2,1,0:T(8,128)(2,1)S(1)}, bf16[1,256,768]{2,1,0:T(8,128)(2,1)}, u32[]{:S(2)}) copy-start(bf16[1,256,768]{2,1,0:T(8,128)(2,1)} %param.9) | copy-start | bytes 1179652
  17.8 9.1 %copy-start = (bf16[256,768]{1,0:T(8,128)(2,1)}, bf16[256,768]{1,0:T(8,128)(2,1)S(1)}, u32[]{:S(2)}) copy-start(bf16[256,768]{1,0:T(8,128)(2,1)S(1)} %get-tuple-element.38.mixed_hbm) | copy-start | bytes 1179652
  20.1 6.8 %collective-permute-start.4 = (bf16[2,3,16,768]{3,2,1,0:T(8,128)(2,1)S(1)}, bf16[2,3,16,768]{3,2,1,0:T(8,128)(2,1)S(1)}, u32[]{:S(2)}, u32[]{:S(2)}) collective-permute-start(bf16[2,3,16,768]{3,2,1,0:T(8,128)(2,1)S(1)} %pad_maximum_fusion.1), channel_id=1, source_target_pairs={{0,2},{1,3},{2,0},{3,1},{4,6},{5,7},{6,4},{7,5},{8,10},{9,11},{10,... | collective-permute-start | bytes 442376 | tf_op jit(solution)/shard_map/halo/ppermute | solution.py:410
  22.5 11.5 %collective-permute-start.3 = (bf16[256,768]{1,0:T(8,128)(2,1)S(1)}, bf16[256,768]{1,0:T(8,128)(2,1)S(1)}, u32[]{:S(2)}, u32[]{:S(2)}) collective-permute-start(bf16[256,768]{1,0:T(8,128)(2,1)S(1)} %get-tuple-element.45), channel_id=1, source_target_pairs={{0,2},{1,3},{2,0},{3,1},{4,6},{5,7},{6,4},{7,5},{8,10},{9,11},{10,... | collective-permute-start | bytes 1179656 | tf_op jit(solution)/shard_map/halo/ppermute | solution.py:410
  26.9 1.6 %collective-permute-start.5 = (bf16[4,3,16,768]{3,2,1,0:T(8,128)(2,1)S(1)}, bf16[4,3,16,768]{3,2,1,0:T(8,128)(2,1)S(1)}, u32[]{:S(2)}, u32[]{:S(2)}) collective-permute-start(bf16[4,3,16,768]{3,2,1,0:T(8,128)(2,1)S(1)} %pad_maximum_fusion), channel_id=1, source_target_pairs={{0,1},{1,0},{2,3},{3,2},{4,5},{5,4},{6,7},{7,6},{8,9},{9,8},{10,11... | collective-permute-start | bytes 884744 | tf_op jit(solution)/shard_map/halo/ppermute | solution.py:410
  27.1 11.3 %collective-permute-start.7 = (bf16[256,768]{1,0:T(8,128)(2,1)}, bf16[256,768]{1,0:T(8,128)(2,1)S(1)}, u32[]{:S(2)}, u32[]{:S(2)}) collective-permute-start(bf16[256,768]{1,0:T(8,128)(2,1)} %get-tuple-element.44), channel_id=1, source_target_pairs={{0,1},{1,0},{2,3},{3,2},{4,5},{5,4},{6,7},{7,6},{8,9},{9,8},{10,11... | collective-permute-start | bytes 1179656 | tf_op jit(solution)/shard_map/halo/ppermute | solution.py:410
  34.1 4.3 %collective-permute-start.6 = (bf16[256,768]{1,0:T(8,128)(2,1)S(1)}, bf16[256,768]{1,0:T(8,128)(2,1)S(1)}, u32[]{:S(2)}, u32[]{:S(2)}) collective-permute-start(bf16[256,768]{1,0:T(8,128)(2,1)S(1)} %collective-permute-done.3.two_ref), channel_id=1, source_target_pairs={{0,1},{1,0},{2,3},{3,2},{4,5},{5,4},{6,7},{7,6},{8,9},{9,8},{10,11... | collective-permute-start | bytes 1179656 | tf_op jit(solution)/shard_map/grad/ppermute | solution.py:410
  34.3 14.6 %all-to-all-start = ((f32[32,1,128]{2,1,0:T(1,128)}), f32[32,1,128]{2,1,0:T(1,128)S(1)}, u32[]{:S(2)}, u32[]{:S(2)}) async-start(f32[32,1,128]{2,1,0:T(1,128)} %bitcast.9), calls=%async_computation | async-start | bytes 32768 | tf_op jit(solution)/shard_map/grad/all_to_all | solution.py:488

commit v5 on v4

--- a/solution.py
+++ b/solution.py
@@ -16,6 +16,7 @@
 CLIP = 0.25
 LANES = 128
 NEVER = -1e30
+SCALARS = 48
 GROUP = 4
 F32 = jnp.float32
 BF16 = jnp.bfloat16
@@ -71,6 +72,10 @@
     low = iota(pair.shape, 1) < HEAD_DIM
     wide = pair.astype(F32)
     return jnp.concatenate([jnp.where(low, wide, 0.0), jnp.where(low, 0.0, wide)], axis=0).astype(BF16)
+
+
+def head_spread(width):
+    return iota((LANES, width), 1) // HEAD_DIM == iota((LANES, width), 0)
 
 
 def local_kernel(
@@ -88,7 +93,7 @@
     )
     tok, width = clean_ref.shape
     blocks = tok // BLOCK
-    head_of = iota((LANES, width), 1) // HEAD_DIM == iota((LANES, width), 0)
+    head_of = head_spread(width)
     spread = jnp.where(head_of, 1.0, 0.0).astype(BF16)
     copies[0].wait()
     copies[1].wait()
@@ -157,22 +162,20 @@
     packed = jnp.where(in_heads, top, 0.0)
     for place, part in enumerate((top_n, grad_mix)):
         packed = packed + pltpu.roll(jnp.where(in_heads, part, 0.0), 16 * (place + 1), 1)
-    high = packed.astype(BF16)
-    rest = packed - high.astype(F32)
-    mid = rest.astype(BF16)
-    low = (rest - mid.astype(F32)).astype(BF16)
-    stats_ref[0] = grad_sum.astype(BF16)
-    stats_ref[1] = mixed.astype(BF16)
-    stats_ref[2] = jnp.zeros((blocks, width), BF16)
-    stats_ref[2, :, 0:LANES] = high
-    stats_ref[2, :, LANES : 2 * LANES] = mid
-    stats_ref[2, :, 2 * LANES : 3 * LANES] = low
+    high = packed.astype(BF16).astype(F32)
+    rest = packed - high
+    mid = rest.astype(BF16).astype(F32)
+    low = rest - mid
+    stats_ref[:, 0:width] = grad_sum.astype(BF16)
+    stats_ref[:, width : 2 * width] = mixed.astype(BF16)
+    stats_ref[:, 2 * width : 2 * width + LANES] = (high + pltpu.roll(mid, SCALARS, 1)).astype(BF16)
+    stats_ref[:, 2 * width + LANES :] = low.astype(BF16)
 
 
 def grad_kernel(
     place_ref, back_hbm, ahead_hbm, y_hbm, c_hbm, own_hbm, wv_hbm, a_ref, v_ref, qk_ref,
-    square_ref, raw_ref,
-    held, wv_ref, dvalues, in_sems,
+    square_ref, raw_ref, wv_ref,
+    held, dvalues, in_sems,
 ):
     tok, width = v_ref.shape
     blocks = tok // BLOCK
@@ -208,13 +211,11 @@
     bias = jnp.where(seen, 0.0, -jnp.inf)
     for copy in copies[:9]:
         copy.wait()
-    grads = held[GROUP:, 0].reshape(count_b, width)
-    mixed = held[:, 1].reshape(count_u, width)
-    scalars = (
-        held[:, 2, :, 0:LANES].astype(F32)
-        + held[:, 2, :, LANES : 2 * LANES].astype(F32)
-        + held[:, 2, :, 2 * LANES : 3 * LANES].astype(F32)
-    ).reshape(count_u, LANES)
+    grads = held[GROUP:, :, 0:width].reshape(count_b, width)
+    mixed = held[:, :, width : 2 * width].reshape(count_u, width)
+    scalars = held[:, :, 2 * width : 2 * width + LANES].astype(F32).reshape(count_u, LANES)
+    scalars = scalars + pltpu.roll(scalars, LANES - SCALARS, 1)
+    scalars = scalars + held[:, :, 2 * width + LANES :].astype(F32).reshape(count_u, LANES)
     padded = jnp.concatenate(
         [scalars[near:], jnp.zeros((pad_u - count_b, LANES), F32)], axis=0
     )
@@ -266,9 +267,19 @@
     square_ref[...] = jnp.broadcast_to(total, square_ref.shape)
 
 
-def own_kernel(q_ref, k_ref, v_ref, km_ref, vm_ref, flags_ref, log_ref, mixed_ref):
+def own_kernel(
+    wk_hbm, wv_hbm, q_ref, k_ref, v_ref, km_ref, vm_ref, flags_ref,
+    log_ref, mixed_ref, wk_ref, wv_ref,
+    sems,
+):
     tok, width = q_ref.shape
     pairs = HEADS // 2
+    copies = start_all(
+        [
+            pltpu.make_async_copy(src, dst, sems.at[i])
+            for i, (src, dst) in enumerate(((wk_hbm, wk_ref), (wv_hbm, wv_ref)))
+        ]
+    )
     row_b, col_b = iota((tok, tok), 0) // BLOCK, iota((tok, tok), 1) // BLOCK
     masked = flags_ref[0:1]
     own_bias = jnp.where((col_b < row_b) | ((col_b == row_b) & (masked < 0.5)), 0.0, -jnp.inf)
@@ -294,79 +305,103 @@
         logs = jnp.where(lane == 2 * pair_at + 1, log[tok:], logs)
         mixed_ref[:, pair] = jnp.where(lane < HEAD_DIM, mixed[:tok], mixed[tok:]).astype(BF16)
     log_ref[...] = logs
-
-
-def rest_kernel(
-    place_ref, after_hbm, mixed_hbm, wk_hbm, wv_hbm,
-    far_ref, two_ref, two_over_ref, over_ref, q_ref, log_ref,
-    out_ref,
-    wk_ref, wv_ref, mixed_ref, keys, vals, total_ref, in_sems,
+    for copy in copies:
+        copy.wait()
+
+
+def attend_pair(q_pair, keys, vals, biases):
+    tok = q_pair.shape[0]
+    score = dot_t(both_heads(q_pair), keys)
+    pieces = [score[:, columns(place, tok)] + bias for place, bias in enumerate(biases)]
+    peak = pieces[0]
+    for piece in pieces[1:]:
+        peak = jnp.maximum(peak, piece)
+    peak = jnp.max(peak, axis=1, keepdims=True)
+    pieces = [jnp.exp(piece - peak) for piece in pieces]
+    den = pieces[0]
+    for piece in pieces[1:]:
+        den = den + piece
+    den = jnp.sum(den, axis=1, keepdims=True)
+    mixed = dot(jnp.concatenate([piece.astype(BF16) for piece in pieces], axis=1), vals) / den
+    low = iota((tok, LANES), 1) < HEAD_DIM
+    return jnp.where(low, mixed[:tok], mixed[tok:]), peak + jnp.log(den)
+
+
+def keep_logs(logs, pair_at, log):
+    tok = logs.shape[0]
+    lane = iota(logs.shape, 1)
+    logs = jnp.where(lane == 2 * pair_at, log[:tok], logs)
+    return jnp.where(lane == 2 * pair_at + 1, log[tok:], logs)
+
+
+def blend(logs, total, old_logs, old_mixed):
+    share = 1.0 / (1.0 + jnp.exp(logs - old_logs))
+    high = share.astype(BF16)
+    low = (share - high.astype(F32)).astype(BF16)
+    spread = jnp.where(head_spread(total.shape[1]), 1.0, 0.0).astype(BF16)
+    share = dot(high, spread) + dot(low, spread)
+    return (total + share * (old_mixed.astype(F32) - total)).astype(BF16)
+
+
+def far_kernel(
+    place_ref, far_ref, q_ref, wk_ref, wv_ref, old_log_ref, old_mixed_ref,
+    log_ref, mixed_ref,
+    total_ref,
 ):
     tok, width = q_ref.shape
-    rows = (far_ref, two_ref, two_over_ref, over_ref)
+    row_b, col_b = iota((tok, tok), 0) // BLOCK, iota((tok, tok), 1) // BLOCK
+    bias = jnp.where((col_b >= row_b) & (place_ref[0] >= GROUP), 0.0, NEVER)
+    bias = jnp.concatenate([bias, bias], axis=0)
+    keys = dot(far_ref[...], wk_ref[...]).astype(BF16)
+    vals = dot(far_ref[...], wv_ref[...]).astype(BF16)
+    logs = jnp.zeros((tok, LANES), F32)
+    for pair_at in range(HEADS // 2):
+        pair = columns(pair_at, LANES)
+        mixed, log = attend_pair(q_ref[:, pair], keys[:, pair], vals[:, pair], [bias])
+        total_ref[:, pair] = mixed
+        logs = keep_logs(logs, pair_at, log)
+    old = old_log_ref[...]
+    mixed_ref[...] = blend(logs, total_ref[...], old, old_mixed_ref[...])
+    top = jnp.maximum(logs, old)
+    log_ref[...] = top + jnp.log(jnp.exp(logs - top) + jnp.exp(old - top))
+
+
+def rest_kernel(
+    place_ref, after_hbm, wk_hbm, mixed_hbm,
+    two_ref, two_over_ref, over_ref, q_ref, log_ref, wv_ref,
+    out_ref,
+    wk_ref, mixed_ref, keys, vals, total_ref, in_sems,
+):
+    tok, width = q_ref.shape
+    rows = (two_ref, two_over_ref, over_ref)
     shards = len(rows)
     mine = place_ref[0]
     part = 2 * LANES
     parts = width // part
-    weights = []
-    for at in range(parts):
-        cols = columns(at, part)
-        for i, (src, dst) in enumerate(((wk_hbm, wk_ref), (wv_hbm, wv_ref))):
-            weights.append(
-                pltpu.make_async_copy(src.at[:, cols], dst.at[:, cols], in_sems.at[2 * at + i])
-            )
-    start_all(weights)
-    mixed_copy = pltpu.make_async_copy(mixed_hbm, mixed_ref, in_sems.at[2 * parts])
+    key_copy = pltpu.make_async_copy(wk_hbm, wk_ref, in_sems.at[0])
+    key_copy.start()
+    mixed_copy = pltpu.make_async_copy(mixed_hbm, mixed_ref, in_sems.at[1])
     mixed_copy.start()
-    row_b, col_b = iota((tok, tok), 0) // BLOCK, iota((tok, tok), 1) // BLOCK
-    far_bias = jnp.where((col_b >= row_b) & (mine >= GROUP), 0.0, NEVER)
-    far_bias = jnp.concatenate([far_bias, far_bias], axis=0)
     over = jnp.where(mine & 1 == 0, 1, 3)
-    biases = [far_bias] + [jnp.where(mine >= back, 0.0, NEVER) for back in (2, over, 4 - over)]
-    lane = iota((tok, LANES), 1)
-
-    def project(at):
-        cols = columns(at, part)
-        for place in range(shards):
-            span = columns(place, tok)
-            keys[span, cols] = dot(rows[place][...], wk_ref[:, cols]).astype(BF16)
-            vals[span, cols] = dot(rows[place][...], wv_ref[:, cols]).astype(BF16)
-
-    def attend(pair_at, logs):
+    biases = [jnp.where(mine >= back, 0.0, NEVER) for back in (2, over, 4 - over)]
+
+    def project(weight, kept):
+        for at in range(parts):
+            cols = columns(at, part)
+            for place in range(shards):
+                kept[columns(place, tok), cols] = dot(rows[place][...], weight[:, cols]).astype(BF16)
+
+    project(wv_ref, vals)
+    key_copy.wait()
+    project(wk_ref, keys)
+    logs = jnp.zeros((tok, LANES), F32)
+    for pair_at in range(HEADS // 2):
         pair = columns(pair_at, LANES)
-        score = dot_t(both_heads(q_ref[:, pair]), keys[:, pair])
-        pieces = [score[:, columns(place, tok)] + biases[place] for place in range(shards)]
-        peak = jnp.maximum(jnp.maximum(pieces[0], pieces[1]), jnp.maximum(pieces[2], pieces[3]))
-        peak = jnp.max(peak, axis=1, keepdims=True)
-        pieces = [jnp.exp(piece - peak) for piece in pieces]
-        den = jnp.sum((pieces[0] + pieces[1]) + (pieces[2] + pieces[3]), axis=1, keepdims=True)
-        expo = jnp.concatenate([piece.astype(BF16) for piece in pieces], axis=1)
-        mixed = dot(expo, vals[:, pair]) / den
-        total_ref[:, pair] = jnp.where(lane < HEAD_DIM, mixed[:tok], mixed[tok:])
-        log = peak + jnp.log(den)
-        logs = jnp.where(lane == 2 * pair_at, log[:tok], logs)
-        return jnp.where(lane == 2 * pair_at + 1, log[tok:], logs)
-
-    logs = jnp.zeros((tok, LANES), F32)
-    for copy in weights[:2]:
-        copy.wait()
-    project(0)
-    for copy in weights[2:]:
-        copy.wait()
-    for at in range(parts):
-        if at + 1 < parts:
-            project(at + 1)
-        for pair_at in (2 * at, 2 * at + 1):
-            logs = attend(pair_at, logs)
+        mixed, log = attend_pair(q_ref[:, pair], keys[:, pair], vals[:, pair], biases)
+        total_ref[:, pair] = mixed
+        logs = keep_logs(logs, pair_at, log)
     mixed_copy.wait()
-    share = 1.0 / (1.0 + jnp.exp(logs - log_ref[...]))
-    high = share.astype(BF16)
-    less = (share - high.astype(F32)).astype(BF16)
-    head_of = iota((LANES, width), 1) // HEAD_DIM == iota((LANES, width), 0)
-    spread = jnp.where(head_of, 1.0, 0.0).astype(BF16)
-    share = dot(high, spread) + dot(less, spread)
-    total = total_ref[...]
-    out_ref[...] = (total + share * (mixed_ref[...].astype(F32) - total)).astype(BF16)
+    out_ref[...] = blend(logs, total_ref[...], log_ref[...], mixed_ref[...])
 
 
 def scale_kernel(entries, square_ref, raw_ref, out_hbm, out_ref, sems):
@@ -420,6 +455,7 @@
     where = jnp.stack([place, jnp.int32(count * blocks)]).astype(jnp.int32)
     rows = (tok, width)
     square_w = (width, width)
+    packed = 2 * width + 2 * LANES
 
     def like(*dims, dtype=BF16):
         return jax.ShapeDtypeStruct(dims, dtype)
@@ -437,7 +473,7 @@
         stats, a, qk, km, vm, flags, q, k, v = call(
             local_kernel,
             [
-                like(3, blocks, width), like(tok, LANES, dtype=F32), like(LANES, width),
+                like(blocks, packed), like(tok, LANES, dtype=F32), like(LANES, width),
                 like(BLOCK, width), like(BLOCK, width), like(8, tok, dtype=F32),
                 like(*rows), like(*rows), like(*rows),
             ],
@@ -452,32 +488,45 @@
         )
     with jax.named_scope("halo"):
         back, ahead = shift(stats, GROUP), shift(stats, -GROUP)
+        other = jnp.where(place & 2 == 0, clean_rows, far)
+        q, other = lax.optimization_barrier((q, other))
+        two = swap(other, 2)
     with jax.named_scope("own"):
-        log, mixed = call(
+        log, mixed, wk, wv = call(
             own_kernel,
-            [like(tok, LANES, dtype=F32), like(*rows)],
+            [like(tok, LANES, dtype=F32), like(*rows), like(*square_w), like(*square_w)],
             0,
-            [],
-            [],
+            [w_key, w_value],
+            [sems(2)],
             vmem=[q, k, v, km, vm, flags],
             flops=1_000_000_000,
         )
     with jax.named_scope("halo"):
-        back, ahead, far, log = lax.optimization_barrier((back, ahead, far, log))
+        back, ahead, log = lax.optimization_barrier((back, ahead, log))
         over = swap(jnp.where(place & 1 == 0, clean_rows, far), 1)
         y2 = swap(jnp.stack([stats, jnp.where(place & 2 == 0, ahead, back)]), 2)
-        two = swap(jnp.where(place & 2 == 0, clean_rows, far), 2)
+    with jax.named_scope("far"):
+        log, mixed = call(
+            far_kernel,
+            [like(tok, LANES, dtype=F32), like(*rows)],
+            0,
+            [],
+            [vmem(*rows, dtype=F32)],
+            smem=[where],
+            vmem=[far, q, wk, wv, log, mixed],
+            flops=100_000_000,
+        )
+    with jax.named_scope("halo"):
+        y2, log = lax.optimization_barrier((y2, log))
         sides = jnp.stack([stats, jnp.where(place & 1 == 0, ahead, back)])
         core4 = swap(jnp.concatenate([sides, y2]), 1)
     with jax.named_scope("grad"):
-        square, raw = call(
+        square, raw, wv = call(
             grad_kernel,
-            [like(parts, LANES, dtype=F32), like(*rows, dtype=F32)],
+            [like(parts, LANES, dtype=F32), like(*rows, dtype=F32), like(*square_w)],
             0,
             [w_value],
-            [
-                vmem(3 * GROUP, 3, blocks, width), vmem(*square_w), vmem(*rows), sems(10),
-            ],
+            [vmem(3 * GROUP, blocks, packed), vmem(*rows), sems(10)],
             smem=[where],
             loose=[back, ahead, y2, core4, stats],
             vmem=[a, v, qk],
@@ -491,14 +540,14 @@
             rest_kernel,
             [like(*rows)],
             0,
-            [mixed, w_key, w_value],
+            [w_key, mixed],
             [
-                vmem(*square_w), vmem(*square_w), vmem(*rows), vmem(GROUP * tok, width),
-                vmem(GROUP * tok, width), vmem(*rows, dtype=F32), sems(width // LANES + 1),
+                vmem(*square_w), vmem(*rows), vmem(3 * tok, width), vmem(3 * tok, width),
+                vmem(*rows, dtype=F32), sems(2),
             ],
             smem=[where],
             loose=[square],
-            vmem=[far, two, two_over, over, q, log],
+            vmem=[two, two_over, over, q, log, wv],
             flops=8_000_000_000,
         )
     with jax.named_scope("clip"):

time: 50.3 us -> 47.9 us (0.952)
  waiting for transfers between devices: 7.13 us -> 1.97 us
  starting transfers between devices: 16.7 us -> 18.8 us
  Pallas kernels: 24.3 us -> 24.9 us
    ppermute x5, waiting for transfers between devices: 4.86 us -> 1.96 us  [swap(): lax.ppermute(rows, 'seq', [(i, i ^ bit) for i in range(lax.axis_size('seq...]
    ppermute x3, waiting for transfers between devices: 2.27 us -> 0.01 us  [shift(): lax.ppermute(rows, 'seq', [(i, i + distance) for i in devices if i + dist...]
    ppermute x3, starting transfers between devices: 9.71 us -> 10.8 us  [shift(): lax.ppermute(rows, 'seq', [(i, i + distance) for i in devices if i + dist...]
    all_to_all x1, starting transfers between devices: 4.12 us -> 5.19 us  [on_device(): squares = lax.all_to_all(square, ('dp', 'seq'), 0, 0)]
    pallas_call x5 -> x6, Pallas kernels: 24.3 us -> 24.9 us  [call(): pl.pallas_call(kernel, out_shape=out_shape, in_specs=[pl.BlockSpec(memory...]
  transfers between devices with their start and end apart: 9 -> 9, of which waited for: 3 -> 2; matrix products, arithmetic and copies ran while one was open for 2% -> 2% of each run, Pallas kernels for 47% -> 50%
where the time goes in v5:
time: 47.9 us; the launch traced here: 47.7 us
  Pallas kernels  24.9 us (52%)
  starting transfers between devices  18.8 us (39%)
  waiting for transfers between devices  1.97 us (4%)
  between operations  0.98 us (2%)
  other arithmetic  0.94 us (2%)
    pallas_call x6, Pallas kernels, call(): pl.pallas_call(kernel, out_shape=out_shape, in_specs=[pl.BlockSpec(memory...  24.9 us
    ppermute x3, starting transfers between devices, shift(): lax.ppermute(rows, 'seq', [(i, i + distance) for i in devices if i + dist...  10.8 us
    all_to_all x1, starting transfers between devices, on_device(): squares = lax.all_to_all(square, ('dp', 'seq'), 0, 0)  5.19 us
    ppermute x5, starting transfers between devices, swap(): lax.ppermute(rows, 'seq', [(i, i ^ bit) for i in range(lax.axis_size('seq...  2.86 us
    ppermute x5, waiting for transfers between devices, swap(): lax.ppermute(rows, 'seq', [(i, i ^ bit) for i in range(lax.axis_size('seq...  1.96 us
  transfers between devices with their start and end apart: 9, of which 2 were waited for; matrix products, arithmetic and copies ran while one was open for 2% of the time, Pallas kernels for 50%

profile of v5, /device:TPU:0, one launch (start us, length us, event | category | flops | bytes accessed | tf_op | source)
XLA Modules:
  0.0 47.7 jit_solution(7967905018027916860)
XLA Ops:
  0.6 5.0 %collective-permute-start = (bf16[256,768]{1,0:T(8,128)(2,1)}, bf16[256,768]{1,0:T(8,128)(2,1)S(1)}, u32[]{:S(2)}, u32[]{:S(2)}) collective-permute-start(bf16[256,768]{1,0:T(8,128)(2,1)} %bitcast.22), channel_id=1, source_target_pairs={{0,4},{1,5},{2,6},{3,7},{4,8},{5,9},{6,10},{7,11},{8,12},{9,13},{1... | collective-permute-start | bytes 1179656 | tf_op jit(solution)/shard_map/halo/ppermute | solution.py:441
  5.6 0.0 copy-start.1
  5.6 4.9 %local.1 = (bf16[16,1792]{1,0:T(8,128)(2,1)S(1)}, f32[256,128]{1,0:T(8,128)S(1)}, bf16[128,768]{1,0:T(8,128)(2,1)S(1)}, bf16[16,768]{1,0:T(8,128)(2,1)S(1)}, bf1...) custom-call(bf16[256,768]{1,0:T(8,128)(2,1)} %bitcast.23, ...), custom_call_target="tpu_custom_call" | custom-call | flops 1000000000 | bytes 1024 | tf_op jit(solution)/shard_map/local/pallas_call | solution.py:428
  10.5 1.3 %collective-permute-start.3 = (bf16[16,1792]{1,0:T(8,128)(2,1)S(1)}, bf16[16,1792]{1,0:T(8,128)(2,1)S(1)}, u32[]{:S(2)}, u32[]{:S(2)}) collective-permute-start(bf16[16,1792]{1,0:T(8,128)(2,1)S(1)} %get-tuple-element.33.own_hbm), channel_id=1, source_target_pairs={{4,0},{5,1},{6,2},{7,3},{8,4},{9,5},{10,6},{11,7},{12,8},{13,9},{1... | collective-permute-start | bytes 172040 | tf_op jit(solution)/shard_map/halo/ppermute | solution.py:441
  11.8 4.5 %collective-permute-start.2 = (bf16[16,1792]{1,0:T(8,128)(2,1)S(1)}, bf16[16,1792]{1,0:T(8,128)(2,1)S(1)}, u32[]{:S(2)}, u32[]{:S(2)}) collective-permute-start(bf16[16,1792]{1,0:T(8,128)(2,1)S(1)} %get-tuple-element.33.own_hbm), channel_id=1, source_target_pairs={{0,4},{1,5},{2,6},{3,7},{4,8},{5,9},{6,10},{7,11},{8,12},{9,13},{1... | collective-permute-start | bytes 172040 | tf_op jit(solution)/shard_map/halo/ppermute | solution.py:441
  16.3 0.0 collective-permute-done.far_ref
  16.4 0.0 copy-done.1
  16.4 0.8 %broadcast_select_fusion = (bf16[256,768]{1,0:T(8,128)(2,1)}, bf16[256,768]{1,0:T(8,128)(2,1)S(1)}) fusion(bf16[256,768]{1,0:T(8,128)(2,1)S(1)} %collective-permute-done.far_ref, pred[]{:T(512)S(6)} %eq.9, bf16[1,256,768]{2,1,0:T(8,128)(2,1)S(1)} %copy-done.1, pred[]{:T(512)S(6)} %eq.8), kind=kLoop, calls=%fused_computation | loop fusion | flops 393216 | bytes 1572866 | tf_op jit(solution)/shard_map/halo/jit(_where)/select_n | solution.py:506
  17.2 2.7 %own.1 = (f32[256,128]{1,0:T(8,128)S(1)}, bf16[256,768]{1,0:T(8,128)(2,1)S(1)}, bf16[768,768]{1,0:T(8,128)(2,1)S(1)}, bf16[768,768]{1,0:T(8,128)(2,1)S(1)}) custom-call(bf16[768,768]{1,0:T(8,128)(2,1)} %wk_hbm.5, bf16[768,768]{1,0:T(8,128)(2,1)} %wv_hbm.5, bf16[256,768]{1,0:T(8,128)(2,1)S(1)} %get-tuple-element.34.q_ref, ...), custom_call_target="tpu_custom_call" | custom-call | flops 1000000000 | bytes 1024 | tf_op jit(solution)/shard_map/own/pallas_call | solution.py:428
  19.8 0.0 collective-permute-done.3.ahead_hbm
  19.8 0.0 collective-permute-done.2.back_hbm
  19.9 1.6 %collective-permute-start.4 = (bf16[2,16,1792]{2,1,0:T(8,128)(2,1)S(1)}, bf16[2,16,1792]{2,1,0:T(8,128)(2,1)S(1)}, u32[]{:S(2)}, u32[]{:S(2)}) collective-permute-start(bf16[2,16,1792]{2,1,0:T(8,128)(2,1)S(1)} %pad_maximum_fusion.1), channel_id=1, source_target_pairs={{0,2},{1,3},{2,0},{3,1},{4,6},{5,7},{6,4},{7,5},{8,10},{9,11},{10,... | collective-permute-start | bytes 344072 | tf_op jit(solution)/shard_map/halo/ppermute | solution.py:445
  21.5 0.1 pad_add_fusion.place_ref
  21.6 0.5 %collective-permute-start.1 = (bf16[256,768]{1,0:T(8,128)(2,1)S(1)}, bf16[256,768]{1,0:T(8,128)(2,1)}, u32[]{:S(2)}, u32[]{:S(2)}) collective-permute-start(bf16[256,768]{1,0:T(8,128)(2,1)S(1)} %get-tuple-element.32), channel_id=1, source_target_pairs={{0,2},{1,3},{2,0},{3,1},{4,6},{5,7},{6,4},{7,5},{8,10},{9,11},{10,... | collective-permute-start | bytes 1179656 | tf_op jit(solution)/shard_map/halo/ppermute | solution.py:445
  22.1 2.9 %far.1 = (f32[256,128]{1,0:T(8,128)S(1)}, bf16[256,768]{1,0:T(8,128)(2,1)S(1)}) custom-call(s32[2]{0:T(128)S(1)} %pad_add_fusion.place_ref, bf16[256,768]{1,0:T(8,128)(2,1)S(1)} %collective-permute-done.far_ref, bf16[256,768]{1,0:T(8,128)(2,1)S(1)} %get-tuple-element.34.q_ref, bf16[768,768]{1,0:T(8,128)(2,1)S(1)} %get-tuple-element.43.wk_ref, ...), custom_call_target="tpu_custom_call" | custom-call | flops 100000000 | bytes 1024 | tf_op jit(solution)/shard_map/far/pallas_call | solution.py:428
  25.0 0.0 copy-start
  25.0 1.0 %collective-permute-done.4.y_hbm = bf16[2,16,1792]{2,1,0:T(8,128)(2,1)S(1)} collective-permute-done((bf16[2,16,1792]{2,1,0:T(8,128)(2,1)S(1)}, bf16[2,16,1792]{2,1,0:T(8,128)(2,1)S(1)}, u32[]{:S(2)}, u32[]{:S(2)}) %collective-permute-start.4) | collective-permute-done | bytes 114720 | tf_op jit(solution)/shard_map/halo/ppermute | solution.py:445
  26.0 0.1 collective-permute-start.5
  26.0 0.5 %collective-permute-start.7 = (bf16[256,768]{1,0:T(8,128)(2,1)}, bf16[256,768]{1,0:T(8,128)(2,1)}, u32[]{:S(2)}, u32[]{:S(2)}) collective-permute-start(bf16[256,768]{1,0:T(8,128)(2,1)} %get-tuple-element.60), channel_id=1, source_target_pairs={{0,1},{1,0},{2,3},{3,2},{4,5},{5,4},{6,7},{7,6},{8,9},{9,8},{10,11... | collective-permute-start | bytes 1179656 | tf_op jit(solution)/shard_map/halo/ppermute | solution.py:445
  26.5 1.0 %collective-permute-done.5.c_hbm = bf16[4,16,1792]{2,1,0:T(8,128)(2,1)S(1)} collective-permute-done((bf16[4,16,1792]{2,1,0:T(8,128)(2,1)S(1)}, bf16[4,16,1792]{2,1,0:T(8,128)(2,1)S(1)}, u32[]{:S(2)}, u32[]{:S(2)}) %collective-permute-start.5) | collective-permute-done | bytes 229408 | tf_op jit(solution)/shard_map/halo/ppermute | solution.py:445
  27.5 5.4 %grad.1 = (f32[32,128]{1,0:T(8,128)}, f32[256,768]{1,0:T(8,128)S(1)}, bf16[768,768]{1,0:T(8,128)(2,1)S(1)}) custom-call(s32[2]{0:T(128)S(1)} %pad_add_fusion.place_ref, bf16[16,1792]{1,0:T(8,128)(2,1)S(1)} %collective-permute-done.2.back_hbm, bf16[16,1792]{1,0:T(8,128)(2,1)S(1)} %collective-permute-done.3.ahead_hbm, ...), custom_call_target="tpu_custom_call" | custom-call | flops 100000000 | bytes 1024 | tf_op jit(solution)/shard_map/grad/pallas_call | solution.py:428
  32.9 0.0 copy-done
  32.9 0.0 collective-permute-done.1.two_ref
  33.0 0.2 collective-permute-start.6
  33.2 5.2 %all-to-all-start = ((f32[32,1,128]{2,1,0:T(1,128)}), f32[32,1,128]{2,1,0:T(1,128)S(1)}, u32[]{:S(2)}, u32[]{:S(2)}) async-start(f32[32,1,128]{2,1,0:T(1,128)} %bitcast.9), calls=%async_computation | async-start | bytes 32768 | tf_op jit(solution)/shard_map/grad/all_to_all | solution.py:537
  38.4 0.0 collective-permute-done.7.over_ref
  38.4 0.0 collective-permute-done.6.two_over_ref
  38.4 8.1 %rest.1 = bf16[256,768]{1,0:T(8,128)(2,1)} custom-call(s32[2]{0:T(128)S(1)} %pad_add_fusion.place_ref, f32[32,128]{1,0:T(8,128)} %get-tuple-element.52.after_hbm, bf16[768,768]{1,0:T(8,128)(2,1)} %wk_hbm.5, bf16[256,768]{1,0:T(8,128)(2,1)} %copy-done, bf16[256,768]{1,0:T(8,128)(2,1)} %collective-permute-done.1.two_ref, ...), custom_call_target="tpu_custom_call" | custom-call | flops 8000000000 | bytes 1024 | tf_op jit(solution)/shard_map/rest/pallas_call | solution.py:428
  46.5 0.0 all-to-all-done
  46.5 1.0 %clip.1 = f32[256,768]{1,0:T(8,128)} custom-call(f32[32,128]{1,0:T(8,128)S(1)} %bitcast.21, f32[256,768]{1,0:T(8,128)S(1)} %get-tuple-element.59.refs_1_), custom_call_target="tpu_custom_call" | custom-call | bytes 1024 | tf_op jit(solution)/shard_map/clip/pallas_call | solution.py:428
  (3 shorter events, 0.1 us)
Async XLA Ops:
  0.6 15.7 %collective-permute-start = (bf16[256,768]{1,0:T(8,128)(2,1)}, bf16[256,768]{1,0:T(8,128)(2,1)S(1)}, u32[]{:S(2)}, u32[]{:S(2)}) collective-permute-start(bf16[256,768]{1,0:T(8,128)(2,1)} %bitcast.22), channel_id=1, source_target_pairs={{0,4},{1,5},{2,6},{3,7},{4,8},{5,9},{6,10},{7,11},{8,12},{9,13},{1... | collective-permute-start | bytes 1179656 | tf_op jit(solution)/shard_map/halo/ppermute | solution.py:441
  5.6 10.8 %copy-start.1 = (bf16[1,256,768]{2,1,0:T(8,128)(2,1)S(1)}, bf16[1,256,768]{2,1,0:T(8,128)(2,1)}, u32[]{:S(2)}) copy-start(bf16[1,256,768]{2,1,0:T(8,128)(2,1)} %param.9) | copy-start | bytes 1179652
  10.5 9.4 %collective-permute-start.3 = (bf16[16,1792]{1,0:T(8,128)(2,1)S(1)}, bf16[16,1792]{1,0:T(8,128)(2,1)S(1)}, u32[]{:S(2)}, u32[]{:S(2)}) collective-permute-start(bf16[16,1792]{1,0:T(8,128)(2,1)S(1)} %get-tuple-element.33.own_hbm), channel_id=1, source_target_pairs={{4,0},{5,1},{6,2},{7,3},{8,4},{9,5},{10,6},{11,7},{12,8},{13,9},{1... | collective-permute-start | bytes 172040 | tf_op jit(solution)/shard_map/halo/ppermute | solution.py:441
  11.8 8.1 %collective-permute-start.2 = (bf16[16,1792]{1,0:T(8,128)(2,1)S(1)}, bf16[16,1792]{1,0:T(8,128)(2,1)S(1)}, u32[]{:S(2)}, u32[]{:S(2)}) collective-permute-start(bf16[16,1792]{1,0:T(8,128)(2,1)S(1)} %get-tuple-element.33.own_hbm), channel_id=1, source_target_pairs={{0,4},{1,5},{2,6},{3,7},{4,8},{5,9},{6,10},{7,11},{8,12},{9,13},{1... | collective-permute-start | bytes 172040 | tf_op jit(solution)/shard_map/halo/ppermute | solution.py:441
  19.9 6.0 %collective-permute-start.4 = (bf16[2,16,1792]{2,1,0:T(8,128)(2,1)S(1)}, bf16[2,16,1792]{2,1,0:T(8,128)(2,1)S(1)}, u32[]{:S(2)}, u32[]{:S(2)}) collective-permute-start(bf16[2,16,1792]{2,1,0:T(8,128)(2,1)S(1)} %pad_maximum_fusion.1), channel_id=1, source_target_pairs={{0,2},{1,3},{2,0},{3,1},{4,6},{5,7},{6,4},{7,5},{8,10},{9,11},{10,... | collective-permute-start | bytes 344072 | tf_op jit(solution)/shard_map/halo/ppermute | solution.py:445
  21.6 11.4 %collective-permute-start.1 = (bf16[256,768]{1,0:T(8,128)(2,1)S(1)}, bf16[256,768]{1,0:T(8,128)(2,1)}, u32[]{:S(2)}, u32[]{:S(2)}) collective-permute-start(bf16[256,768]{1,0:T(8,128)(2,1)S(1)} %get-tuple-element.32), channel_id=1, source_target_pairs={{0,2},{1,3},{2,0},{3,1},{4,6},{5,7},{6,4},{7,5},{8,10},{9,11},{10,... | collective-permute-start | bytes 1179656 | tf_op jit(solution)/shard_map/halo/ppermute | solution.py:445
  25.0 8.0 %copy-start = (bf16[256,768]{1,0:T(8,128)(2,1)}, bf16[256,768]{1,0:T(8,128)(2,1)S(1)}, u32[]{:S(2)}) copy-start(bf16[256,768]{1,0:T(8,128)(2,1)S(1)} %get-tuple-element.53.mixed_hbm) | copy-start | bytes 1179652
  26.0 1.6 %collective-permute-start.5 = (bf16[4,16,1792]{2,1,0:T(8,128)(2,1)S(1)}, bf16[4,16,1792]{2,1,0:T(8,128)(2,1)S(1)}, u32[]{:S(2)}, u32[]{:S(2)}) collective-permute-start(bf16[4,16,1792]{2,1,0:T(8,128)(2,1)S(1)} %pad_maximum_fusion), channel_id=1, source_target_pairs={{0,1},{1,0},{2,3},{3,2},{4,5},{5,4},{6,7},{7,6},{8,9},{9,8},{10,11... | collective-permute-start | bytes 688136 | tf_op jit(solution)/shard_map/halo/ppermute | solution.py:445
  26.0 12.3 %collective-permute-start.7 = (bf16[256,768]{1,0:T(8,128)(2,1)}, bf16[256,768]{1,0:T(8,128)(2,1)}, u32[]{:S(2)}, u32[]{:S(2)}) collective-permute-start(bf16[256,768]{1,0:T(8,128)(2,1)} %get-tuple-element.60), channel_id=1, source_target_pairs={{0,1},{1,0},{2,3},{3,2},{4,5},{5,4},{6,7},{7,6},{8,9},{9,8},{10,11... | collective-permute-start | bytes 1179656 | tf_op jit(solution)/shard_map/halo/ppermute | solution.py:445
  33.0 5.4 %collective-permute-start.6 = (bf16[256,768]{1,0:T(8,128)(2,1)}, bf16[256,768]{1,0:T(8,128)(2,1)S(1)}, u32[]{:S(2)}, u32[]{:S(2)}) collective-permute-start(bf16[256,768]{1,0:T(8,128)(2,1)} %collective-permute-done.1.two_ref), channel_id=1, source_target_pairs={{0,1},{1,0},{2,3},{3,2},{4,5},{5,4},{6,7},{7,6},{8,9},{9,8},{10,11... | collective-permute-start | bytes 1179656 | tf_op jit(solution)/shard_map/grad/ppermute | solution.py:445
  33.2 13.3 %all-to-all-start = ((f32[32,1,128]{2,1,0:T(1,128)}), f32[32,1,128]{2,1,0:T(1,128)S(1)}, u32[]{:S(2)}, u32[]{:S(2)}) async-start(f32[32,1,128]{2,1,0:T(1,128)} %bitcast.9), calls=%async_computation | async-start | bytes 32768 | tf_op jit(solution)/shard_map/grad/all_to_all | solution.py:537

commit v6 on v5

--- a/solution.py
+++ b/solution.py
@@ -241,7 +241,7 @@
     seen = (own_at < b_at) & (own_at >= b_at - near) & (b_at + first_block < last)
     bias = jnp.where(seen, 0.0, -jnp.inf)
     lane_u = iota((tok, LANES), 1)
-    sigma = jnp.zeros((tok, LANES), F32)
+    terms = []
     scores = a_ref[...]
     for pair_at in range(HEADS // 2):
         pair = columns(pair_at, LANES)
@@ -252,10 +252,12 @@
             h = 2 * pair_at + half
             prob = jnp.exp(scores[:, h : h + 1] - logs[h] + bias)
             term = prob * (dprobs[columns(half, tok)] - deltas[h])
-            sigma = jnp.where(lane_u == h, jnp.sum(term, axis=1, keepdims=True), sigma)
+            terms.append(term.astype(BF16))
             probs.append(prob.astype(BF16))
         parts = dot(jnp.concatenate(probs, axis=0), grad_pair)
         dvalues[:, pair] = jnp.where(lane_u < HEAD_DIM, parts[:tok], parts[tok:]).astype(BF16)
+    to_head = iota((HEADS * count_b, LANES), 0) // count_b == iota((HEADS * count_b, LANES), 1)
+    sigma = dot(jnp.concatenate(terms, axis=1), jnp.where(to_head, 1.0, 0.0).astype(BF16))
     high = sigma.astype(BF16).astype(F32)
     low = (sigma - high).astype(BF16).astype(F32)
     split = (high + pltpu.roll(low, 16, 1) + pltpu.roll(high, 32, 1)).astype(BF16)
@@ -317,12 +319,9 @@
     for piece in pieces[1:]:
         peak = jnp.maximum(peak, piece)
     peak = jnp.max(peak, axis=1, keepdims=True)
-    pieces = [jnp.exp(piece - peak) for piece in pieces]
-    den = pieces[0]
-    for piece in pieces[1:]:
-        den = den + piece
-    den = jnp.sum(den, axis=1, keepdims=True)
-    mixed = dot(jnp.concatenate([piece.astype(BF16) for piece in pieces], axis=1), vals) / den
+    expo = jnp.concatenate([jnp.exp(piece - peak).astype(BF16) for piece in pieces], axis=1)
+    mixed = dot(expo, jnp.concatenate([vals, jnp.ones(vals.shape, BF16)], axis=1))
+    mixed, den = mixed[:, :LANES] / mixed[:, LANES:], mixed[:, LANES:]
     low = iota((tok, LANES), 1) < HEAD_DIM
     return jnp.where(low, mixed[:tok], mixed[tok:]), peak + jnp.log(den)
 

time: 47.9 us -> 47 us (0.981)
  Pallas kernels: 24.9 us -> 23.8 us
  waiting for transfers between devices: 1.97 us -> 2.61 us
    pallas_call x6, Pallas kernels: 24.9 us -> 23.8 us  [call(): pl.pallas_call(kernel, out_shape=out_shape, in_specs=[pl.BlockSpec(memory...]
    ppermute x5, waiting for transfers between devices: 1.96 us -> 2.6 us  [swap(): lax.ppermute(rows, 'seq', [(i, i ^ bit) for i in range(lax.axis_size('seq...]
  transfers between devices with their start and end apart: 9 -> 9, of which waited for: 2 -> 3; matrix products, arithmetic and copies ran while one was open for 2% -> 2% of each run, Pallas kernels for 50% -> 49%
where the time goes in v6:
time: 47 us; the launch traced here: 46.8 us
  Pallas kernels  23.8 us (51%)
  starting transfers between devices  18.5 us (39%)
  waiting for transfers between devices  2.61 us (6%)
  between operations  0.98 us (2%)
  other arithmetic  0.94 us (2%)
    pallas_call x6, Pallas kernels, call(): pl.pallas_call(kernel, out_shape=out_shape, in_specs=[pl.BlockSpec(memory...  23.8 us
    ppermute x3, starting transfers between devices, shift(): lax.ppermute(rows, 'seq', [(i, i + distance) for i in devices if i + dist...  10.8 us
    all_to_all x1, starting transfers between devices, on_device(): squares = lax.all_to_all(square, ('dp', 'seq'), 0, 0)  5.03 us
    ppermute x5, starting transfers between devices, swap(): lax.ppermute(rows, 'seq', [(i, i ^ bit) for i in range(lax.axis_size('seq...  2.66 us
    ppermute x5, waiting for transfers between devices, swap(): lax.ppermute(rows, 'seq', [(i, i ^ bit) for i in range(lax.axis_size('seq...  2.6 us
  transfers between devices with their start and end apart: 9, of which 3 were waited for; matrix products, arithmetic and copies ran while one was open for 2% of the time, Pallas kernels for 49%

profile of v6, /device:TPU:0, one launch (start us, length us, event | category | flops | bytes accessed | tf_op | source)
XLA Modules:
  0.0 46.8 jit_solution(5047622858394095284)
XLA Ops:
  0.6 5.0 %collective-permute-start = (bf16[256,768]{1,0:T(8,128)(2,1)}, bf16[256,768]{1,0:T(8,128)(2,1)S(1)}, u32[]{:S(2)}, u32[]{:S(2)}) collective-permute-start(bf16[256,768]{1,0:T(8,128)(2,1)} %bitcast.22), channel_id=1, source_target_pairs={{0,4},{1,5},{2,6},{3,7},{4,8},{5,9},{6,10},{7,11},{8,12},{9,13},{1... | collective-permute-start | bytes 1179656 | tf_op jit(solution)/shard_map/halo/ppermute | solution.py:440
  5.6 0.0 copy-start.1
  5.6 4.9 %local.1 = (bf16[16,1792]{1,0:T(8,128)(2,1)S(1)}, f32[256,128]{1,0:T(8,128)S(1)}, bf16[128,768]{1,0:T(8,128)(2,1)S(1)}, bf16[16,768]{1,0:T(8,128)(2,1)S(1)}, bf1...) custom-call(bf16[256,768]{1,0:T(8,128)(2,1)} %bitcast.23, ...), custom_call_target="tpu_custom_call" | custom-call | flops 1000000000 | bytes 1024 | tf_op jit(solution)/shard_map/local/pallas_call | solution.py:427
  10.5 1.3 %collective-permute-start.3 = (bf16[16,1792]{1,0:T(8,128)(2,1)S(1)}, bf16[16,1792]{1,0:T(8,128)(2,1)S(1)}, u32[]{:S(2)}, u32[]{:S(2)}) collective-permute-start(bf16[16,1792]{1,0:T(8,128)(2,1)S(1)} %get-tuple-element.33.own_hbm), channel_id=1, source_target_pairs={{4,0},{5,1},{6,2},{7,3},{8,4},{9,5},{10,6},{11,7},{12,8},{13,9},{1... | collective-permute-start | bytes 172040 | tf_op jit(solution)/shard_map/halo/ppermute | solution.py:440
  11.8 4.5 %collective-permute-start.2 = (bf16[16,1792]{1,0:T(8,128)(2,1)S(1)}, bf16[16,1792]{1,0:T(8,128)(2,1)S(1)}, u32[]{:S(2)}, u32[]{:S(2)}) collective-permute-start(bf16[16,1792]{1,0:T(8,128)(2,1)S(1)} %get-tuple-element.33.own_hbm), channel_id=1, source_target_pairs={{0,4},{1,5},{2,6},{3,7},{4,8},{5,9},{6,10},{7,11},{8,12},{9,13},{1... | collective-permute-start | bytes 172040 | tf_op jit(solution)/shard_map/halo/ppermute | solution.py:440
  16.3 0.0 collective-permute-done.far_ref
  16.4 0.0 copy-done.1
  16.4 0.8 %broadcast_select_fusion = (bf16[256,768]{1,0:T(8,128)(2,1)}, bf16[256,768]{1,0:T(8,128)(2,1)S(1)}) fusion(bf16[256,768]{1,0:T(8,128)(2,1)S(1)} %collective-permute-done.far_ref, pred[]{:T(512)S(6)} %eq.9, bf16[1,256,768]{2,1,0:T(8,128)(2,1)S(1)} %copy-done.1, pred[]{:T(512)S(6)} %eq.8), kind=kLoop, calls=%fused_computation | loop fusion | flops 393216 | bytes 1572866 | tf_op jit(solution)/shard_map/halo/jit(_where)/select_n | solution.py:505
  17.2 2.7 %own.1 = (f32[256,128]{1,0:T(8,128)S(1)}, bf16[256,768]{1,0:T(8,128)(2,1)S(1)}, bf16[768,768]{1,0:T(8,128)(2,1)S(1)}, bf16[768,768]{1,0:T(8,128)(2,1)S(1)}) custom-call(bf16[768,768]{1,0:T(8,128)(2,1)} %wk_hbm.5, bf16[768,768]{1,0:T(8,128)(2,1)} %wv_hbm.5, bf16[256,768]{1,0:T(8,128)(2,1)S(1)} %get-tuple-element.34.q_ref, ...), custom_call_target="tpu_custom_call" | custom-call | flops 1000000000 | bytes 1024 | tf_op jit(solution)/shard_map/own/pallas_call | solution.py:427
  19.8 0.0 collective-permute-done.3.ahead_hbm
  19.8 0.0 collective-permute-done.2.back_hbm
  19.9 1.6 %collective-permute-start.4 = (bf16[2,16,1792]{2,1,0:T(8,128)(2,1)S(1)}, bf16[2,16,1792]{2,1,0:T(8,128)(2,1)S(1)}, u32[]{:S(2)}, u32[]{:S(2)}) collective-permute-start(bf16[2,16,1792]{2,1,0:T(8,128)(2,1)S(1)} %pad_maximum_fusion.1), channel_id=1, source_target_pairs={{0,2},{1,3},{2,0},{3,1},{4,6},{5,7},{6,4},{7,5},{8,10},{9,11},{10,... | collective-permute-start | bytes 344072 | tf_op jit(solution)/shard_map/halo/ppermute | solution.py:444
  21.5 0.1 pad_add_fusion.place_ref
  21.6 0.5 %collective-permute-start.1 = (bf16[256,768]{1,0:T(8,128)(2,1)S(1)}, bf16[256,768]{1,0:T(8,128)(2,1)}, u32[]{:S(2)}, u32[]{:S(2)}) collective-permute-start(bf16[256,768]{1,0:T(8,128)(2,1)S(1)} %get-tuple-element.32), channel_id=1, source_target_pairs={{0,2},{1,3},{2,0},{3,1},{4,6},{5,7},{6,4},{7,5},{8,10},{9,11},{10,... | collective-permute-start | bytes 1179656 | tf_op jit(solution)/shard_map/halo/ppermute | solution.py:444
  22.1 2.9 %far.1 = (f32[256,128]{1,0:T(8,128)S(1)}, bf16[256,768]{1,0:T(8,128)(2,1)S(1)}) custom-call(s32[2]{0:T(128)S(1)} %pad_add_fusion.place_ref, bf16[256,768]{1,0:T(8,128)(2,1)S(1)} %collective-permute-done.far_ref, bf16[256,768]{1,0:T(8,128)(2,1)S(1)} %get-tuple-element.34.q_ref, bf16[768,768]{1,0:T(8,128)(2,1)S(1)} %get-tuple-element.43.wk_ref, ...), custom_call_target="tpu_custom_call" | custom-call | flops 100000000 | bytes 1024 | tf_op jit(solution)/shard_map/far/pallas_call | solution.py:427
  24.9 0.0 copy-start
  24.9 1.0 %collective-permute-done.4.y_hbm = bf16[2,16,1792]{2,1,0:T(8,128)(2,1)S(1)} collective-permute-done((bf16[2,16,1792]{2,1,0:T(8,128)(2,1)S(1)}, bf16[2,16,1792]{2,1,0:T(8,128)(2,1)S(1)}, u32[]{:S(2)}, u32[]{:S(2)}) %collective-permute-start.4) | collective-permute-done | bytes 114720 | tf_op jit(solution)/shard_map/halo/ppermute | solution.py:444
  26.0 0.1 collective-permute-start.5
  26.0 0.5 %collective-permute-start.7 = (bf16[256,768]{1,0:T(8,128)(2,1)}, bf16[256,768]{1,0:T(8,128)(2,1)}, u32[]{:S(2)}, u32[]{:S(2)}) collective-permute-start(bf16[256,768]{1,0:T(8,128)(2,1)} %get-tuple-element.60), channel_id=1, source_target_pairs={{0,1},{1,0},{2,3},{3,2},{4,5},{5,4},{6,7},{7,6},{8,9},{9,8},{10,11... | collective-permute-start | bytes 1179656 | tf_op jit(solution)/shard_map/halo/ppermute | solution.py:444
  26.5 1.0 %collective-permute-done.5.c_hbm = bf16[4,16,1792]{2,1,0:T(8,128)(2,1)S(1)} collective-permute-done((bf16[4,16,1792]{2,1,0:T(8,128)(2,1)S(1)}, bf16[4,16,1792]{2,1,0:T(8,128)(2,1)S(1)}, u32[]{:S(2)}, u32[]{:S(2)}) %collective-permute-start.5) | collective-permute-done | bytes 229408 | tf_op jit(solution)/shard_map/halo/ppermute | solution.py:444
  27.5 4.5 %grad.1 = (f32[32,128]{1,0:T(8,128)}, f32[256,768]{1,0:T(8,128)S(1)}, bf16[768,768]{1,0:T(8,128)(2,1)S(1)}) custom-call(s32[2]{0:T(128)S(1)} %pad_add_fusion.place_ref, bf16[16,1792]{1,0:T(8,128)(2,1)S(1)} %collective-permute-done.2.back_hbm, bf16[16,1792]{1,0:T(8,128)(2,1)S(1)} %collective-permute-done.3.ahead_hbm, ...), custom_call_target="tpu_custom_call" | custom-call | flops 100000000 | bytes 1024 | tf_op jit(solution)/shard_map/grad/pallas_call | solution.py:427
  32.0 0.0 copy-done
  32.0 0.6 %collective-permute-done.1.two_ref = bf16[256,768]{1,0:T(8,128)(2,1)} collective-permute-done((bf16[256,768]{1,0:T(8,128)(2,1)S(1)}, bf16[256,768]{1,0:T(8,128)(2,1)}, u32[]{:S(2)}, u32[]{:S(2)}) %collective-permute-start.1) | collective-permute-done | bytes 393248 | tf_op jit(solution)/shard_map/halo/ppermute | solution.py:444
  32.6 0.0 collective-permute-start.6
  32.6 5.0 %all-to-all-start = ((f32[32,1,128]{2,1,0:T(1,128)}), f32[32,1,128]{2,1,0:T(1,128)S(1)}, u32[]{:S(2)}, u32[]{:S(2)}) async-start(f32[32,1,128]{2,1,0:T(1,128)} %bitcast.9), calls=%async_computation | async-start | bytes 32768 | tf_op jit(solution)/shard_map/grad/all_to_all | solution.py:536
  37.7 0.0 collective-permute-done.7.over_ref
  37.7 0.0 collective-permute-done.6.two_over_ref
  37.7 7.9 %rest.1 = bf16[256,768]{1,0:T(8,128)(2,1)} custom-call(s32[2]{0:T(128)S(1)} %pad_add_fusion.place_ref, f32[32,128]{1,0:T(8,128)} %get-tuple-element.52.after_hbm, bf16[768,768]{1,0:T(8,128)(2,1)} %wk_hbm.5, bf16[256,768]{1,0:T(8,128)(2,1)} %copy-done, bf16[256,768]{1,0:T(8,128)(2,1)} %collective-permute-done.1.two_ref, ...), custom_call_target="tpu_custom_call" | custom-call | flops 8000000000 | bytes 1024 | tf_op jit(solution)/shard_map/rest/pallas_call | solution.py:427
  45.6 0.0 all-to-all-done
  45.6 1.0 %clip.1 = f32[256,768]{1,0:T(8,128)} custom-call(f32[32,128]{1,0:T(8,128)S(1)} %bitcast.21, f32[256,768]{1,0:T(8,128)S(1)} %get-tuple-element.59.refs_1_), custom_call_target="tpu_custom_call" | custom-call | bytes 1024 | tf_op jit(solution)/shard_map/clip/pallas_call | solution.py:427
  (3 shorter events, 0.1 us)
Async XLA Ops:
  0.6 15.7 %collective-permute-start = (bf16[256,768]{1,0:T(8,128)(2,1)}, bf16[256,768]{1,0:T(8,128)(2,1)S(1)}, u32[]{:S(2)}, u32[]{:S(2)}) collective-permute-start(bf16[256,768]{1,0:T(8,128)(2,1)} %bitcast.22), channel_id=1, source_target_pairs={{0,4},{1,5},{2,6},{3,7},{4,8},{5,9},{6,10},{7,11},{8,12},{9,13},{1... | collective-permute-start | bytes 1179656 | tf_op jit(solution)/shard_map/halo/ppermute | solution.py:440
  5.6 10.8 %copy-start.1 = (bf16[1,256,768]{2,1,0:T(8,128)(2,1)S(1)}, bf16[1,256,768]{2,1,0:T(8,128)(2,1)}, u32[]{:S(2)}) copy-start(bf16[1,256,768]{2,1,0:T(8,128)(2,1)} %param.9) | copy-start | bytes 1179652
  10.5 9.4 %collective-permute-start.3 = (bf16[16,1792]{1,0:T(8,128)(2,1)S(1)}, bf16[16,1792]{1,0:T(8,128)(2,1)S(1)}, u32[]{:S(2)}, u32[]{:S(2)}) collective-permute-start(bf16[16,1792]{1,0:T(8,128)(2,1)S(1)} %get-tuple-element.33.own_hbm), channel_id=1, source_target_pairs={{4,0},{5,1},{6,2},{7,3},{8,4},{9,5},{10,6},{11,7},{12,8},{13,9},{1... | collective-permute-start | bytes 172040 | tf_op jit(solution)/shard_map/halo/ppermute | solution.py:440
  11.8 8.1 %collective-permute-start.2 = (bf16[16,1792]{1,0:T(8,128)(2,1)S(1)}, bf16[16,1792]{1,0:T(8,128)(2,1)S(1)}, u32[]{:S(2)}, u32[]{:S(2)}) collective-permute-start(bf16[16,1792]{1,0:T(8,128)(2,1)S(1)} %get-tuple-element.33.own_hbm), channel_id=1, source_target_pairs={{0,4},{1,5},{2,6},{3,7},{4,8},{5,9},{6,10},{7,11},{8,12},{9,13},{1... | collective-permute-start | bytes 172040 | tf_op jit(solution)/shard_map/halo/ppermute | solution.py:440
  19.9 6.0 %collective-permute-start.4 = (bf16[2,16,1792]{2,1,0:T(8,128)(2,1)S(1)}, bf16[2,16,1792]{2,1,0:T(8,128)(2,1)S(1)}, u32[]{:S(2)}, u32[]{:S(2)}) collective-permute-start(bf16[2,16,1792]{2,1,0:T(8,128)(2,1)S(1)} %pad_maximum_fusion.1), channel_id=1, source_target_pairs={{0,2},{1,3},{2,0},{3,1},{4,6},{5,7},{6,4},{7,5},{8,10},{9,11},{10,... | collective-permute-start | bytes 344072 | tf_op jit(solution)/shard_map/halo/ppermute | solution.py:444
  21.6 11.1 %collective-permute-start.1 = (bf16[256,768]{1,0:T(8,128)(2,1)S(1)}, bf16[256,768]{1,0:T(8,128)(2,1)}, u32[]{:S(2)}, u32[]{:S(2)}) collective-permute-start(bf16[256,768]{1,0:T(8,128)(2,1)S(1)} %get-tuple-element.32), channel_id=1, source_target_pairs={{0,2},{1,3},{2,0},{3,1},{4,6},{5,7},{6,4},{7,5},{8,10},{9,11},{10,... | collective-permute-start | bytes 1179656 | tf_op jit(solution)/shard_map/halo/ppermute | solution.py:444
  24.9 7.1 %copy-start = (bf16[256,768]{1,0:T(8,128)(2,1)}, bf16[256,768]{1,0:T(8,128)(2,1)S(1)}, u32[]{:S(2)}) copy-start(bf16[256,768]{1,0:T(8,128)(2,1)S(1)} %get-tuple-element.53.mixed_hbm) | copy-start | bytes 1179652
  26.0 1.6 %collective-permute-start.5 = (bf16[4,16,1792]{2,1,0:T(8,128)(2,1)S(1)}, bf16[4,16,1792]{2,1,0:T(8,128)(2,1)S(1)}, u32[]{:S(2)}, u32[]{:S(2)}) collective-permute-start(bf16[4,16,1792]{2,1,0:T(8,128)(2,1)S(1)} %pad_maximum_fusion), channel_id=1, source_target_pairs={{0,1},{1,0},{2,3},{3,2},{4,5},{5,4},{6,7},{7,6},{8,9},{9,8},{10,11... | collective-permute-start | bytes 688136 | tf_op jit(solution)/shard_map/halo/ppermute | solution.py:444
  26.0 11.6 %collective-permute-start.7 = (bf16[256,768]{1,0:T(8,128)(2,1)}, bf16[256,768]{1,0:T(8,128)(2,1)}, u32[]{:S(2)}, u32[]{:S(2)}) collective-permute-start(bf16[256,768]{1,0:T(8,128)(2,1)} %get-tuple-element.60), channel_id=1, source_target_pairs={{0,1},{1,0},{2,3},{3,2},{4,5},{5,4},{6,7},{7,6},{8,9},{9,8},{10,11... | collective-permute-start | bytes 1179656 | tf_op jit(solution)/shard_map/halo/ppermute | solution.py:444
  32.6 5.1 %collective-permute-start.6 = (bf16[256,768]{1,0:T(8,128)(2,1)}, bf16[256,768]{1,0:T(8,128)(2,1)S(1)}, u32[]{:S(2)}, u32[]{:S(2)}) collective-permute-start(bf16[256,768]{1,0:T(8,128)(2,1)} %collective-permute-done.1.two_ref), channel_id=1, source_target_pairs={{0,1},{1,0},{2,3},{3,2},{4,5},{5,4},{6,7},{7,6},{8,9},{9,8},{10,11... | collective-permute-start | bytes 1179656 | tf_op jit(solution)/shard_map/grad/ppermute | solution.py:444
  32.6 13.0 %all-to-all-start = ((f32[32,1,128]{2,1,0:T(1,128)}), f32[32,1,128]{2,1,0:T(1,128)S(1)}, u32[]{:S(2)}, u32[]{:S(2)}) async-start(f32[32,1,128]{2,1,0:T(1,128)} %bitcast.9), calls=%async_computation | async-start | bytes 32768 | tf_op jit(solution)/shard_map/grad/all_to_all | solution.py:536

commit v7 on v6

--- a/solution.py
+++ b/solution.py
@@ -173,14 +173,14 @@
 
 
 def grad_kernel(
-    place_ref, back_hbm, ahead_hbm, y_hbm, c_hbm, own_hbm, wv_hbm, a_ref, v_ref, qk_ref,
+    back_hbm, ahead_hbm, y_hbm, c_hbm, own_hbm, wv_hbm, a_ref, v_ref, qk_ref,
     square_ref, raw_ref, wv_ref,
     held, dvalues, in_sems,
 ):
     tok, width = v_ref.shape
     blocks = tok // BLOCK
-    mine = place_ref[0]
-    last = place_ref[1]
+    mine = lax.axis_index("seq")
+    last = lax.axis_size("seq") * blocks
     at = mine % GROUP
     held[...] = jnp.zeros(held.shape, BF16)
     y_side = jnp.where(at & 2 == 0, 0, 2 * GROUP)
@@ -343,13 +343,13 @@
 
 
 def far_kernel(
-    place_ref, far_ref, q_ref, wk_ref, wv_ref, old_log_ref, old_mixed_ref,
+    far_ref, q_ref, wk_ref, wv_ref, old_log_ref, old_mixed_ref,
     log_ref, mixed_ref,
     total_ref,
 ):
     tok, width = q_ref.shape
     row_b, col_b = iota((tok, tok), 0) // BLOCK, iota((tok, tok), 1) // BLOCK
-    bias = jnp.where((col_b >= row_b) & (place_ref[0] >= GROUP), 0.0, NEVER)
+    bias = jnp.where((col_b >= row_b) & (lax.axis_index("seq") >= GROUP), 0.0, NEVER)
     bias = jnp.concatenate([bias, bias], axis=0)
     keys = dot(far_ref[...], wk_ref[...]).astype(BF16)
     vals = dot(far_ref[...], wv_ref[...]).astype(BF16)
@@ -366,7 +366,7 @@
 
 
 def rest_kernel(
-    place_ref, after_hbm, wk_hbm, mixed_hbm,
+    after_hbm, wk_hbm, mixed_hbm,
     two_ref, two_over_ref, over_ref, q_ref, log_ref, wv_ref,
     out_ref,
     wk_ref, mixed_ref, keys, vals, total_ref, in_sems,
@@ -374,7 +374,7 @@
     tok, width = q_ref.shape
     rows = (two_ref, two_over_ref, over_ref)
     shards = len(rows)
-    mine = place_ref[0]
+    mine = lax.axis_index("seq")
     part = 2 * LANES
     parts = width // part
     key_copy = pltpu.make_async_copy(wk_hbm, wk_ref, in_sems.at[0])
@@ -419,10 +419,10 @@
         copy.wait()
 
 
-def call(kernel, out_shape, hbm_out, args, scratch, smem=(), vmem=(), loose=(), flops=0):
+def call(kernel, out_shape, hbm_out, args, scratch, vmem=(), loose=(), flops=0):
     args = [pltpu.with_memory_space_constraint(array, pltpu.HBM) for array in args]
     args = [*loose, *args, *vmem]
-    kinds = [pltpu.SMEM] * len(smem) + [pl.ANY] * (len(args) - len(vmem)) + [pltpu.VMEM] * len(vmem)
+    kinds = [pl.ANY] * (len(args) - len(vmem)) + [pltpu.VMEM] * len(vmem)
     out_kinds = [pltpu.VMEM] * (len(out_shape) - hbm_out) + [pl.ANY] * hbm_out
     return pl.pallas_call(
         kernel,
@@ -432,7 +432,7 @@
         scratch_shapes=scratch,
         compiler_params=pltpu.CompilerParams(vmem_limit_bytes=VMEM_LIMIT),
         cost_estimate=pl.CostEstimate(flops=flops, bytes_accessed=1 << 10, transcendentals=0),
-    )(*smem, *args)
+    )(*args)
 
 
 def shift(rows, distance):
@@ -451,7 +451,6 @@
     place = lax.axis_index("seq")
     count = lax.axis_size("seq")
     parts = lax.axis_size("dp") * count
-    where = jnp.stack([place, jnp.int32(count * blocks)]).astype(jnp.int32)
     rows = (tok, width)
     square_w = (width, width)
     packed = 2 * width + 2 * LANES
@@ -511,7 +510,6 @@
             0,
             [],
             [vmem(*rows, dtype=F32)],
-            smem=[where],
             vmem=[far, q, wk, wv, log, mixed],
             flops=100_000_000,
         )
@@ -526,7 +524,6 @@
             0,
             [w_value],
             [vmem(3 * GROUP, blocks, packed), vmem(*rows), sems(10)],
-            smem=[where],
             loose=[back, ahead, y2, core4, stats],
             vmem=[a, v, qk],
             flops=100_000_000,
@@ -544,7 +541,6 @@
                 vmem(*square_w), vmem(*rows), vmem(3 * tok, width), vmem(3 * tok, width),
                 vmem(*rows, dtype=F32), sems(2),
             ],
-            smem=[where],
             loose=[square],
             vmem=[two, two_over, over, q, log, wv],
             flops=8_000_000_000,

time: 47 us -> 47 us (level)
  Pallas kernels: 23.8 us -> 22.7 us
  waiting for transfers between devices: 2.61 us -> 3.7 us
    pallas_call x6, Pallas kernels: 23.8 us -> 22.7 us  [call(): pl.pallas_call(kernel, out_shape=out_shape, in_specs=[pl.BlockSpec(memory...]
    ppermute x5, waiting for transfers between devices: 2.6 us -> 3.69 us  [swap(): lax.ppermute(rows, 'seq', [(i, i ^ bit) for i in range(lax.axis_size('seq...]
  transfers between devices with their start and end apart: 9 -> 9, of which waited for: 3 -> 3; matrix products, arithmetic and copies ran while one was open for 2% -> 2% of each run, Pallas kernels for 49% -> 46%
where the time goes in v7:
time: 47 us; the launch traced here: 46.8 us
  Pallas kernels  22.7 us (48%)
  starting transfers between devices  18.6 us (40%)
  waiting for transfers between devices  3.7 us (8%)
  between operations  0.98 us (2%)
  other arithmetic  0.86 us (2%)
    pallas_call x6, Pallas kernels, call(): pl.pallas_call(kernel, out_shape=out_shape, in_specs=[pl.BlockSpec(memory...  22.7 us
    ppermute x3, starting transfers between devices, shift(): lax.ppermute(rows, 'seq', [(i, i + distance) for i in devices if i + dist...  10.8 us
    all_to_all x1, starting transfers between devices, on_device(): squares = lax.all_to_all(square, ('dp', 'seq'), 0, 0)  5.1 us
    ppermute x5, waiting for transfers between devices, swap(): lax.ppermute(rows, 'seq', [(i, i ^ bit) for i in range(lax.axis_size('seq...  3.69 us
    ppermute x5, starting transfers between devices, swap(): lax.ppermute(rows, 'seq', [(i, i ^ bit) for i in range(lax.axis_size('seq...  2.66 us
  transfers between devices with their start and end apart: 9, of which 3 were waited for; matrix products, arithmetic and copies ran while one was open for 2% of the time, Pallas kernels for 46%

profile of v7, /device:TPU:0, one launch (start us, length us, event | category | flops | bytes accessed | tf_op | source)
XLA Modules:
  0.0 46.8 jit_solution(14083093681804567539)
XLA Ops:
  0.6 5.0 %collective-permute-start = (bf16[256,768]{1,0:T(8,128)(2,1)}, bf16[256,768]{1,0:T(8,128)(2,1)S(1)}, u32[]{:S(2)}, u32[]{:S(2)}) collective-permute-start(bf16[256,768]{1,0:T(8,128)(2,1)} %bitcast.21), channel_id=1, source_target_pairs={{0,4},{1,5},{2,6},{3,7},{4,8},{5,9},{6,10},{7,11},{8,12},{9,13},{1... | collective-permute-start | bytes 1179656 | tf_op jit(solution)/shard_map/halo/ppermute | solution.py:440
  5.6 0.0 copy-start.1
  5.6 4.9 %local.1 = (bf16[16,1792]{1,0:T(8,128)(2,1)S(1)}, f32[256,128]{1,0:T(8,128)S(1)}, bf16[128,768]{1,0:T(8,128)(2,1)S(1)}, bf16[16,768]{1,0:T(8,128)(2,1)S(1)}, bf1...) custom-call(bf16[256,768]{1,0:T(8,128)(2,1)} %bitcast.22, ...), custom_call_target="tpu_custom_call" | custom-call | flops 1000000000 | bytes 1024 | tf_op jit(solution)/shard_map/local/pallas_call | solution.py:427
  10.5 1.3 %collective-permute-start.3 = (bf16[16,1792]{1,0:T(8,128)(2,1)S(1)}, bf16[16,1792]{1,0:T(8,128)(2,1)S(1)}, u32[]{:S(2)}, u32[]{:S(2)}) collective-permute-start(bf16[16,1792]{1,0:T(8,128)(2,1)S(1)} %get-tuple-element.33.own_hbm), channel_id=1, source_target_pairs={{4,0},{5,1},{6,2},{7,3},{8,4},{9,5},{10,6},{11,7},{12,8},{13,9},{1... | collective-permute-start | bytes 172040 | tf_op jit(solution)/shard_map/halo/ppermute | solution.py:440
  11.8 4.5 %collective-permute-start.2 = (bf16[16,1792]{1,0:T(8,128)(2,1)S(1)}, bf16[16,1792]{1,0:T(8,128)(2,1)S(1)}, u32[]{:S(2)}, u32[]{:S(2)}) collective-permute-start(bf16[16,1792]{1,0:T(8,128)(2,1)S(1)} %get-tuple-element.33.own_hbm), channel_id=1, source_target_pairs={{0,4},{1,5},{2,6},{3,7},{4,8},{5,9},{6,10},{7,11},{8,12},{9,13},{1... | collective-permute-start | bytes 172040 | tf_op jit(solution)/shard_map/halo/ppermute | solution.py:440
  16.3 0.0 collective-permute-done.far_ref
  16.3 0.0 copy-done.1
  16.4 0.8 %broadcast_select_fusion = (bf16[256,768]{1,0:T(8,128)(2,1)}, bf16[256,768]{1,0:T(8,128)(2,1)S(1)}) fusion(bf16[256,768]{1,0:T(8,128)(2,1)S(1)} %collective-permute-done.far_ref, pred[]{:T(512)S(6)} %eq.9, bf16[1,256,768]{2,1,0:T(8,128)(2,1)S(1)} %copy-done.1, pred[]{:T(512)S(6)} %eq.8), kind=kLoop, calls=%fused_computation | loop fusion | flops 393216 | bytes 1572866 | tf_op jit(solution)/shard_map/halo/jit(_where)/select_n | solution.py:504
  17.2 2.7 %own.1 = (f32[256,128]{1,0:T(8,128)S(1)}, bf16[256,768]{1,0:T(8,128)(2,1)S(1)}, bf16[768,768]{1,0:T(8,128)(2,1)S(1)}, bf16[768,768]{1,0:T(8,128)(2,1)S(1)}) custom-call(bf16[768,768]{1,0:T(8,128)(2,1)} %wk_hbm.5, bf16[768,768]{1,0:T(8,128)(2,1)} %wv_hbm.5, bf16[256,768]{1,0:T(8,128)(2,1)S(1)} %get-tuple-element.34.q_ref, ...), custom_call_target="tpu_custom_call" | custom-call | flops 1000000000 | bytes 1024 | tf_op jit(solution)/shard_map/own/pallas_call | solution.py:427
  19.8 0.0 collective-permute-done.3.ahead_hbm
  19.8 0.0 collective-permute-done.2.back_hbm
  19.9 1.6 %collective-permute-start.4 = (bf16[2,16,1792]{2,1,0:T(8,128)(2,1)S(1)}, bf16[2,16,1792]{2,1,0:T(8,128)(2,1)S(1)}, u32[]{:S(2)}, u32[]{:S(2)}) collective-permute-start(bf16[2,16,1792]{2,1,0:T(8,128)(2,1)S(1)} %pad_maximum_fusion.1), channel_id=1, source_target_pairs={{0,2},{1,3},{2,0},{3,1},{4,6},{5,7},{6,4},{7,5},{8,10},{9,11},{10,... | collective-permute-start | bytes 344072 | tf_op jit(solution)/shard_map/halo/ppermute | solution.py:444
  21.5 0.5 %collective-permute-start.1 = (bf16[256,768]{1,0:T(8,128)(2,1)S(1)}, bf16[256,768]{1,0:T(8,128)(2,1)}, u32[]{:S(2)}, u32[]{:S(2)}) collective-permute-start(bf16[256,768]{1,0:T(8,128)(2,1)S(1)} %get-tuple-element.32), channel_id=1, source_target_pairs={{0,2},{1,3},{2,0},{3,1},{4,6},{5,7},{6,4},{7,5},{8,10},{9,11},{10,... | collective-permute-start | bytes 1179656 | tf_op jit(solution)/shard_map/halo/ppermute | solution.py:444
  22.0 2.3 %far.1 = (f32[256,128]{1,0:T(8,128)S(1)}, bf16[256,768]{1,0:T(8,128)(2,1)S(1)}) custom-call(bf16[256,768]{1,0:T(8,128)(2,1)S(1)} %collective-permute-done.far_ref, bf16[256,768]{1,0:T(8,128)(2,1)S(1)} %get-tuple-element.34.q_ref, bf16[768,768]{1,0:T(8,128)(2,1)S(1)} %get-tuple-element.43.wk_ref, bf16[768,768]{1,0:T(8,128)(2,1)S(1)} %get-tuple-element.44.wv_ref, ...), custom_call_target="tpu_custom_call" | custom-call | flops 100000000 | bytes 1024 | tf_op jit(solution)/shard_map/far/pallas_call | solution.py:427
  24.3 0.0 copy-start
  24.3 1.6 %collective-permute-done.4.y_hbm = bf16[2,16,1792]{2,1,0:T(8,128)(2,1)S(1)} collective-permute-done((bf16[2,16,1792]{2,1,0:T(8,128)(2,1)S(1)}, bf16[2,16,1792]{2,1,0:T(8,128)(2,1)S(1)}, u32[]{:S(2)}, u32[]{:S(2)}) %collective-permute-start.4) | collective-permute-done | bytes 114720 | tf_op jit(solution)/shard_map/halo/ppermute | solution.py:444
  26.0 0.1 collective-permute-start.5
  26.1 0.5 %collective-permute-start.7 = (bf16[256,768]{1,0:T(8,128)(2,1)}, bf16[256,768]{1,0:T(8,128)(2,1)}, u32[]{:S(2)}, u32[]{:S(2)}) collective-permute-start(bf16[256,768]{1,0:T(8,128)(2,1)} %get-tuple-element.60), channel_id=1, source_target_pairs={{0,1},{1,0},{2,3},{3,2},{4,5},{5,4},{6,7},{7,6},{8,9},{9,8},{10,11... | collective-permute-start | bytes 1179656 | tf_op jit(solution)/shard_map/halo/ppermute | solution.py:444
  26.6 1.0 %collective-permute-done.5.c_hbm = bf16[4,16,1792]{2,1,0:T(8,128)(2,1)S(1)} collective-permute-done((bf16[4,16,1792]{2,1,0:T(8,128)(2,1)S(1)}, bf16[4,16,1792]{2,1,0:T(8,128)(2,1)S(1)}, u32[]{:S(2)}, u32[]{:S(2)}) %collective-permute-start.5) | collective-permute-done | bytes 229408 | tf_op jit(solution)/shard_map/halo/ppermute | solution.py:444
  27.5 3.9 %grad.1 = (f32[32,128]{1,0:T(8,128)}, f32[256,768]{1,0:T(8,128)S(1)}, bf16[768,768]{1,0:T(8,128)(2,1)S(1)}) custom-call(bf16[16,1792]{1,0:T(8,128)(2,1)S(1)} %collective-permute-done.2.back_hbm, bf16[16,1792]{1,0:T(8,128)(2,1)S(1)} %collective-permute-done.3.ahead_hbm, bf16[2,16,1792]{2,1,0:T(8,128)(2,1)S(1)} %collective-permute-done.4.y_hbm, ...), custom_call_target="tpu_custom_call" | custom-call | flops 100000000 | bytes 1024 | tf_op jit(solution)/shard_map/grad/pallas_call | solution.py:427
  31.5 0.0 copy-done
  31.5 1.1 %collective-permute-done.1.two_ref = bf16[256,768]{1,0:T(8,128)(2,1)} collective-permute-done((bf16[256,768]{1,0:T(8,128)(2,1)S(1)}, bf16[256,768]{1,0:T(8,128)(2,1)}, u32[]{:S(2)}, u32[]{:S(2)}) %collective-permute-start.1) | collective-permute-done | bytes 393248 | tf_op jit(solution)/shard_map/halo/ppermute | solution.py:444
  32.6 0.0 collective-permute-start.6
  32.6 5.1 %all-to-all-start = ((f32[32,1,128]{2,1,0:T(1,128)}), f32[32,1,128]{2,1,0:T(1,128)S(1)}, u32[]{:S(2)}, u32[]{:S(2)}) async-start(f32[32,1,128]{2,1,0:T(1,128)} %bitcast.8), calls=%async_computation | async-start | bytes 32768 | tf_op jit(solution)/shard_map/grad/all_to_all | solution.py:533
  37.7 0.0 collective-permute-done.7.over_ref
  37.7 0.0 collective-permute-done.6.two_over_ref
  37.7 7.9 %rest.1 = bf16[256,768]{1,0:T(8,128)(2,1)} custom-call(f32[32,128]{1,0:T(8,128)} %get-tuple-element.52.after_hbm, bf16[768,768]{1,0:T(8,128)(2,1)} %wk_hbm.5, bf16[256,768]{1,0:T(8,128)(2,1)} %copy-done, bf16[256,768]{1,0:T(8,128)(2,1)} %collective-permute-done.1.two_ref, bf16[256,768]{1,0:T(8,128)(2,1)S(1)} %collective-permute-done.6.two_over_ref, ...), custom_call_target="tpu_custom_call" | custom-call | flops 8000000000 | bytes 1024 | tf_op jit(solution)/shard_map/rest/pallas_call | solution.py:427
  45.6 0.0 all-to-all-done
  45.6 1.0 %clip.1 = f32[256,768]{1,0:T(8,128)} custom-call(f32[32,128]{1,0:T(8,128)S(1)} %bitcast.20, f32[256,768]{1,0:T(8,128)S(1)} %get-tuple-element.59.refs_1_), custom_call_target="tpu_custom_call" | custom-call | bytes 1024 | tf_op jit(solution)/shard_map/clip/pallas_call | solution.py:427
  (3 shorter events, 0.1 us)
Async XLA Ops:
  0.6 15.7 %collective-permute-start = (bf16[256,768]{1,0:T(8,128)(2,1)}, bf16[256,768]{1,0:T(8,128)(2,1)S(1)}, u32[]{:S(2)}, u32[]{:S(2)}) collective-permute-start(bf16[256,768]{1,0:T(8,128)(2,1)} %bitcast.21), channel_id=1, source_target_pairs={{0,4},{1,5},{2,6},{3,7},{4,8},{5,9},{6,10},{7,11},{8,12},{9,13},{1... | collective-permute-start | bytes 1179656 | tf_op jit(solution)/shard_map/halo/ppermute | solution.py:440
  5.6 10.8 %copy-start.1 = (bf16[1,256,768]{2,1,0:T(8,128)(2,1)S(1)}, bf16[1,256,768]{2,1,0:T(8,128)(2,1)}, u32[]{:S(2)}) copy-start(bf16[1,256,768]{2,1,0:T(8,128)(2,1)} %param.9) | copy-start | bytes 1179652
  10.5 9.4 %collective-permute-start.3 = (bf16[16,1792]{1,0:T(8,128)(2,1)S(1)}, bf16[16,1792]{1,0:T(8,128)(2,1)S(1)}, u32[]{:S(2)}, u32[]{:S(2)}) collective-permute-start(bf16[16,1792]{1,0:T(8,128)(2,1)S(1)} %get-tuple-element.33.own_hbm), channel_id=1, source_target_pairs={{4,0},{5,1},{6,2},{7,3},{8,4},{9,5},{10,6},{11,7},{12,8},{13,9},{1... | collective-permute-start | bytes 172040 | tf_op jit(solution)/shard_map/halo/ppermute | solution.py:440
  11.8 8.1 %collective-permute-start.2 = (bf16[16,1792]{1,0:T(8,128)(2,1)S(1)}, bf16[16,1792]{1,0:T(8,128)(2,1)S(1)}, u32[]{:S(2)}, u32[]{:S(2)}) collective-permute-start(bf16[16,1792]{1,0:T(8,128)(2,1)S(1)} %get-tuple-element.33.own_hbm), channel_id=1, source_target_pairs={{0,4},{1,5},{2,6},{3,7},{4,8},{5,9},{6,10},{7,11},{8,12},{9,13},{1... | collective-permute-start | bytes 172040 | tf_op jit(solution)/shard_map/halo/ppermute | solution.py:440
  19.9 6.0 %collective-permute-start.4 = (bf16[2,16,1792]{2,1,0:T(8,128)(2,1)S(1)}, bf16[2,16,1792]{2,1,0:T(8,128)(2,1)S(1)}, u32[]{:S(2)}, u32[]{:S(2)}) collective-permute-start(bf16[2,16,1792]{2,1,0:T(8,128)(2,1)S(1)} %pad_maximum_fusion.1), channel_id=1, source_target_pairs={{0,2},{1,3},{2,0},{3,1},{4,6},{5,7},{6,4},{7,5},{8,10},{9,11},{10,... | collective-permute-start | bytes 344072 | tf_op jit(solution)/shard_map/halo/ppermute | solution.py:444
  21.5 11.1 %collective-permute-start.1 = (bf16[256,768]{1,0:T(8,128)(2,1)S(1)}, bf16[256,768]{1,0:T(8,128)(2,1)}, u32[]{:S(2)}, u32[]{:S(2)}) collective-permute-start(bf16[256,768]{1,0:T(8,128)(2,1)S(1)} %get-tuple-element.32), channel_id=1, source_target_pairs={{0,2},{1,3},{2,0},{3,1},{4,6},{5,7},{6,4},{7,5},{8,10},{9,11},{10,... | collective-permute-start | bytes 1179656 | tf_op jit(solution)/shard_map/halo/ppermute | solution.py:444
  24.3 7.2 %copy-start = (bf16[256,768]{1,0:T(8,128)(2,1)}, bf16[256,768]{1,0:T(8,128)(2,1)S(1)}, u32[]{:S(2)}) copy-start(bf16[256,768]{1,0:T(8,128)(2,1)S(1)} %get-tuple-element.53.mixed_hbm) | copy-start | bytes 1179652
  26.0 1.6 %collective-permute-start.5 = (bf16[4,16,1792]{2,1,0:T(8,128)(2,1)S(1)}, bf16[4,16,1792]{2,1,0:T(8,128)(2,1)S(1)}, u32[]{:S(2)}, u32[]{:S(2)}) collective-permute-start(bf16[4,16,1792]{2,1,0:T(8,128)(2,1)S(1)} %pad_maximum_fusion), channel_id=1, source_target_pairs={{0,1},{1,0},{2,3},{3,2},{4,5},{5,4},{6,7},{7,6},{8,9},{9,8},{10,11... | collective-permute-start | bytes 688136 | tf_op jit(solution)/shard_map/halo/ppermute | solution.py:444
  26.1 11.6 %collective-permute-start.7 = (bf16[256,768]{1,0:T(8,128)(2,1)}, bf16[256,768]{1,0:T(8,128)(2,1)}, u32[]{:S(2)}, u32[]{:S(2)}) collective-permute-start(bf16[256,768]{1,0:T(8,128)(2,1)} %get-tuple-element.60), channel_id=1, source_target_pairs={{0,1},{1,0},{2,3},{3,2},{4,5},{5,4},{6,7},{7,6},{8,9},{9,8},{10,11... | collective-permute-start | bytes 1179656 | tf_op jit(solution)/shard_map/halo/ppermute | solution.py:444
  32.6 5.1 %collective-permute-start.6 = (bf16[256,768]{1,0:T(8,128)(2,1)}, bf16[256,768]{1,0:T(8,128)(2,1)S(1)}, u32[]{:S(2)}, u32[]{:S(2)}) collective-permute-start(bf16[256,768]{1,0:T(8,128)(2,1)} %collective-permute-done.1.two_ref), channel_id=1, source_target_pairs={{0,1},{1,0},{2,3},{3,2},{4,5},{5,4},{6,7},{7,6},{8,9},{9,8},{10,11... | collective-permute-start | bytes 1179656 | tf_op jit(solution)/shard_map/grad/ppermute | solution.py:444
  32.6 13.0 %all-to-all-start = ((f32[32,1,128]{2,1,0:T(1,128)}), f32[32,1,128]{2,1,0:T(1,128)S(1)}, u32[]{:S(2)}, u32[]{:S(2)}) async-start(f32[32,1,128]{2,1,0:T(1,128)} %bitcast.8), calls=%async_computation | async-start | bytes 32768 | tf_op jit(solution)/shard_map/grad/all_to_all | solution.py:533
